TPU v7x, 32 devices: a whole 2x2x4 slice. The times are simulated.
32 devices in a mesh: dp: 4 (over x, core), fsdp: 8 (over z, y).
Axes of the slice: x: 2, y: 2, z: 4, core: 2. Of those that a mesh axis runs over, the one named last changes fastest.
Arguments:
- tokens: bfloat16 [32768, 1024], P(('dp', 'fsdp')), may hold values from -6 to 6
- doc_lengths: int32 [32, 8], P(('dp', 'fsdp')), may hold values from 0 to 1024, as said below
- gain_one: bfloat16 [1024], P(('dp', 'fsdp')), may hold values from 0.099609375 to 1.8984375
- query_weight: bfloat16 [1024, 1024], P(('dp', 'fsdp')), may hold values from -0.1875 to 0.1875
- key_weight: bfloat16 [1024, 128], P(('dp', 'fsdp')), may hold values from -0.1875 to 0.1875
- value_weight: bfloat16 [1024, 128], P(('dp', 'fsdp')), may hold values from -0.1875 to 0.1875
- out_weight: bfloat16 [1024, 1024], P(('dp', 'fsdp')), may hold values from -0.75 to 0.75
- gain_two: bfloat16 [1024], P(('dp', 'fsdp')), may hold values from 0.099609375 to 1.8984375
- up_weight: bfloat16 [1024, 4096], P(('dp', 'fsdp')), may hold values from -0.1875 to 0.1875
- down_weight: bfloat16 [4096, 1024], P(('dp', 'fsdp')), may hold values from -0.09375 to 0.09375
- cotangent: bfloat16 [32768, 1024], P(('dp', 'fsdp')), may hold values from -6 to 6
Outputs:
- output: bfloat16 [32768, 1024], P(('dp', 'fsdp'))
- grad_tokens: bfloat16 [32768, 1024], P(('dp', 'fsdp'))
- grad_gain_one: float32 [1024], P(('dp', 'fsdp'))
- grad_query_weight: float32 [1024, 1024], P(('dp', 'fsdp'))
- grad_key_weight: float32 [1024, 128], P(('dp', 'fsdp'))
- grad_value_weight: float32 [1024, 128], P(('dp', 'fsdp'))
- grad_out_weight: float32 [1024, 1024], P(('dp', 'fsdp'))
- grad_gain_two: float32 [1024], P(('dp', 'fsdp'))
- grad_up_weight: float32 [1024, 4096], P(('dp', 'fsdp'))
- grad_down_weight: float32 [4096, 1024], P(('dp', 'fsdp'))
Inputs may be any that keep to these rules, and one draw needn't show every extreme that they name: `doc_lengths`: row d belongs to device d along dp+fsdp (dp outer). Each row sums to at most 1024; a zero length is an empty slot. In every draw one device holds a single sequence of 1024 tokens.
All inputs are finite; a program needn't handle non-finite values.
Results may differ from a plain program's by a relative error of at most 0.012.
Values may be sent and summed in bfloat16 or wider, within the bound.
No kernel may reach another device: no remote copies, remote signals or barrier semaphores. Data moves between devices by JAX's collectives and lax.ppermute only.
A program may use at most 256 MiB of HBM per device.

v0:
```python
import math

import jax
import jax.numpy as jnp
from jax import lax
from jax.sharding import PartitionSpec as P

epsilon = 1e-06


def pack_mask(lengths, row_count):
    position = jnp.arange(row_count, dtype=jnp.int32)
    seq_ends = jnp.cumsum(lengths)
    segment = jnp.sum((position[:, None] >= seq_ends[None, :]).astype(jnp.int32), axis=1)
    padding = position >= seq_ends[-1]
    causal = position[None, :] <= position[:, None]
    allowed = (segment[:, None] == segment[None, :]) & causal & jnp.logical_not(padding)[None, :]
    return allowed | (position[:, None] == position[None, :])


def norm_rows(inputs, gain):
    return inputs * lax.rsqrt(jnp.mean(inputs * inputs, axis=-1, keepdims=True) + epsilon) * gain


def on_device(
    tokens,
    doc_lengths,
    gain_one,
    query_weight,
    key_weight,
    value_weight,
    out_weight,
    gain_two,
    up_weight,
    down_weight,
    cotangent,
):
    attention_set = (
        lax.all_gather(gain_one, ("dp", "fsdp"), axis=0, tiled=True),
        lax.all_gather(query_weight, ("dp", "fsdp"), axis=0, tiled=True),
        lax.all_gather(key_weight, ("dp", "fsdp"), axis=0, tiled=True),
        lax.all_gather(value_weight, ("dp", "fsdp"), axis=0, tiled=True),
        lax.all_gather(out_weight, ("dp", "fsdp"), axis=0, tiled=True),
    )
    full_gain_one, full_query, full_key, full_value, full_out = attention_set
    token_rows = tokens.astype(jnp.float32)
    row_count = token_rows.shape[0]
    head_size = full_key.shape[1]
    head_count = full_query.shape[1] // head_size
    score_scale = 1.0 / math.sqrt(head_size)
    allowed = pack_mask(doc_lengths[0], row_count)
    normed = norm_rows(token_rows, full_gain_one.astype(jnp.float32)).astype(jnp.bfloat16)
    queries = jnp.dot(normed, full_query, preferred_element_type=jnp.float32).astype(jnp.bfloat16)
    key_rows = jnp.dot(normed, full_key, preferred_element_type=jnp.float32).astype(jnp.bfloat16)
    value_rows = jnp.dot(normed, full_value, preferred_element_type=jnp.float32).astype(
        jnp.bfloat16
    )
    query_heads = queries.reshape(row_count, head_count, head_size)
    scores = (
        jnp.einsum("qhe,ke->hqk", query_heads, key_rows, preferred_element_type=jnp.float32)
        * score_scale
    )
    scores = jnp.where(allowed[None], scores, -1e30)
    row_peak = jnp.max(scores, axis=-1, keepdims=True)
    exponent = jnp.exp(scores - row_peak)
    probabilities = exponent / jnp.sum(exponent, axis=-1, keepdims=True)
    prob_low = probabilities.astype(jnp.bfloat16)
    attended = jnp.einsum("hqk,ke->qhe", prob_low, value_rows, preferred_element_type=jnp.float32)
    attended = attended.reshape(row_count, head_count * head_size).astype(jnp.bfloat16)
    hidden = token_rows + jnp.dot(attended, full_out, preferred_element_type=jnp.float32)
    ffn_set = (
        lax.all_gather(gain_two, ("dp", "fsdp"), axis=0, tiled=True),
        lax.all_gather(up_weight, ("dp", "fsdp"), axis=0, tiled=True),
        lax.all_gather(down_weight, ("dp", "fsdp"), axis=0, tiled=True),
    )
    full_gain_two, full_up, full_down = ffn_set
    normed_two = norm_rows(hidden, full_gain_two.astype(jnp.float32)).astype(jnp.bfloat16)
    inner = jnp.dot(normed_two, full_up, preferred_element_type=jnp.float32)
    active_value, gelu_pull = jax.vjp(jax.nn.gelu, inner)
    active = active_value.astype(jnp.bfloat16)
    output = (hidden + jnp.dot(active, full_down, preferred_element_type=jnp.float32)).astype(
        jnp.bfloat16
    )
    back_gain_two, back_up, back_down = (
        lax.all_gather(gain_two, ("dp", "fsdp"), axis=0, tiled=True),
        lax.all_gather(up_weight, ("dp", "fsdp"), axis=0, tiled=True),
        lax.all_gather(down_weight, ("dp", "fsdp"), axis=0, tiled=True),
    )
    back_gain_one, back_query, back_key, back_value, back_out = (
        lax.all_gather(gain_one, ("dp", "fsdp"), axis=0, tiled=True),
        lax.all_gather(query_weight, ("dp", "fsdp"), axis=0, tiled=True),
        lax.all_gather(key_weight, ("dp", "fsdp"), axis=0, tiled=True),
        lax.all_gather(value_weight, ("dp", "fsdp"), axis=0, tiled=True),
        lax.all_gather(out_weight, ("dp", "fsdp"), axis=0, tiled=True),
    )
    grad_output = cotangent.astype(jnp.float32)
    grad_down = jnp.einsum("tf,td->fd", active, cotangent, preferred_element_type=jnp.float32)
    grad_active = jnp.einsum("td,fd->tf", cotangent, back_down, preferred_element_type=jnp.float32)
    grad_inner = gelu_pull(grad_active)[0].astype(jnp.bfloat16)
    grad_up = jnp.einsum("td,tf->df", normed_two, grad_inner, preferred_element_type=jnp.float32)
    grad_normed_two = jnp.einsum(
        "tf,df->td", grad_inner, back_up, preferred_element_type=jnp.float32
    )
    unused, norm_pull_two = jax.vjp(norm_rows, hidden, back_gain_two.astype(jnp.float32))
    grad_hidden_part, grad_gain_two = norm_pull_two(grad_normed_two)
    grad_hidden = grad_output + grad_hidden_part
    grad_branch = grad_hidden.astype(jnp.bfloat16)
    grad_out = jnp.einsum("tj,td->jd", attended, grad_branch, preferred_element_type=jnp.float32)
    grad_attended = jnp.einsum(
        "td,jd->tj", grad_branch, back_out, preferred_element_type=jnp.float32
    ).astype(jnp.bfloat16)
    grad_attended = grad_attended.reshape(row_count, head_count, head_size)
    grad_values = jnp.einsum(
        "hqk,qhe->ke", prob_low, grad_attended, preferred_element_type=jnp.float32
    ).astype(jnp.bfloat16)
    grad_probs = jnp.einsum(
        "qhe,ke->hqk", grad_attended, value_rows, preferred_element_type=jnp.float32
    )
    grad_scores = probabilities * (
        grad_probs - jnp.sum(probabilities * grad_probs, axis=-1, keepdims=True)
    )
    grad_scores = grad_scores.astype(jnp.bfloat16)
    grad_queries = (
        jnp.einsum("hqk,ke->qhe", grad_scores, key_rows, preferred_element_type=jnp.float32)
        * score_scale
    )
    grad_queries = grad_queries.astype(jnp.bfloat16).reshape(row_count, head_count * head_size)
    grad_keys = (
        jnp.einsum("hqk,qhe->ke", grad_scores, query_heads, preferred_element_type=jnp.float32)
        * score_scale
    ).astype(jnp.bfloat16)
    grad_query = jnp.einsum("td,tj->dj", normed, grad_queries, preferred_element_type=jnp.float32)
    grad_key = jnp.einsum("td,te->de", normed, grad_keys, preferred_element_type=jnp.float32)
    grad_value = jnp.einsum("td,te->de", normed, grad_values, preferred_element_type=jnp.float32)
    grad_normed = jnp.einsum(
        "tj,dj->td", grad_queries, back_query, preferred_element_type=jnp.float32
    )
    grad_normed = grad_normed + jnp.einsum(
        "te,de->td", grad_keys, back_key, preferred_element_type=jnp.float32
    )
    grad_normed = grad_normed + jnp.einsum(
        "te,de->td", grad_values, back_value, preferred_element_type=jnp.float32
    )
    unused, norm_pull_one = jax.vjp(norm_rows, token_rows, back_gain_one.astype(jnp.float32))
    grad_token_part, grad_gain_one = norm_pull_one(grad_normed)
    grad_tokens = (grad_hidden + grad_token_part).astype(jnp.bfloat16)
    every_sum = (
        lax.psum_scatter(grad_gain_one, ("dp", "fsdp"), scatter_dimension=0, tiled=True),
        lax.psum_scatter(grad_query, ("dp", "fsdp"), scatter_dimension=0, tiled=True),
        lax.psum_scatter(grad_key, ("dp", "fsdp"), scatter_dimension=0, tiled=True),
        lax.psum_scatter(grad_value, ("dp", "fsdp"), scatter_dimension=0, tiled=True),
        lax.psum_scatter(grad_out, ("dp", "fsdp"), scatter_dimension=0, tiled=True),
        lax.psum_scatter(grad_gain_two, ("dp", "fsdp"), scatter_dimension=0, tiled=True),
        lax.psum_scatter(grad_up, ("dp", "fsdp"), scatter_dimension=0, tiled=True),
        lax.psum_scatter(grad_down, ("dp", "fsdp"), scatter_dimension=0, tiled=True),
    )
    attention_sums = every_sum[:5]
    ffn_sums = every_sum[5:]
    return (
        output,
        grad_tokens,
        attention_sums[0],
        attention_sums[1],
        attention_sums[2],
        attention_sums[3],
        attention_sums[4],
        ffn_sums[0],
        ffn_sums[1],
        ffn_sums[2],
    )


def solution(mesh):
    return jax.shard_map(
        on_device,
        mesh=mesh,
        in_specs=(
            P(("dp", "fsdp"), None),
            P(("dp", "fsdp"), None),
            P(("dp", "fsdp")),
            P(("dp", "fsdp"), None),
            P(("dp", "fsdp"), None),
            P(("dp", "fsdp"), None),
            P(("dp", "fsdp"), None),
            P(("dp", "fsdp")),
            P(("dp", "fsdp"), None),
            P(("dp", "fsdp"), None),
            P(("dp", "fsdp"), None),
        ),
        out_specs=(
            P(("dp", "fsdp"), None),
            P(("dp", "fsdp"), None),
            P(("dp", "fsdp")),
            P(("dp", "fsdp"), None),
            P(("dp", "fsdp"), None),
            P(("dp", "fsdp"), None),
            P(("dp", "fsdp"), None),
            P(("dp", "fsdp")),
            P(("dp", "fsdp"), None),
            P(("dp", "fsdp"), None),
        ),
        check_vma=False,
    )
```

profile of v0, /device:TPU:0, one launch (start us, length us, event | category | flops | bytes accessed | tf_op | source)
XLA Modules:
  0.0 1660.9 jit_solution(1503715283154881663)
XLA Ops:
  13.1 42.1 %all-reduce.5 = (bf16[1024]{0:T(1024)(128)(2,1)S(1)}, bf16[1024]{0:T(1024)(128)(2,1)S(1)}) all-reduce(bf16[1024]{0:T(1024)(128)(2,1)S(1)} %dynamic-update-slice, bf16[1024]{0:T(1024)(128)(2,1)S(1)} %dynamic-update-slice.1), channel_id=1, replica_groups=mesh['dp'=4,'fsdp'=8] {'dp','fsdp'}, use_global_device_ids=true, to_apply=%add | all-reduce | flops 2048 | bytes 8192
  63.5 67.7 %all_gather.34 = bf16[1024,128]{1,0:T(8,128)(2,1)S(1)} all-gather(bf16[32,128]{1,0:T(8,128)(2,1)S(1)} %copy-done.23), channel_id=1, replica_groups=mesh['dp'=4,'fsdp'=8] {'dp','fsdp'}, dimensions={0}, use_global_device_ids=true | all-gather | bytes 270336 | tf_op jit(solution)/shard_map/all_gather | solution.py:41
  131.2 66.1 %all_gather.33 = bf16[1024,128]{1,0:T(8,128)(2,1)S(1)} all-gather(bf16[32,128]{1,0:T(8,128)(2,1)S(1)} %copy-done.24), channel_id=1, replica_groups=mesh['dp'=4,'fsdp'=8] {'dp','fsdp'}, dimensions={0}, use_global_device_ids=true | all-gather | bytes 270336 | tf_op jit(solution)/shard_map/all_gather | solution.py:42
  209.4 19.0 %fusion.57 = (f32[8,1024]{1,0:T(8,128)S(1)}, f32[8,1024,1024]{1,2,0:T(8,128)}) fusion(pred[1024,1024]{0,1:T(8,128)(4,1)S(1)} %fusion.30, bf16[1024,128,1]{1,0,2:T(8,128)(2,1)S(1)} %fusion.45, bf16[1024,8,128]{0,2,1:T(8,128)(2,1)} %bitcast.95), kind=kOutput, calls=%fused_computation.86 | convolution fusion | flops 2181039104 | bytes 36995072 | tf_op jit(solution)/shard_map/sub | solution.py:65
  228.3 13.8 fusion.33
  249.1 16.1 fusion.58
  265.2 23.2 %all-gather.9.cloned.1.call-done = bf16[1024,4096]{1,0:T(8,128)(2,1)} async-done(((bf16[32,4096]{1,0:T(8,128)(2,1)}), bf16[1024,4096]{1,0:T(8,128)(2,1)}) %all-gather.9.cloned.1.call-update) | async-done | bytes 8388624 | tf_op jit(solution)/shard_map/all_gather | solution.py:73
  288.4 30.0 %fusion.11 = (bf16[1024,4096]{1,0:T(8,128)(2,1)}, f32[1024,4096]{1,0:T(8,128)}) fusion(f32[1024,4096]{1,0:T(8,128)} %fusion.58, bf16[1024,4096]{1,0:T(8,128)(2,1)} %all-gather.9.cloned.1.call-done, f32[1024,1024]{0,1:T(8,128)} %get-tuple-element.51, f32[1024]{0:T(1024)S(1)} %convert_element_type.88, f32[1024]{0:T(1024)S(1)} %fusion.51), kind=kOutput, calls=%fused_computation.17 | convolution fusion | flops 8676966400 | bytes 54534144 | tf_op jit(solution)/shard_map/dot_general | solution.py:78
  318.3 15.7 multiply_reduce_fusion
  339.4 15.1 fusion.41
  354.5 25.5 %fusion.1 = (f32[8,1024]{1,0:T(8,128)S(1)}, f32[1024,1024,8]{1,0,2:T(8,128)}) fusion(f32[8,1024,1024]{1,2,0:T(8,128)} %get-tuple-element.49, f32[8,1024]{1,0:T(8,128)S(1)} %get-tuple-element.48, bf16[1024,128,1]{1,0,2:T(8,128)(2,1)S(1)} %copy-done.29, bf16[1024,8,128]{0,2,1:T(8,128)(2,1)} %bitcast.98), kind=kOutput, calls=%fused_computation.3 | convolution fusion | flops 2172641280 | bytes 69533696 | tf_op jit(solution)/shard_map/qhe,ke->hqk/dot_general | solution.py:116
  381.6 28.0 %fusion.3 = bf16[8,1024,1024]{1,2,0:T(8,128)(2,1)} fusion(f32[1024,1024,8]{1,0,2:T(8,128)} %get-tuple-element.56, f32[8,1024]{1,0:T(8,128)S(1)} %get-tuple-element.55, f32[8,1024,1024]{1,2,0:T(8,128)} %get-tuple-element.49, f32[8,1024]{1,0:T(8,128)S(1)} %get-tuple-element.48), kind=kLoop, calls=%fused_computation.5 | loop fusion | flops 33554432 | bytes 83951616 | tf_op jit(solution)/shard_map/convert_element_type | solution.py:122
  409.6 10.9 fusion.40
  422.1 7.3 fusion.46
  430.3 8.5 multiply_convert_fusion.1
  444.6 15.8 fusion.54
  461.9 18.5 %fusion.56 = f32[4096,1024]{1,0:T(8,128)} fusion(bf16[1024,1024]{1,0:T(8,128)(2,1)S(1)} %copy-done.10, f32[1024,4096]{1,0:T(8,128)} %get-tuple-element.53), kind=kOutput, calls=%fused_computation.85 | convolution fusion | flops 8627683328 | bytes 35651584 | tf_op jit(solution)/shard_map/tf,td->fd/dot_general | solution.py:97
  480.4 16.7 %add_convert_fusion = bf16[1024,1024]{0,1:T(8,128)(2,1)} fusion(f32[1024,1024]{0,1:T(8,128)} %get-tuple-element.51, bf16[4096,1024]{1,0:T(8,128)(2,1)} %all-gather.11.cloned.1.call-done, f32[1024,4096]{1,0:T(8,128)} %get-tuple-element.53), kind=kOutput, calls=%fused_computation.47 | convolution fusion | flops 8629780480 | bytes 31457280 | tf_op jit(solution)/shard_map/dot_general | solution.py:81
  511.3 39.4 %all-reduce.4 = (f32[1024]{0:T(1024)S(1)}, f32[1024]{0:T(1024)S(1)}) all-reduce(f32[1024]{0:T(1024)S(1)} %get-tuple-element.42, f32[1024]{0:T(1024)S(1)} %copy-done.25), channel_id=2, replica_groups=mesh['dp'=4,'fsdp'=8] {'dp','fsdp'}, use_global_device_ids=true, to_apply=%region_10.11.clone | all-reduce | flops 2048 | bytes 16384
  551.9 95.6 %reduce-scatter.9.cloned.1.call-done = f32[32,128]{1,0:T(8,128)} async-done(((f32[1024,128]{1,0:T(8,128)}), f32[32,128]{1,0:T(8,128)}) %reduce-scatter.9.cloned.1.call-update) | async-done | bytes 16400 | tf_op jit(solution)/shard_map/reduce_scatter | solution.py:150
  647.6 143.0 %reduce-scatter.13.cloned.1.call-done = f32[32,1024]{1,0:T(8,128)} async-done(((f32[1024,1024]{1,0:T(8,128)}), f32[32,1024]{1,0:T(8,128)}) %reduce-scatter.13.cloned.1.call-update) | async-done | bytes 131088 | tf_op jit(solution)/shard_map/reduce_scatter | solution.py:152
  790.6 144.2 %reduce-scatter.7.cloned.1.call-done = f32[32,1024]{1,0:T(8,128)} async-done(((f32[1024,1024]{1,0:T(8,128)}), f32[32,1024]{1,0:T(8,128)}) %reduce-scatter.7.cloned.1.call-update) | async-done | bytes 131088 | tf_op jit(solution)/shard_map/reduce_scatter | solution.py:149
  934.9 358.9 %reduce-scatter.15.cloned.1.call-done = f32[32,4096]{1,0:T(8,128)} async-done(((f32[1024,4096]{1,0:T(8,128)}), f32[32,4096]{1,0:T(8,128)}) %reduce-scatter.15.cloned.1.call-update) | async-done | bytes 524304 | tf_op jit(solution)/shard_map/reduce_scatter | solution.py:154
  1293.8 360.1 %reduce-scatter.17.cloned.1.call-done = f32[128,1024]{1,0:T(8,128)} async-done(((f32[4096,1024]{1,0:T(8,128)}), f32[128,1024]{1,0:T(8,128)}) %reduce-scatter.17.cloned.1.call-update) | async-done | bytes 524304 | tf_op jit(solution)/shard_map/reduce_scatter | solution.py:155
  (120 shorter events, 64.9 us)
Async XLA Ops:
  7.2 196.1 %all-gather.5.cloned.1.call-start = ((), (), s32[]{:S(2)}) async-start(), calls=%async_computation.6 | async-start | bytes 2162688 | tf_op jit(solution)/shard_map/all_gather | solution.py:40
  7.9 234.3 %all-gather.7.cloned.1.call-start = ((), (), s32[]{:S(2)}) async-start(), calls=%async_computation.7 | async-start | bytes 2162688 | tf_op jit(solution)/shard_map/all_gather | solution.py:43
  8.7 240.4 %all-gather.11.cloned.1.call-start = ((), (), s32[]{:S(2)}) async-start(), calls=%async_computation.9 | async-start | bytes 8650752 | tf_op jit(solution)/shard_map/all_gather | solution.py:74
  9.4 279.0 %all-gather.9.cloned.1.call-start = ((), (), s32[]{:S(2)}) async-start(), calls=%async_computation.8 | async-start | bytes 8650752 | tf_op jit(solution)/shard_map/all_gather | solution.py:73
  10.0 542.0 %reduce-scatter.11.cloned.1.call-start = ((), (), s32[]{:S(2)}) async-start(), calls=%async_computation.12 | async-start | bytes 540672 | tf_op jit(solution)/shard_map/reduce_scatter | solution.py:151
  55.2 143.1 %copy-start.17 = (f32[1024]{0:T(1024)}, f32[1024]{0:T(1024)S(1)}, u32[]{:S(2)}) copy-start(f32[1024]{0:T(1024)S(1)} %convert_element_type.78) | copy-start | bytes 12292
  55.2 8.2 copy-start.23
  55.2 75.9 %copy-start.24 = (bf16[32,128]{1,0:T(8,128)(2,1)S(1)}, bf16[32,128]{1,0:T(8,128)(2,1)}, u32[]{:S(2)}) copy-start(bf16[32,128]{1,0:T(8,128)(2,1)} %param.16) | copy-start | bytes 24580
  58.1 184.1 %copy-start = (bf16[1024,1024]{0,1:T(8,128)(2,1)}, bf16[1024,1024]{0,1:T(8,128)(2,1)S(1)}, u32[]{:S(2)}) copy-start(bf16[1024,1024]{0,1:T(8,128)(2,1)S(1)} %copy.57) | copy-start | bytes 6291460
  131.2 68.5 %copy-start.13 = (bf16[1024,128]{1,0:T(8,128)(2,1)}, bf16[1024,128]{1,0:T(8,128)(2,1)S(1)}, u32[]{:S(2)}) copy-start(bf16[1024,128]{1,0:T(8,128)(2,1)S(1)} %all_gather.34) | copy-start | bytes 786436
  197.3 2.4 copy-start.11
  199.7 9.7 copy-start.15
  318.3 15.8 copy-start.6
  318.3 15.8 copy-start.7
  339.4 15.1 copy-start.29
  354.5 25.5 %copy-start.3 = (bf16[1024,1024]{0,1:T(8,128)(2,1)S(1)}, bf16[1024,1024]{0,1:T(8,128)(2,1)}, u32[]{:S(2)}) copy-start(bf16[1024,1024]{0,1:T(8,128)(2,1)} %copy-done.2) | copy-start | bytes 6291460
  381.5 266.0 %reduce-scatter.9.cloned.1.call-start = ((), (), s32[]{:S(2)}) async-start(), calls=%async_computation.11 | async-start | bytes 540672 | tf_op jit(solution)/shard_map/reduce_scatter | solution.py:150
  422.1 368.6 %reduce-scatter.13.cloned.1.call-start = ((), (), s32[]{:S(2)}) async-start(), calls=%async_computation.13 | async-start | bytes 4325376 | tf_op jit(solution)/shard_map/reduce_scatter | solution.py:152
  429.4 505.5 %reduce-scatter.7.cloned.1.call-start = ((), (), s32[]{:S(2)}) async-start(), calls=%async_computation.10 | async-start | bytes 4325376 | tf_op jit(solution)/shard_map/reduce_scatter | solution.py:149
  444.5 849.3 %reduce-scatter.15.cloned.1.call-start = ((), (), s32[]{:S(2)}) async-start(), calls=%async_computation.14 | async-start | bytes 17301504 | tf_op jit(solution)/shard_map/reduce_scatter | solution.py:154
  460.4 1193.5 %reduce-scatter.17.cloned.1.call-start = ((), (), s32[]{:S(2)}) async-start(), calls=%async_computation.15 | async-start | bytes 17301504 | tf_op jit(solution)/shard_map/reduce_scatter | solution.py:155
  497.1 4.3 copy-start.14
  497.1 5.0 copy-start.9
  508.7 2.6 copy-start.25
  (16 other events, 28.2 us)
Sparse Core Ops, SparseCore 0:
  11.0 59.2 all-gather.4
  73.3 55.7 all-gather.6
  132.0 77.4 all-gather.10
  212.4 75.9 all-gather.8
  381.7 132.4 reduce-scatter.10
  517.0 130.5 reduce-scatter.8
  650.4 140.1 reduce-scatter.12
  793.5 141.3 reduce-scatter.6
  937.7 355.9 reduce-scatter.14
  1296.5 357.3 reduce-scatter.16
where the time goes:
time: 1670 us; the launch traced here: 1660 us
  waiting for transfers between devices  1130 us (68%)
  matrix products  242 us (14%)
  blocking collectives  215 us (13%)
  other arithmetic  34.9 us (2%)
  local copies, waits for them, and re-layouts  24.9 us (1%)
    reduce_scatter x1, waiting for transfers between devices, on_device(): lax.psum_scatter(grad_down, ('dp', 'fsdp'), scatter_dimension=0, tiled=True)  360 us
    reduce_scatter x1, waiting for transfers between devices, on_device(): lax.psum_scatter(grad_up, ('dp', 'fsdp'), scatter_dimension=0, tiled=True)  359 us
    reduce_scatter x1, waiting for transfers between devices, on_device(): lax.psum_scatter(grad_query, ('dp', 'fsdp'), scatter_dimension=0, tiled=T...  144 us
    reduce_scatter x1, waiting for transfers between devices, on_device(): lax.psum_scatter(grad_out, ('dp', 'fsdp'), scatter_dimension=0, tiled=True)  143 us
    reduce_scatter x1, waiting for transfers between devices, on_device(): lax.psum_scatter(grad_key, ('dp', 'fsdp'), scatter_dimension=0, tiled=True)  95.6 us
    unnamed x2, blocking collectives  81.6 us
    all_gather x1, blocking collectives, on_device(): lax.all_gather(key_weight, ('dp', 'fsdp'), axis=0, tiled=True)  67.7 us
    all_gather x1, blocking collectives, on_device(): lax.all_gather(value_weight, ('dp', 'fsdp'), axis=0, tiled=True)  66.1 us
  transfers between devices with their start and end apart: 10, of which 6 were waited for; matrix products, arithmetic and copies ran while one was open for 12% of the time, Pallas kernels for 0%

commit v1 on v0

v1 whole, which is shorter than its diff:
```python
import functools
import math

import jax
import jax.numpy as jnp
from jax import lax
from jax.experimental import pallas as pl
from jax.experimental.pallas import tpu as pltpu
from jax.sharding import Mesh, PartitionSpec as P

EPS = 1e-06
HEAD = 128
MIB = 2**20
f32 = jnp.float32
bf16 = jnp.bfloat16
VM = pl.BlockSpec(memory_space=pltpu.VMEM)
SM = pl.BlockSpec(memory_space=pltpu.SMEM)
GELU_A = math.sqrt(2.0 / math.pi)
GELU_B = GELU_A * 0.044715
SCORE_SCALE = 1.0 / math.sqrt(HEAD)
LOG2E = math.log2(math.e)


def nn(a, b):
    return lax.dot_general(a, b, (((1,), (0,)), ((), ())), preferred_element_type=f32)


def nt(a, b):
    return lax.dot_general(a, b, (((1,), (1,)), ((), ())), preferred_element_type=f32)


def tn(a, b):
    return lax.dot_general(a, b, (((0,), (0,)), ((), ())), preferred_element_type=f32)


def shape(dims, dtype):
    return jax.ShapeDtypeStruct(dims, dtype)


def call(kernel, outs, args, flops, exps=0, scratch=(), vmem=48, name=None, in_specs=None, **kw):
    moved = sum(math.prod(a.shape) * a.dtype.itemsize for a in (*args, *outs))
    return pl.pallas_call(
        kernel,
        out_shape=outs,
        in_specs=in_specs or [VM] * len(args),
        out_specs=kw.pop("out_specs", [VM] * len(outs)),
        scratch_shapes=list(scratch),
        compiler_params=pltpu.CompilerParams(vmem_limit_bytes=vmem * MIB),
        cost_estimate=pl.CostEstimate(flops=flops, bytes_accessed=moved, transcendentals=exps),
        name=name,
        **kw,
    )(*args)


def mask_bias(len_ref, first, rows, cols):
    q_pos = first + lax.broadcasted_iota(jnp.int32, (rows, 1), 0)
    k_pos = lax.broadcasted_iota(jnp.int32, (1, cols), 1)
    q_seg = jnp.zeros((rows, 1), jnp.int32)
    k_seg = jnp.zeros((1, cols), jnp.int32)
    end = jnp.int32(0)
    for slot in range(len_ref.shape[1]):
        end = end + len_ref[0, slot]
        q_seg = q_seg + (q_pos >= end).astype(jnp.int32)
        k_seg = k_seg + (k_pos >= end).astype(jnp.int32)
    k_seg = jnp.where(k_pos >= end, -1, k_seg)
    allowed = ((q_seg == k_seg) & (k_pos <= q_pos)) | (k_pos == q_pos)
    return jnp.where(allowed, 0.0, -1e30).astype(f32)


def gain_rows(block):
    return block.astype(f32).T


def norm_tile(x, gain):
    r = lax.rsqrt(jnp.mean(x * x, axis=-1, keepdims=True) + EPS)
    return x * r * gain


def attention_forward_kernel(len_ref, x_ref, w_ref, qkv_ref, att_ref, gains, normed, bias):
    rows, model = x_ref.shape
    wide = qkv_ref.shape[1]
    heads = (wide - 2 * HEAD) // HEAD
    gains[...] = gain_rows(w_ref[:, wide : wide + HEAD])[:8]

    @pl.loop(0, rows // 128)
    def _(t):
        at = pl.ds(pl.multiple_of(t * 128, 128), 128)
        normed[at, :] = norm_tile(x_ref[at, :].astype(f32), gains[0:1, :]).astype(bf16)

    @pl.loop(0, wide // 256)
    def _(j):
        at = pl.ds(pl.multiple_of(j * 256, 256), 256)
        qkv_ref[:, at] = nn(normed[...], w_ref[:, at]).astype(bf16)

    key_at = heads * HEAD
    for i in range(rows // 128):
        ext = (i + 1) * 128
        q_at = slice(i * 128, ext)
        bias[:, :ext] = mask_bias(len_ref, i * 128, 128, ext)

        @pl.loop(0, heads // 2)
        def _(pair):
            at = pl.ds(pl.multiple_of(pair * 256, 256), 256)
            both = qkv_ref[q_at, at]
            q = jnp.concatenate([both[:, :HEAD], both[:, HEAD:]], axis=0)
            s = nt(q, qkv_ref[:ext, key_at : key_at + HEAD]) * (SCORE_SCALE * LOG2E)
            s = s.reshape(2, 128, ext) + bias[:, :ext][None]
            s = s.reshape(256, ext)
            e = jnp.exp2(s - jnp.max(s, axis=-1, keepdims=True))
            p = e * (1.0 / jnp.sum(e, axis=-1, keepdims=True))
            o = nn(p.astype(bf16), qkv_ref[:ext, key_at + HEAD :]).astype(bf16)
            att_ref[q_at, at] = jnp.concatenate([o[:128], o[128:]], axis=1)


def attention_forward(lengths, x, w):
    rows, model = x.shape
    wide = w.shape[1] - HEAD
    return call(
        attention_forward_kernel,
        [shape((rows, wide), bf16), shape((rows, wide - 2 * HEAD), bf16)],
        (lengths, x, w),
        2 * rows * model * wide + 4 * rows * rows * model,
        rows * rows * 4,
        [pltpu.VMEM((8, model), f32), pltpu.VMEM((rows, model), bf16), pltpu.VMEM((128, rows), f32)],
        40,
        "attention_forward",
        [SM, VM, VM],
    )


def branch_kernel(x_ref, att_ref, wo_ref, w_ref, hidden_ref, nt_ref, gains):
    rows = x_ref.shape[0]
    gains[...] = gain_rows(w_ref[...])[:8]
    model = wo_ref.shape[1]

    @pl.loop(0, model // 256)
    def _(j):
        at = pl.ds(pl.multiple_of(j * 256, 256), 256)
        hidden_ref[:, at] = x_ref[:, at].astype(f32) + nn(att_ref[...], wo_ref[:, at])

    @pl.loop(0, rows // 128)
    def _(t):
        at = pl.ds(pl.multiple_of(t * 128, 128), 128)
        nt_ref[at, :] = norm_tile(hidden_ref[at, :], gains[1:2, :]).astype(bf16)


def branch(x, att, wo, w):
    rows, model = x.shape
    last = w.shape[1] // HEAD - 1
    whole = lambda a: pl.BlockSpec(a.shape, lambda i: (0, 0))
    return call(
        branch_kernel,
        [shape((rows, model), f32), shape((rows, model), bf16)],
        (x, att, wo, w),
        2 * rows * model * model,
        0,
        [pltpu.VMEM((8, model), f32)],
        40,
        "branch",
        [whole(x), whole(att), whole(wo), pl.BlockSpec((model, HEAD), lambda i: (0, last))],
        grid=(1,),
        out_specs=[whole(x), whole(x)],
    )


def gelu_both(v):
    v2 = v * v
    t = jnp.tanh(v * (GELU_A + GELU_B * v2))
    h = 0.5 + 0.5 * t
    a = v * h
    return a, h + (a - a * h) * ((2 * GELU_A) + (6 * GELU_B) * v2)


def ffn_kernel(groups, nt_o, nt_p, dy_o, dy_p, g_ref, act_o, act_p, gi_o, gi_p, gg_ref, us):
    model = nt_o.shape[1]
    part = g_ref.shape[1] // 4
    rows = model // groups
    for g in range(groups):
        us[g * rows : (g + 1) * rows, :] = g_ref[
            (g // 2) * rows : (g // 2 + 1) * rows, (g % 2) * part : (g % 2 + 1) * part
        ]
    tile = min(256, part)
    for j in range(part // tile):
        cols = slice(j * tile, (j + 1) * tile)
        for n_ref, y_ref, a_ref, i_ref in ((nt_o, dy_o, act_o, gi_o), (nt_p, dy_p, act_p, gi_p)):
            inner = nn(n_ref[...], us[:, cols])
            ga = nt(y_ref[...], g_ref[cols, 2 * part :])
            a, slope = gelu_both(inner)
            a_ref[:, cols] = a.astype(bf16)
            i_ref[:, cols] = (ga * slope).astype(bf16)
        v = (tn(nt_o[...], gi_o[:, cols]) + tn(nt_p[...], gi_p[:, cols])).astype(bf16)
        for g in range(groups):
            gg_ref[
                (g // 2) * rows : (g // 2 + 1) * rows,
                (g % 2) * part + j * tile : (g % 2) * part + (j + 1) * tile,
            ] = v[g * rows : (g + 1) * rows]
        v = tn(act_o[:, cols], dy_o[...]) + tn(act_p[:, cols], dy_p[...])
        gg_ref[cols, 2 * part :] = v.astype(bf16)


def ffn(groups, nt_o, nt_p, dy_o, dy_p, g):
    rows, model = nt_o.shape
    steps = g.shape[1] // (2 * model)
    part = model // 2
    once = pl.BlockSpec((rows, model), lambda c: (0, 0), pipeline_mode=pl.Buffered(1))
    piece = pl.BlockSpec((part, 2 * model), lambda c: (0, c))
    seen = pl.BlockSpec((rows, part), lambda c: (0, c))
    return call(
        functools.partial(ffn_kernel, groups),
        [shape((rows, steps * part), bf16)] * 4 + [shape(g.shape, bf16)],
        (nt_o, nt_p, dy_o, dy_p, g),
        steps * 16 * rows * model * part,
        steps * 2 * rows * part,
        [pltpu.VMEM((model, part), bf16)],
        48,
        "ffn",
        [once] * 4 + [piece],
        grid=(steps,),
        out_specs=[seen] * 4 + [piece],
    )


def ffn_sum_kernel(count, *refs):
    acts, gis = refs[:count], refs[count : 2 * count]
    downs, ups = refs[2 * count : 3 * count], refs[3 * count : 4 * count]
    out_ref, gn_ref = refs[4 * count :]
    out = gn = None
    for a, i, d, u in zip(acts, gis, downs, ups):
        o = nn(a[...], d[...])
        n = nt(i[...], u[...])
        out = o if out is None else out + o
        gn = n if gn is None else gn + n
    out_ref[...] = out.astype(bf16)
    gn_ref[...] = gn.astype(bf16)


def ffn_sum(groups, acts, gis, gathered):
    rows, part = acts[0][0].shape[0], gathered[0][0].shape[0]
    model = 2 * part
    count = len(acts)
    wide = model // groups
    a_specs = [pl.BlockSpec((rows, part), lambda g, c=c: (0, c), pipeline_mode=pl.Buffered(1)) for _, c in acts]
    d_specs = [pl.BlockSpec((part, wide), lambda g, c=c: (0, (c * 2 + 1) * groups + g)) for _, c in gathered]
    u_specs = [pl.BlockSpec((wide, part), lambda g, c=c: (g // 2, c * 4 + g % 2)) for _, c in gathered]
    out = pl.BlockSpec((rows, wide), lambda g: (0, g))
    return call(
        functools.partial(ffn_sum_kernel, count),
        [shape((rows, model), bf16)] * 2,
        (*[a for a, _ in acts], *[a for a, _ in gis], *[a for a, _ in gathered], *[a for a, _ in gathered]),
        count * 4 * rows * part * model,
        0,
        (),
        48,
        "ffn_sum",
        a_specs * 2 + d_specs + u_specs,
        grid=(groups,),
        out_specs=[out, out],
    )


def branch_backward_kernel(
    hidden_ref, gn_o, gn_p, out_o, out_p, dy_ref, wo_ref, w_ref, att_ref,
    output_ref, gh_ref, gatt_ref, gwo_ref, gg_ref, gains, gb,
):
    rows, model = hidden_ref.shape
    gains[...] = gain_rows(w_ref[...])[:8]
    gg_ref[...] = jnp.zeros_like(gg_ref)

    @pl.loop(0, rows // 64)
    def _(t):
        at = pl.ds(pl.multiple_of(t * 64, 64), 64)
        h = hidden_ref[at, :]
        output_ref[at, :] = (h + (out_o[at, :].astype(f32) + out_p[at, :].astype(f32))).astype(bf16)
        gn = gn_o[at, :].astype(f32) + gn_p[at, :].astype(f32)
        r = lax.rsqrt(jnp.mean(h * h, axis=-1, keepdims=True) + EPS)
        z = h * r
        gg_ref[1:2, :] += jnp.sum(gn * z, axis=0, keepdims=True)
        g = gn * gains[1:2, :]
        gh = dy_ref[at, :].astype(f32) + r * (g - z * jnp.mean(g * z, axis=-1, keepdims=True))
        gh_ref[at, :] = gh
        gb[at, :] = gh.astype(bf16)

    @pl.loop(0, model // 256)
    def _(j):
        at = pl.ds(pl.multiple_of(j * 256, 256), 256)
        gatt_ref[:, at] = nt(gb[...], wo_ref[at, :]).astype(bf16)
        gwo_ref[:, at] = tn(att_ref[...], gb[:, at]).astype(bf16)


def branch_backward(hidden, gn_o, gn_p, out_o, out_p, dy, wo, w, att):
    rows, model = hidden.shape
    last = w.shape[1] // HEAD - 1
    whole = lambda a: pl.BlockSpec(a.shape, lambda i: (0, 0))
    args = (hidden, gn_o, gn_p, out_o, out_p, dy, wo, w, att)
    outs = [
        shape((rows, model), bf16),
        shape((rows, model), f32),
        shape((rows, model), bf16),
        shape(wo.shape, bf16),
        shape((8, model), f32),
    ]
    return call(
        branch_backward_kernel,
        outs,
        args,
        4 * rows * model * model,
        0,
        [pltpu.VMEM((8, model), f32), pltpu.VMEM((rows, model), bf16)],
        56,
        "branch_backward",
        [*map(whole, args[:7]), pl.BlockSpec((model, HEAD), lambda i: (0, last)), whole(att)],
        grid=(1,),
        out_specs=[*map(whole, outs)],
    )


def attention_backward_kernel(len_ref, qkv_ref, ga_ref, g_ref, bias, dk, dv):
    rows, wide = qkv_ref.shape
    heads = (wide - 2 * HEAD) // HEAD
    key_at = heads * HEAD
    dk[...] = jnp.zeros_like(dk)
    dv[...] = jnp.zeros_like(dv)
    for i in range(rows // 128):
        ext = (i + 1) * 128
        q_at = slice(i * 128, ext)
        bias[:, :ext] = mask_bias(len_ref, i * 128, 128, ext)

        @pl.loop(0, heads // 2)
        def _(pair):
            at = pl.ds(pl.multiple_of(pair * 256, 256), 256)
            both = qkv_ref[q_at, at]
            q = jnp.concatenate([both[:, :HEAD], both[:, HEAD:]], axis=0)
            both = ga_ref[q_at, at]
            ga = jnp.concatenate([both[:, :HEAD], both[:, HEAD:]], axis=0)
            keys = qkv_ref[:ext, key_at : key_at + HEAD]
            s = nt(q, keys) * (SCORE_SCALE * LOG2E)
            s = s.reshape(2, 128, ext) + bias[:, :ext][None]
            s = s.reshape(256, ext)
            e = jnp.exp2(s - jnp.max(s, axis=-1, keepdims=True))
            p = e * (1.0 / jnp.sum(e, axis=-1, keepdims=True))
            gp = nt(ga, qkv_ref[:ext, key_at + HEAD :])
            pg = p * gp
            gs = (pg - p * jnp.sum(pg, axis=-1, keepdims=True)).astype(bf16)
            dv[:ext, :] += tn(p.astype(bf16), ga)
            dk[:ext, :] += tn(gs, q)
            gq = (nn(gs, keys) * SCORE_SCALE).astype(bf16)
            g_ref[q_at, at] = jnp.concatenate([gq[:128], gq[128:]], axis=1)

    g_ref[:, key_at : key_at + HEAD] = (dk[...] * SCORE_SCALE).astype(bf16)
    g_ref[:, key_at + HEAD :] = dv[...].astype(bf16)


def attention_backward(lengths, qkv, ga):
    rows, wide = qkv.shape
    model = ga.shape[1]
    return call(
        attention_backward_kernel,
        [shape(qkv.shape, bf16)],
        (lengths, qkv, ga),
        10 * rows * rows * model,
        rows * rows * 4,
        [pltpu.VMEM((128, rows), f32), pltpu.VMEM((rows, HEAD), f32), pltpu.VMEM((rows, HEAD), f32)],
        40,
        "attention_backward",
        [SM, VM, VM],
    )[0]


def input_backward_kernel(x_ref, g_ref, w_ref, gh_ref, gg_ref, gx_ref, gw_ref, gains, normed, gn, sums):
    rows, model = x_ref.shape
    wide = g_ref.shape[1]
    gains[...] = gain_rows(w_ref[:, wide : wide + HEAD])[:8]
    sums[...] = jnp.zeros_like(sums)
    sums[0:8, :] = gg_ref[...]

    @pl.loop(0, rows // 128)
    def _(t):
        at = pl.ds(pl.multiple_of(t * 128, 128), 128)
        normed[at, :] = norm_tile(x_ref[at, :].astype(f32), gains[0:1, :]).astype(bf16)

    @pl.loop(0, model // 256)
    def _(j):
        at = pl.ds(pl.multiple_of(j * 256, 256), 256)
        gn[:, at] = nt(g_ref[...], w_ref[at, :wide])

    @pl.loop(0, wide // 256)
    def _(j):
        at = pl.ds(pl.multiple_of(j * 256, 256), 256)
        gw_ref[:, at] = tn(normed[...], g_ref[:, at]).astype(bf16)

    @pl.loop(0, rows // 64)
    def _(t):
        at = pl.ds(pl.multiple_of(t * 64, 64), 64)
        x = x_ref[at, :].astype(f32)
        n = gn[at, :]
        r = lax.rsqrt(jnp.mean(x * x, axis=-1, keepdims=True) + EPS)
        z = x * r
        sums[0:1, :] += jnp.sum(n * z, axis=0, keepdims=True)
        g = n * gains[0:1, :]
        gx_ref[at, :] = (gh_ref[at, :] + r * (g - z * jnp.mean(g * z, axis=-1, keepdims=True))).astype(bf16)

    gw_ref[:, wide : wide + HEAD] = sums[...].T.astype(bf16)


def input_backward(x, g, w, gh, gg):
    rows, model = x.shape
    wide = g.shape[1]
    return call(
        input_backward_kernel,
        [shape(x.shape, bf16), shape(w.shape, bf16)],
        (x, g, w, gh, gg),
        4 * rows * model * wide,
        0,
        [
            pltpu.VMEM((8, model), f32),
            pltpu.VMEM((rows, model), bf16),
            pltpu.VMEM((rows, model), f32),
            pltpu.VMEM((HEAD, model), f32),
        ],
        56,
        "input_backward",
    )


def on_device(
    sizes, tokens, doc_lengths, gain_one, query_weight, key_weight, value_weight, out_weight,
    gain_two, up_weight, down_weight, cotangent,
):
    chips_x, fsdp = sizes
    every = ("x", "core", "fsdp")
    chips = ("x", "fsdp")
    core = lax.axis_index("core")
    swap = lambda a: lax.ppermute(a, "core", [(0, 1), (1, 0)])
    rows, model = tokens.shape
    shard = query_weight.shape[0]
    ff = up_weight.shape[1]
    chunks = down_weight.shape[0] // shard
    part = ff // (2 * chunks)
    groups = chips_x * 2

    gain_block = jnp.zeros((shard, HEAD), bf16).at[:, 0].set(gain_one).at[:, 1].set(gain_two)
    w_rows = jnp.concatenate([query_weight, key_weight, value_weight, gain_block], axis=1)
    w = lax.all_gather(w_rows, every, axis=0, tiled=True)
    wo = lax.all_gather(out_weight, every, axis=0, tiled=True)

    dy_p = swap(cotangent)
    up = up_weight.reshape(shard, chips_x, 2, fsdp, chunks, shard).transpose(2, 0, 4, 1, 3, 5)
    up = up.reshape(2, shard, chunks, part)
    up_keep = jnp.where(core == 0, up[0], up[1])
    up_come = swap(jnp.where(core == 0, up[1], up[0]))
    up_pair = jnp.where(core == 0, jnp.stack([up_keep, up_come], 2), jnp.stack([up_come, up_keep], 2))
    up_pair = up_pair.reshape(shard, chunks, 2 * part)
    down = down_weight.reshape(chunks, shard, model)
    per_call = 2
    gathered = []
    for first in range(0, chunks, per_call):
        pieces = []
        for c in range(first, first + per_call):
            pieces += [up_pair[:, c], down[c]]
        gathered.append(lax.all_gather(jnp.concatenate(pieces, axis=1), chips, axis=0, tiled=True))

    qkv, att = attention_forward(doc_lengths, tokens, w)
    hidden, nt_o = branch(tokens, att, wo, w)
    nt_p = swap(nt_o)

    acts_o, acts_p, gis_o, gis_p, places, ffn_sums = [], [], [], [], [], []
    for g in gathered:
        act_o, act_p, gi_o, gi_p, grads = ffn(groups, nt_o, nt_p, cotangent, dy_p, g)
        ffn_sums.append(lax.psum_scatter(grads, chips, scatter_dimension=0, tiled=True))
        for c in range(per_call):
            acts_o.append((act_o, c))
            acts_p.append((act_p, c))
            gis_o.append((gi_o, c))
            gis_p.append((gi_p, c))
            places.append((g, c))
    out_p, gn_p = ffn_sum(groups, acts_p, gis_p, places)
    out_r, gn_r = swap(out_p), swap(gn_p)
    out_o, gn_o = ffn_sum(groups, acts_o, gis_o, places)

    output, gh, gatt, gwo, gg = branch_backward(hidden, gn_o, gn_r, out_o, out_r, cotangent, wo, w, att)
    grad_out = lax.psum_scatter(gwo, every, scatter_dimension=0, tiled=True).astype(f32)
    gqkv = attention_backward(doc_lengths, qkv, gatt)
    grad_tokens, gw = input_backward(tokens, gqkv, w, gh, gg)
    gw = lax.psum_scatter(gw, every, scatter_dimension=0, tiled=True).astype(f32)

    sums = jnp.concatenate([s.reshape(shard, per_call, 2 * model) for s in ffn_sums], axis=1)
    grad_down = sums[:, :, model:].transpose(1, 0, 2).reshape(chunks * shard, model).astype(f32)
    g_up = sums[:, :, :model].reshape(shard, chunks, 2, part)
    keep = jnp.where(core == 0, g_up[:, :, 0], g_up[:, :, 1])
    come = swap(jnp.where(core == 0, g_up[:, :, 1], g_up[:, :, 0]))
    grad_up = jnp.where(core == 0, jnp.stack([keep, come], 0), jnp.stack([come, keep], 0))
    grad_up = grad_up.reshape(2, shard, chunks, chips_x, fsdp, shard).transpose(1, 3, 0, 4, 2, 5)
    grad_up = grad_up.reshape(shard, ff).astype(f32)

    qw = query_weight.shape[1]
    return (
        output,
        grad_tokens,
        gw[:, qw + 2 * HEAD],
        gw[:, :qw],
        gw[:, qw : qw + HEAD],
        gw[:, qw + HEAD : qw + 2 * HEAD],
        grad_out,
        gw[:, qw + 2 * HEAD + 1],
        grad_up,
        grad_down,
    )


def solution(mesh):
    dp, fsdp = mesh.shape["dp"], mesh.shape["fsdp"]
    split = Mesh(mesh.devices.reshape(dp // 2, 2, fsdp), ("x", "core", "fsdp"))
    rows = P(("x", "core", "fsdp"), None)
    line = P(("x", "core", "fsdp"))
    return jax.shard_map(
        functools.partial(on_device, (dp // 2, fsdp)),
        mesh=split,
        in_specs=(rows, rows, line, rows, rows, rows, rows, line, rows, rows, rows),
        out_specs=(rows, rows, line, rows, rows, rows, rows, line, rows, rows),
        check_vma=False,
    )
```

time: 1670 us -> 865 us (0.52)
  waiting for transfers between devices: 1130 us -> 602 us
  matrix products: 242 us -> 0 us
  blocking collectives: 215 us -> 0 us
  Pallas kernels: 0 us -> 187 us
  other arithmetic: 34.9 us -> 11.5 us
    reduce_scatter x6 -> x4, waiting for transfers between devices: 1100 us -> 406 us  [the longest x2 189 us: on_device(): lax.psum_scatter(grads, chips, scatter_dimension=0, tiled=True)]
    dot_general x23 -> x0, matrix products: 223 us -> none  [the longest x1 30 us: on_device(): inner = jnp.dot(normed_two, full_up, preferred_element_type=jnp.float32)]
    pallas_call x0 -> x9, Pallas kernels: none -> 187 us  [call(): pl.pallas_call(kernel, out_shape=outs, in_specs=in_specs or [VM] * len(ar...]
    all_gather x4, waiting for transfers between devices: 23.2 us -> 190 us  [the longest x2 110 us: on_device(): lax.all_gather(jnp.concatenate(pieces, axis=1), chips, axis=0, tiled=True)]
    all_gather x2 -> x0, blocking collectives: 134 us -> none  [the longest x1 67.7 us: on_device(): lax.all_gather(key_weight, ('dp', 'fsdp'), axis=0, tiled=True)]
    unnamed x2 -> x0, blocking collectives: 81.6 us -> none
    convert_element_type x5 -> x4, other arithmetic: 29.7 us -> 3.7 us  [the longest x1 1.5 us: on_device(): lax.psum_scatter(gwo, every, scatter_dimension=0, tiled=True).astype(f32)]
    sub x1 -> x0, matrix products: 19 us -> none  [on_device(): exponent = jnp.exp(scores - row_peak)]
  transfers between devices with their start and end apart: 10 -> 14, of which waited for: 6 -> 10; matrix products, arithmetic and copies ran while one was open for 12% -> 2% of each run, Pallas kernels for 0% -> 15%
where the time goes in v1:
time: 865 us; the launch traced here: 858 us
  waiting for transfers between devices  602 us (70%)
  Pallas kernels  187 us (22%)
  local copies, waits for them, and re-layouts  39.9 us (5%)
  between operations  14.7 us (2%)
  other arithmetic  11.5 us (1%)
    reduce_scatter x2, waiting for transfers between devices, on_device(): lax.psum_scatter(grads, chips, scatter_dimension=0, tiled=True)  189 us
    pallas_call x9, Pallas kernels, call(): pl.pallas_call(kernel, out_shape=outs, in_specs=in_specs or [VM] * len(ar...  187 us
    reduce_scatter x1, waiting for transfers between devices, on_device(): lax.psum_scatter(gw, every, scatter_dimension=0, tiled=True).astype(f32)  138 us
    all_gather x2, waiting for transfers between devices, on_device(): lax.all_gather(jnp.concatenate(pieces, axis=1), chips, axis=0, tiled=True)  110 us
    reduce_scatter x1, waiting for transfers between devices, on_device(): lax.psum_scatter(gwo, every, scatter_dimension=0, tiled=True).astype(f32)  78.4 us
    all_gather x1, waiting for transfers between devices, on_device(): w = lax.all_gather(w_rows, every, axis=0, tiled=True)  54.7 us
    unnamed x48, local copies, waits for them, and re-layouts  27.4 us
    all_gather x1, waiting for transfers between devices, on_device(): wo = lax.all_gather(out_weight, every, axis=0, tiled=True)  25.2 us
  transfers between devices with their start and end apart: 14, of which 10 were waited for; matrix products, arithmetic and copies ran while one was open for 2% of the time, Pallas kernels for 15%

profile of v1, /device:TPU:0, one launch (start us, length us, event | category | flops | bytes accessed | tf_op | source)
XLA Modules:
  0.0 857.7 jit_solution(15109352874926448090)
XLA Ops:
  13.8 1.7 reshape.163
  19.8 54.7 %all-gather.5.cloned.1.call-done.w_ref = bf16[1024,1408]{1,0:T(8,128)(2,1)} async-done(((bf16[32,1408]{1,0:T(8,128)(2,1)}), bf16[1024,1408]{1,0:T(8,128)(2,1)}) %all-gather.5.cloned.1.call-update) | async-done | bytes 2883600 | tf_op jit(solution)/shard_map/all_gather | solution.py:443
  74.5 1.8 copy-done
  76.3 1.6 copy-done.9
  77.9 26.8 %attention_forward.1 = (bf16[1024,1280]{1,0:T(8,128)(2,1)S(1)}, bf16[1024,1024]{1,0:T(8,128)(2,1)S(1)}) custom-call(s32[1,8]{1,0:T(1,128)S(1)} %copy-done.15, bf16[1024,1024]{1,0:T(8,128)(2,1)S(1)} %copy-done.9, bf16[1024,1408]{1,0:T(8,128)(2,1)S(1)} %copy-done), custom_call_target="tpu_custom_call" | custom-call | flops 6979321856 | bytes 9699360 | tf_op jit(solution)/shard_map/attention_forward/pallas_call | solution.py:42
  107.6 25.2 %all-gather.7.cloned.1.call-done.wo_ref = bf16[1024,1024]{1,0:T(8,128)(2,1)} async-done(((bf16[32,1024]{1,0:T(8,128)(2,1)}), bf16[1024,1024]{1,0:T(8,128)(2,1)}) %all-gather.7.cloned.1.call-update) | async-done | bytes 2097168 | tf_op jit(solution)/shard_map/all_gather | solution.py:444
  132.8 1.6 copy-done.6
  137.6 6.1 branch.1
  145.3 3.9 collective-permute-done.nt_p
  149.2 61.8 %all-gather.11.cloned.1.call-done.g_ref.refs_10_.refs_11_.refs_14_.refs_15_ = bf16[512,4096]{1,0:T(8,128)(2,1)} async-done(((bf16[32,4096]{1,0:T(8,128)(2,1)}), bf16[512,4096]{1,0:T(8,128)(2,1)}) %all-gather.11.cloned.1.call-update) | async-done | bytes 4194320 | tf_op jit(solution)/shard_map/all_gather | solution.py:460
  211.0 26.9 %ffn.3 = (bf16[1024,1024]{1,0:T(8,128)(2,1)S(1)}, bf16[1024,1024]{1,0:T(8,128)(2,1)S(1)}, bf16[1024,1024]{1,0:T(8,128)(2,1)}, bf16[1024,1024]{1,0:T(8,128)(2,1)}, bf16[512,4096]{1,0:T(8,128)(2,1)}) custom-call(bf16[1024,1024]{1,0:T(8,128)(2,1)} %copy-done.14, bf16[1024,1024]{1,0:T(8,128)(2,1)} %copy-done.22, bf16[1024,1024]{1,0:T(8,128)(2,1)} %dy_ref.1, ...), custom_call_target="tpu_custom_call" | custom-call | flops 17179869184 | bytes 25165824 | tf_op jit(solution)/shard_map/ffn/pallas_call | solution.py:42
  240.6 48.2 %all-gather.9.cloned.1.call-done.g_ref.refs_8_.refs_9_.refs_12_.refs_13_ = bf16[512,4096]{1,0:T(8,128)(2,1)} async-done(((bf16[32,4096]{1,0:T(8,128)(2,1)}), bf16[512,4096]{1,0:T(8,128)(2,1)}) %all-gather.9.cloned.1.call-update) | async-done | bytes 4194320 | tf_op jit(solution)/shard_map/all_gather | solution.py:460
  288.8 27.2 %ffn.2 = (bf16[1024,1024]{1,0:T(8,128)(2,1)S(1)}, bf16[1024,1024]{1,0:T(8,128)(2,1)S(1)}, bf16[1024,1024]{1,0:T(8,128)(2,1)}, bf16[1024,1024]{1,0:T(8,128)(2,1)}, bf16[512,4096]{1,0:T(8,128)(2,1)}) custom-call(bf16[1024,1024]{1,0:T(8,128)(2,1)} %copy-done.14, bf16[1024,1024]{1,0:T(8,128)(2,1)} %copy-done.22, bf16[1024,1024]{1,0:T(8,128)(2,1)} %dy_ref.1, ...), custom_call_target="tpu_custom_call" | custom-call | flops 17179869184 | bytes 25165824 | tf_op jit(solution)/shard_map/ffn/pallas_call | solution.py:42
  318.6 14.6 %ffn_sum.3 = (bf16[1024,1024]{1,0:T(8,128)(2,1)S(1)}, bf16[1024,1024]{1,0:T(8,128)(2,1)S(1)}) custom-call(bf16[1024,1024]{1,0:T(8,128)(2,1)} %copy-done.5, bf16[1024,1024]{1,0:T(8,128)(2,1)} %copy-done.5, bf16[1024,1024]{1,0:T(8,128)(2,1)} %copy-done.4, bf16[1024,1024]{1,0:T(8,128)(2,1)} %copy-done.4, bf16[1024,1024]{1,0:T(8,128)(2,1)} %get-tuple-element.69.refs_4_.refs_5_, ...), custom_call_target="tpu_custom_call" | custom-call | flops 8589934592 | bytes 54525952 | tf_op jit(solution)/shard_map/ffn_sum/pallas_call | solution.py:42
  333.8 14.8 %ffn_sum.2 = (bf16[1024,1024]{1,0:T(8,128)(2,1)S(1)}, bf16[1024,1024]{1,0:T(8,128)(2,1)S(1)}) custom-call(bf16[1024,1024]{1,0:T(8,128)(2,1)} %copy-done.3, bf16[1024,1024]{1,0:T(8,128)(2,1)} %copy-done.3, bf16[1024,1024]{1,0:T(8,128)(2,1)} %copy-done.2, bf16[1024,1024]{1,0:T(8,128)(2,1)} %copy-done.2, bf16[1024,1024]{1,0:T(8,128)(2,1)} %get-tuple-element.64.refs_4_.refs_5_, ...), custom_call_target="tpu_custom_call" | custom-call | flops 8589934592 | bytes 54525952 | tf_op jit(solution)/shard_map/ffn_sum/pallas_call | solution.py:42
  353.2 18.6 %branch_backward.1 = (bf16[1024,1024]{1,0:T(8,128)(2,1)}, f32[1024,1024]{1,0:T(8,128)}, bf16[1024,1024]{1,0:T(8,128)(2,1)}, bf16[1024,1024]{1,0:T(8,128)(2,1)}, f32[8,1024]{1,0:T(8,128)}) custom-call(f32[1024,1024]{1,0:T(8,128)} %get-tuple-element.60.hidden_ref, bf16[1024,1024]{1,0:T(8,128)(2,1)} %copy-done.12, bf16[1024,1024]{1,0:T(8,128)(2,1)} %copy-done.19, ...), custom_call_target="tpu_custom_call" | custom-call | flops 4294967296 | bytes 32276480 | tf_op jit(solution)/shard_map/branch_backward/pallas_call | solution.py:42
  374.1 1.7 copy-done.18
  375.8 33.0 %attention_backward.1.g_ref = bf16[1024,1280]{1,0:T(8,128)(2,1)S(1)} custom-call(s32[1,8]{1,0:T(1,128)S(1)} %copy-done.15, bf16[1024,1280]{1,0:T(8,128)(2,1)S(1)} %copy-done.18, bf16[1024,1024]{1,0:T(8,128)(2,1)S(1)} %copy-done.13), custom_call_target="tpu_custom_call" | custom-call | flops 10737418240 | bytes 7340064 | tf_op jit(solution)/shard_map/attention_backward/pallas_call | solution.py:42
  410.3 19.5 %input_backward.1 = (bf16[1024,1024]{1,0:T(8,128)(2,1)}, bf16[1024,1408]{1,0:T(8,128)(2,1)}) custom-call(bf16[1024,1024]{1,0:T(8,128)(2,1)} %x_ref.5, bf16[1024,1280]{1,0:T(8,128)(2,1)} %copy-done.16, bf16[1024,1408]{1,0:T(8,128)(2,1)} %all-gather.5.cloned.1.call-done.w_ref, f32[1024,1024]{1,0:T(8,128)} %get-tuple-element.77.gh_ref, ...), custom_call_target="tpu_custom_call" | custom-call | flops 5368709120 | bytes 16809984 | tf_op jit(solution)/shard_map/input_backward/pallas_call | solution.py:42
  429.8 78.4 %reduce-scatter.7.cloned.1.call-done = bf16[32,1024]{1,0:T(8,128)(2,1)} async-done(((bf16[1024,1024]{1,0:T(8,128)(2,1)}), bf16[32,1024]{1,0:T(8,128)(2,1)}) %reduce-scatter.7.cloned.1.call-update) | async-done | bytes 65552 | tf_op jit(solution)/shard_map/reduce_scatter | solution.py:481
  509.7 93.1 %reduce-scatter.9.cloned.1.call-done = bf16[32,4096]{1,0:T(8,128)(2,1)} async-done(((bf16[512,4096]{1,0:T(8,128)(2,1)}), bf16[32,4096]{1,0:T(8,128)(2,1)}) %reduce-scatter.9.cloned.1.call-update) | async-done | bytes 262160 | tf_op jit(solution)/shard_map/reduce_scatter | solution.py:469
  603.8 95.9 %reduce-scatter.11.cloned.1.call-done = bf16[32,4096]{1,0:T(8,128)(2,1)} async-done(((bf16[512,4096]{1,0:T(8,128)(2,1)}), bf16[32,4096]{1,0:T(8,128)(2,1)}) %reduce-scatter.11.cloned.1.call-update) | async-done | bytes 262160 | tf_op jit(solution)/shard_map/reduce_scatter | solution.py:469
  702.7 138.4 %reduce-scatter.5.cloned.1.call-done = bf16[32,1408]{1,0:T(8,128)(2,1)} async-done(((bf16[1024,1408]{1,0:T(8,128)(2,1)}), bf16[32,1408]{1,0:T(8,128)(2,1)}) %reduce-scatter.5.cloned.1.call-update) | async-done | bytes 90128 | tf_op jit(solution)/shard_map/reduce_scatter | solution.py:484
  847.9 2.8 reshape.167
  (103 shorter events, 44.8 us)
Async XLA Ops:
  7.2 67.3 %all-gather.5.cloned.1.call-start = ((), (), s32[]{:S(2)}) async-start(), calls=%async_computation.4 | async-start | bytes 2973696 | tf_op jit(solution)/shard_map/all_gather | solution.py:443
  13.0 119.8 %all-gather.7.cloned.1.call-start = ((), (), s32[]{:S(2)}) async-start(), calls=%async_computation.5 | async-start | bytes 2162688 | tf_op jit(solution)/shard_map/all_gather | solution.py:444
  13.8 197.2 %all-gather.11.cloned.1.call-start = ((), (), s32[]{:S(2)}) async-start(), calls=%async_computation.7 | async-start | bytes 4456448 | tf_op jit(solution)/shard_map/all_gather | solution.py:460
  16.2 1.5 collective-permute-start.2
  16.8 57.8 %copy-start.15 = (s32[1,8]{1,0:T(1,128)S(1)}, s32[1,8]{1,0:T(1,128)}, u32[]{:S(2)}) copy-start(s32[1,8]{1,0:T(1,128)} %len_ref.3) | copy-start | bytes 100
  18.6 270.2 %all-gather.9.cloned.1.call-start = ((), (), s32[]{:S(2)}) async-start(), calls=%async_computation.6 | async-start | bytes 4456448 | tf_op jit(solution)/shard_map/all_gather | solution.py:460
  19.4 488.9 %reduce-scatter.7.cloned.1.call-start = ((), (), s32[]{:S(2)}) async-start(), calls=%async_computation.9 | async-start | bytes 2162688 | tf_op jit(solution)/shard_map/reduce_scatter | solution.py:481
  19.4 125.9 %collective-permute-start.1 = (bf16[1024,1024]{1,0:T(8,128)(2,1)}, bf16[1024,1024]{1,0:T(8,128)(2,1)}, u32[]{:S(2)}, u32[]{:S(2)}) collective-permute-start(bf16[1024,1024]{1,0:T(8,128)(2,1)} %dy_ref.1), channel_id=1, source_target_pairs={{0,8},{8,0},{1,9},{9,1},{2,10},{10,2},{3,11},{11,3},{4,12},{12,4},... | collective-permute-start | bytes 6291464 | tf_op jit(solution)/shard_map/ppermute | solution.py:433
  74.5 1.8 copy-start
  76.3 1.6 copy-start.9
  77.9 54.9 %copy-start.1 = (bf16[1024,1408]{1,0:T(8,128)(2,1)S(1)}, bf16[1024,1408]{1,0:T(8,128)(2,1)}, u32[]{:S(2)}) copy-start(bf16[1024,1408]{1,0:T(8,128)(2,1)} %all-gather.5.cloned.1.call-done.w_ref) | copy-start | bytes 8650756
  132.8 1.6 copy-start.6
  134.4 1.6 copy-start.8
  145.1 4.2 collective-permute-start
  149.2 61.8 %copy-start.22 = (bf16[1024,1024]{1,0:T(8,128)(2,1)}, bf16[1024,1024]{1,0:T(8,128)(2,1)S(1)}, u32[]{:S(2)}) copy-start(bf16[1024,1024]{1,0:T(8,128)(2,1)S(1)} %collective-permute-done.nt_p) | copy-start | bytes 6291460
  333.2 18.0 %collective-permute-start.3 = (bf16[1024,1024]{1,0:T(8,128)(2,1)S(1)}, bf16[1024,1024]{1,0:T(8,128)(2,1)S(1)}, u32[]{:S(2)}, u32[]{:S(2)}) collective-permute-start(bf16[1024,1024]{1,0:T(8,128)(2,1)S(1)} %get-tuple-element.71), channel_id=1, source_target_pairs={{0,8},{8,0},{1,9},{9,1},{2,10},{10,2},{3,11},{11,3},{4,12},{12,4},... | collective-permute-start | bytes 6291464 | tf_op jit(solution)/shard_map/ppermute | solution.py:433
  333.3 17.9 %collective-permute-start.4 = (bf16[1024,1024]{1,0:T(8,128)(2,1)S(1)}, bf16[1024,1024]{1,0:T(8,128)(2,1)S(1)}, u32[]{:S(2)}, u32[]{:S(2)}) collective-permute-start(bf16[1024,1024]{1,0:T(8,128)(2,1)S(1)} %get-tuple-element.73), channel_id=1, source_target_pairs={{0,8},{8,0},{1,9},{9,1},{2,10},{10,2},{3,11},{11,3},{4,12},{12,4},... | collective-permute-start | bytes 6291464 | tf_op jit(solution)/shard_map/ppermute | solution.py:433
  351.2 2.1 copy-start.20
  371.8 231.0 %reduce-scatter.9.cloned.1.call-start = ((), (), s32[]{:S(2)}) async-start(), calls=%async_computation.10 | async-start | bytes 4456448 | tf_op jit(solution)/shard_map/reduce_scatter | solution.py:469
  372.4 327.3 %reduce-scatter.11.cloned.1.call-start = ((), (), s32[]{:S(2)}) async-start(), calls=%async_computation.11 | async-start | bytes 4456448 | tf_op jit(solution)/shard_map/reduce_scatter | solution.py:469
  372.5 1.6 copy-start.13
  373.2 467.9 %reduce-scatter.5.cloned.1.call-start = ((), (), s32[]{:S(2)}) async-start(), calls=%async_computation.8 | async-start | bytes 2973696 | tf_op jit(solution)/shard_map/reduce_scatter | solution.py:484
  374.1 1.7 copy-start.18
  702.6 143.2 %collective-permute-start.5 = (bf16[32,4,512]{2,0,1:T(8,128)(2,1)S(1)}, bf16[32,4,512]{2,0,1:T(8,128)(2,1)S(1)}, u32[]{:S(2)}, u32[]{:S(2)}) collective-permute-start(bf16[32,4,512]{2,0,1:T(8,128)(2,1)S(1)} %bitcast.54), channel_id=1, source_target_pairs={{0,8},{8,0},{1,9},{9,1},{2,10},{10,2},{3,11},{11,3},{4,12},{12,4},... | collective-permute-start | bytes 393224 | tf_op jit(solution)/shard_map/ppermute | solution.py:433
  (13 other events, 18.0 us)
Sparse Core Ops, SparseCore 0:
  13.1 61.3 all-gather.4
  77.5 55.2 all-gather.6
  136.2 74.7 all-gather.10
  214.2 74.4 all-gather.8
  372.0 136.2 reduce-scatter.6
  510.5 92.3 reduce-scatter.8
  605.3 94.3 reduce-scatter.10
  702.1 138.9 reduce-scatter.4

commit v2 on v1

--- a/solution.py
+++ b/solution.py
@@ -52,6 +52,44 @@
     )(*args)
 
 
+def chip_at(sizes, me_ref, rx, rb, ra, sign):
+    nx, na, nb = sizes
+    x = lax.rem(me_ref[0] + (sign * rx) % nx, nx)
+    a = lax.rem(me_ref[1] + (sign * ra) % na, na)
+    b = lax.rem(me_ref[2] + (sign * rb) % nb, nb)
+    return x, a * nb + b
+
+
+def blocks_of(sizes):
+    nx, na, nb = sizes
+    return [(rx, rb, ra) for rx in range(nx) for rb in range(nb) for ra in range(na)]
+
+
+def row_of(sizes, me_ref, rx, rb, ra, sign, core, shard):
+    x, f = chip_at(sizes, me_ref, rx, rb, ra, sign)
+    return pl.ds(pl.multiple_of(((x * 2 + core) * (sizes[1] * sizes[2]) + f) * shard, shard), shard)
+
+
+def assemble(sizes, me_ref, refs, whole_ref):
+    nx, na, nb = sizes
+    shard = refs[0].shape[0] // na
+    for other in range(2):
+        core = me_ref[3] if other == 0 else 1 - me_ref[3]
+        for rx, rb, ra in blocks_of(sizes):
+            ref = refs[(other * nx + rx) * nb + rb]
+            whole_ref[row_of(sizes, me_ref, rx, rb, ra, -1, core, shard), :] = ref[ra * shard : (ra + 1) * shard, :]
+
+
+def hand_out(sizes, me_ref, whole_ref, keep_ref, send_ref, x_outer):
+    nx, na, nb = sizes
+    shard = keep_ref.shape[0] // (nx * na * nb)
+    for other, ref in enumerate((keep_ref, send_ref)):
+        core = me_ref[3] if other == 0 else 1 - me_ref[3]
+        for rx, rb, ra in blocks_of(sizes):
+            at = (((rx * nb + rb) if x_outer else (rb * nx + rx)) * na + ra) * shard
+            ref[at : at + shard, :] = whole_ref[row_of(sizes, me_ref, rx, rb, ra, 1, core, shard), :]
+
+
 def mask_bias(len_ref, first, rows, cols):
     q_pos = first + lax.broadcasted_iota(jnp.int32, (rows, 1), 0)
     k_pos = lax.broadcasted_iota(jnp.int32, (1, cols), 1)
@@ -76,7 +114,9 @@
     return x * r * gain
 
 
-def attention_forward_kernel(len_ref, x_ref, w_ref, qkv_ref, att_ref, gains, normed, bias):
+def attention_forward_kernel(sizes, me_ref, len_ref, x_ref, *refs):
+    *pieces, w_ref, qkv_ref, att_ref, gains, normed, bias = refs
+    assemble(sizes, me_ref, pieces, w_ref)
     rows, model = x_ref.shape
     wide = qkv_ref.shape[1]
     heads = (wide - 2 * HEAD) // HEAD
@@ -112,23 +152,26 @@
             att_ref[q_at, at] = jnp.concatenate([o[:128], o[128:]], axis=1)
 
 
-def attention_forward(lengths, x, w):
+def attention_forward(sizes, me, lengths, x, pieces):
     rows, model = x.shape
-    wide = w.shape[1] - HEAD
+    columns = pieces[0].shape[1]
+    wide = columns - HEAD
     return call(
-        attention_forward_kernel,
-        [shape((rows, wide), bf16), shape((rows, wide - 2 * HEAD), bf16)],
-        (lengths, x, w),
+        functools.partial(attention_forward_kernel, sizes),
+        [shape((model, columns), bf16), shape((rows, wide), bf16), shape((rows, wide - 2 * HEAD), bf16)],
+        (me, lengths, x, *pieces),
         2 * rows * model * wide + 4 * rows * rows * model,
         rows * rows * 4,
         [pltpu.VMEM((8, model), f32), pltpu.VMEM((rows, model), bf16), pltpu.VMEM((128, rows), f32)],
         40,
         "attention_forward",
-        [SM, VM, VM],
-    )
-
-
-def branch_kernel(x_ref, att_ref, wo_ref, w_ref, hidden_ref, nt_ref, gains):
+        [SM, SM] + [VM] * (1 + len(pieces)),
+    )
+
+
+def branch_kernel(sizes, me_ref, x_ref, att_ref, w_ref, *refs):
+    *pieces, wo_ref, hidden_ref, nt_ref, gains = refs
+    assemble(sizes, me_ref, pieces, wo_ref)
     rows = x_ref.shape[0]
     gains[...] = gain_rows(w_ref[...])[:8]
     model = wo_ref.shape[1]
@@ -144,22 +187,23 @@
         nt_ref[at, :] = norm_tile(hidden_ref[at, :], gains[1:2, :]).astype(bf16)
 
 
-def branch(x, att, wo, w):
+def branch(sizes, me, x, att, w, pieces):
     rows, model = x.shape
     last = w.shape[1] // HEAD - 1
     whole = lambda a: pl.BlockSpec(a.shape, lambda i: (0, 0))
+    wo = shape((model, model), bf16)
     return call(
-        branch_kernel,
-        [shape((rows, model), f32), shape((rows, model), bf16)],
-        (x, att, wo, w),
+        functools.partial(branch_kernel, sizes),
+        [wo, shape((rows, model), f32), shape((rows, model), bf16)],
+        (me, x, att, w, *pieces),
         2 * rows * model * model,
         0,
         [pltpu.VMEM((8, model), f32)],
         40,
         "branch",
-        [whole(x), whole(att), whole(wo), pl.BlockSpec((model, HEAD), lambda i: (0, last))],
+        [SM, whole(x), whole(att), pl.BlockSpec((model, HEAD), lambda i: (0, last)), *map(whole, pieces)],
         grid=(1,),
-        out_specs=[whole(x), whole(x)],
+        out_specs=[whole(wo), whole(x), whole(x)],
     )
 
 
@@ -171,58 +215,77 @@
     return a, h + (a - a * h) * ((2 * GELU_A) + (6 * GELU_B) * v2)
 
 
-def ffn_kernel(groups, nt_o, nt_p, dy_o, dy_p, g_ref, act_o, act_p, gi_o, gi_p, gg_ref, us):
-    model = nt_o.shape[1]
-    part = g_ref.shape[1] // 4
-    rows = model // groups
-    for g in range(groups):
-        us[g * rows : (g + 1) * rows, :] = g_ref[
-            (g // 2) * rows : (g // 2 + 1) * rows, (g % 2) * part : (g % 2 + 1) * part
-        ]
-    tile = min(256, part)
-    for j in range(part // tile):
-        cols = slice(j * tile, (j + 1) * tile)
-        for n_ref, y_ref, a_ref, i_ref in ((nt_o, dy_o, act_o, gi_o), (nt_p, dy_p, act_p, gi_p)):
-            inner = nn(n_ref[...], us[:, cols])
-            ga = nt(y_ref[...], g_ref[cols, 2 * part :])
-            a, slope = gelu_both(inner)
-            a_ref[:, cols] = a.astype(bf16)
-            i_ref[:, cols] = (ga * slope).astype(bf16)
-        v = (tn(nt_o[...], gi_o[:, cols]) + tn(nt_p[...], gi_p[:, cols])).astype(bf16)
-        for g in range(groups):
-            gg_ref[
-                (g // 2) * rows : (g // 2 + 1) * rows,
-                (g % 2) * part + j * tile : (g % 2) * part + (j + 1) * tile,
-            ] = v[g * rows : (g + 1) * rows]
-        v = tn(act_o[:, cols], dy_o[...]) + tn(act_p[:, cols], dy_p[...])
-        gg_ref[cols, 2 * part :] = v.astype(bf16)
-
-
-def ffn(groups, nt_o, nt_p, dy_o, dy_p, g):
+def ffn_kernel(sizes, x_outer, me_ref, nt_o, nt_p, dy_o, dy_p, *refs):
+    nx, na, nb = sizes
+    pieces, refs = refs[: nx * nb], refs[nx * nb :]
+    act_o, act_p, gi_o, gi_p, up_ref, down_ref = refs[:6]
+    outs, (gu, gd) = refs[6:-2], refs[-2:]
+    part, model = down_ref.shape
+    shard = part // (nx * na * nb)
+    step = pl.program_id(0)
+    tile = act_o.shape[1]
+
+    @pl.when(step == 0)
+    def _():
+        for rx, rb, ra in blocks_of(sizes):
+            ref = pieces[rx * nb + rb]
+            at = slice(ra * shard, (ra + 1) * shard)
+            for core in range(2):
+                up_ref[row_of(sizes, me_ref, rx, rb, ra, -1, core, shard), :] = ref[at, core * part : (core + 1) * part]
+            x, f = chip_at(sizes, me_ref, rx, rb, ra, -1)
+            down_ref[pl.ds(pl.multiple_of((x * na * nb + f) * shard, shard), shard), :] = ref[at, 2 * part :]
+
+    cols = pl.ds(pl.multiple_of(step * tile, tile), tile)
+    for n_ref, y_ref, a_ref, i_ref in ((nt_o, dy_o, act_o, gi_o), (nt_p, dy_p, act_p, gi_p)):
+        inner = nn(n_ref[...], up_ref[:, cols])
+        ga = nt(y_ref[...], down_ref[cols, :])
+        a, slope = gelu_both(inner)
+        a_ref[...] = a.astype(bf16)
+        i_ref[...] = (ga * slope).astype(bf16)
+    gu[:, cols] = (tn(nt_o[...], gi_o[...]) + tn(nt_p[...], gi_p[...])).astype(bf16)
+    gd[cols, :] = (tn(act_o[...], dy_o[...]) + tn(act_p[...], dy_p[...])).astype(bf16)
+
+    @pl.when(step == pl.num_programs(0) - 1)
+    def _():
+        for rx, rb, ra in blocks_of(sizes):
+            first, second, count = (rx, rb, nb) if x_outer else (rb, rx, nx)
+            at = slice((second * na + ra) * shard, (second * na + ra + 1) * shard)
+            for core in range(2):
+                outs[first][at, core * part : (core + 1) * part] = gu[row_of(sizes, me_ref, rx, rb, ra, 1, core, shard), :]
+            x, f = chip_at(sizes, me_ref, rx, rb, ra, 1)
+            outs[first][at, 2 * part :] = gd[pl.ds(pl.multiple_of((x * na * nb + f) * shard, shard), shard), :]
+
+
+def ffn(sizes, x_outer, me, nt_o, nt_p, dy_o, dy_p, pieces):
+    nx, na, nb = sizes
     rows, model = nt_o.shape
-    steps = g.shape[1] // (2 * model)
     part = model // 2
+    tile = 256
     once = pl.BlockSpec((rows, model), lambda c: (0, 0), pipeline_mode=pl.Buffered(1))
-    piece = pl.BlockSpec((part, 2 * model), lambda c: (0, c))
-    seen = pl.BlockSpec((rows, part), lambda c: (0, c))
-    return call(
-        functools.partial(ffn_kernel, groups),
-        [shape((rows, steps * part), bf16)] * 4 + [shape(g.shape, bf16)],
-        (nt_o, nt_p, dy_o, dy_p, g),
-        steps * 16 * rows * model * part,
-        steps * 2 * rows * part,
-        [pltpu.VMEM((model, part), bf16)],
-        48,
+    whole = lambda a: pl.BlockSpec(a.shape, lambda c: (0, 0), pipeline_mode=pl.Buffered(1))
+    seen = pl.BlockSpec((rows, tile), lambda c: (0, c))
+    firsts, lines = (nx, nb) if x_outer else (nb, nx)
+    up, down = shape((model, part), bf16), shape((part, model), bf16)
+    grads = [shape((part // firsts, 2 * model), bf16)] * firsts
+    outs = call(
+        functools.partial(ffn_kernel, sizes, x_outer),
+        [shape((rows, part), bf16)] * 4 + [up, down] + grads,
+        (me, nt_o, nt_p, dy_o, dy_p, *pieces),
+        16 * rows * model * part,
+        2 * rows * part,
+        [pltpu.VMEM((model, part), bf16), pltpu.VMEM((part, model), bf16)],
+        44,
         "ffn",
-        [once] * 4 + [piece],
-        grid=(steps,),
-        out_specs=[seen] * 4 + [piece],
-    )
+        [SM] + [once] * 4 + [whole(p) for p in pieces],
+        grid=(part // tile,),
+        out_specs=[seen] * 4 + [whole(up), whole(down), *map(whole, grads)],
+    )
+    return outs[:4], outs[4], outs[5], outs[6:]
 
 
 def ffn_sum_kernel(count, *refs):
     acts, gis = refs[:count], refs[count : 2 * count]
-    downs, ups = refs[2 * count : 3 * count], refs[3 * count : 4 * count]
+    ups, downs = refs[2 * count : 3 * count], refs[3 * count : 4 * count]
     out_ref, gn_ref = refs[4 * count :]
     out = gn = None
     for a, i, d, u in zip(acts, gis, downs, ups):
@@ -234,33 +297,33 @@
     gn_ref[...] = gn.astype(bf16)
 
 
-def ffn_sum(groups, acts, gis, gathered):
-    rows, part = acts[0][0].shape[0], gathered[0][0].shape[0]
+def ffn_sum(acts, gis, ups, downs):
+    rows, part = acts[0].shape
     model = 2 * part
     count = len(acts)
-    wide = model // groups
-    a_specs = [pl.BlockSpec((rows, part), lambda g, c=c: (0, c), pipeline_mode=pl.Buffered(1)) for _, c in acts]
-    d_specs = [pl.BlockSpec((part, wide), lambda g, c=c: (0, (c * 2 + 1) * groups + g)) for _, c in gathered]
-    u_specs = [pl.BlockSpec((wide, part), lambda g, c=c: (g // 2, c * 4 + g % 2)) for _, c in gathered]
+    wide = 256
+    held = pl.BlockSpec((rows, part), lambda g: (0, 0), pipeline_mode=pl.Buffered(1))
     out = pl.BlockSpec((rows, wide), lambda g: (0, g))
     return call(
         functools.partial(ffn_sum_kernel, count),
         [shape((rows, model), bf16)] * 2,
-        (*[a for a, _ in acts], *[a for a, _ in gis], *[a for a, _ in gathered], *[a for a, _ in gathered]),
+        (*acts, *gis, *ups, *downs),
         count * 4 * rows * part * model,
         0,
         (),
-        48,
+        44,
         "ffn_sum",
-        a_specs * 2 + d_specs + u_specs,
-        grid=(groups,),
+        [held] * (2 * count)
+        + [pl.BlockSpec((wide, part), lambda g: (g, 0))] * count
+        + [pl.BlockSpec((part, wide), lambda g: (0, g))] * count,
+        grid=(model // wide,),
         out_specs=[out, out],
     )
 
 
 def branch_backward_kernel(
-    hidden_ref, gn_o, gn_p, out_o, out_p, dy_ref, wo_ref, w_ref, att_ref,
-    output_ref, gh_ref, gatt_ref, gwo_ref, gg_ref, gains, gb,
+    sizes, x_outer, me_ref, hidden_ref, gn_o, gn_p, out_o, out_p, dy_ref, wo_ref, w_ref, att_ref,
+    output_ref, gh_ref, gatt_ref, gg_ref, keep_ref, send_ref, gains, gb, gwo_ref,
 ):
     rows, model = hidden_ref.shape
     gains[...] = gain_rows(w_ref[...])[:8]
@@ -286,29 +349,33 @@
         gatt_ref[:, at] = nt(gb[...], wo_ref[at, :]).astype(bf16)
         gwo_ref[:, at] = tn(att_ref[...], gb[:, at]).astype(bf16)
 
-
-def branch_backward(hidden, gn_o, gn_p, out_o, out_p, dy, wo, w, att):
+    hand_out(sizes, me_ref, gwo_ref, keep_ref, send_ref, x_outer)
+
+
+def branch_backward(sizes, x_outer, me, hidden, gn_o, gn_p, out_o, out_p, dy, wo, w, att):
     rows, model = hidden.shape
     last = w.shape[1] // HEAD - 1
     whole = lambda a: pl.BlockSpec(a.shape, lambda i: (0, 0))
-    args = (hidden, gn_o, gn_p, out_o, out_p, dy, wo, w, att)
+    args = (me, hidden, gn_o, gn_p, out_o, out_p, dy, wo, w, att)
+    half = shape((model // 2, model), bf16)
     outs = [
         shape((rows, model), bf16),
         shape((rows, model), f32),
         shape((rows, model), bf16),
-        shape(wo.shape, bf16),
         shape((8, model), f32),
+        half,
+        half,
     ]
     return call(
-        branch_backward_kernel,
+        functools.partial(branch_backward_kernel, sizes, x_outer),
         outs,
         args,
         4 * rows * model * model,
         0,
-        [pltpu.VMEM((8, model), f32), pltpu.VMEM((rows, model), bf16)],
+        [pltpu.VMEM((8, model), f32), pltpu.VMEM((rows, model), bf16), pltpu.VMEM(wo.shape, bf16)],
         56,
         "branch_backward",
-        [*map(whole, args[:7]), pl.BlockSpec((model, HEAD), lambda i: (0, last)), whole(att)],
+        [SM, *map(whole, args[1:8]), pl.BlockSpec((model, HEAD), lambda i: (0, last)), whole(att)],
         grid=(1,),
         out_specs=[*map(whole, outs)],
     )
@@ -366,7 +433,9 @@
     )[0]
 
 
-def input_backward_kernel(x_ref, g_ref, w_ref, gh_ref, gg_ref, gx_ref, gw_ref, gains, normed, gn, sums):
+def input_backward_kernel(
+    sizes, x_outer, me_ref, x_ref, g_ref, w_ref, gh_ref, gg_ref, gx_ref, keep_ref, send_ref, gains, normed, gn, sums, gw_ref
+):
     rows, model = x_ref.shape
     wide = g_ref.shape[1]
     gains[...] = gain_rows(w_ref[:, wide : wide + HEAD])[:8]
@@ -400,15 +469,17 @@
         gx_ref[at, :] = (gh_ref[at, :] + r * (g - z * jnp.mean(g * z, axis=-1, keepdims=True))).astype(bf16)
 
     gw_ref[:, wide : wide + HEAD] = sums[...].T.astype(bf16)
-
-
-def input_backward(x, g, w, gh, gg):
+    hand_out(sizes, me_ref, gw_ref, keep_ref, send_ref, x_outer)
+
+
+def input_backward(sizes, x_outer, me, x, g, w, gh, gg):
     rows, model = x.shape
     wide = g.shape[1]
+    half = shape((w.shape[0] // 2, w.shape[1]), bf16)
     return call(
-        input_backward_kernel,
-        [shape(x.shape, bf16), shape(w.shape, bf16)],
-        (x, g, w, gh, gg),
+        functools.partial(input_backward_kernel, sizes, x_outer),
+        [shape(x.shape, bf16), half, half],
+        (me, x, g, w, gh, gg),
         4 * rows * model * wide,
         0,
         [
@@ -416,80 +487,130 @@
             pltpu.VMEM((rows, model), bf16),
             pltpu.VMEM((rows, model), f32),
             pltpu.VMEM((HEAD, model), f32),
+            pltpu.VMEM(w.shape, bf16),
         ],
         56,
         "input_backward",
-    )
+        [SM] + [VM] * 5,
+    )
+
+
+def spread(a, axis, n):
+    return [a] + [lax.ppermute(a, axis, [(i, (i + s) % n) for i in range(n)]) for s in range(1, n)]
+
+
+def add(parts):
+    total = parts[0].astype(f32)
+    for p in parts[1:]:
+        total = total + p.astype(f32)
+    return total
+
+
+def gather_chips(sizes, a, x_first):
+    nx, _, nb = sizes
+    if x_first:
+        by_x = [spread(p, "f2", nb) for p in spread(a, "x", nx)]
+        return [by_x[rx][rb] for rx in range(nx) for rb in range(nb)]
+    by_b = [spread(p, "x", nx) for p in spread(a, "f2", nb)]
+    return [by_b[rb][rx] for rx in range(nx) for rb in range(nb)]
+
+
+def send_on(parts, axis, n):
+    return [lax.ppermute(parts[s], axis, [(i, (i + s) % n) for i in range(n)]) for s in range(1, n)]
+
+
+def reduce_chips(sizes, parts, x_outer):
+    nx, na, nb = sizes
+    (first, n1), (second, n2) = (("x", nx), ("f2", nb)) if x_outer else (("f2", nb), ("x", nx))
+    got = [parts[0], *send_on(parts, first, n1)]
+    cut = lambda a, s, n: a[s * (a.shape[0] // n) : (s + 1) * (a.shape[0] // n)]
+    parts = [add([cut(p, s, n2) for p in got]).astype(bf16) for s in range(n2)]
+    got = [parts[0], *send_on(parts, second, n2)]
+    parts = [add([cut(p, s, na) for p in got]).astype(bf16) for s in range(na)]
+    return add([parts[0], *send_on(parts, "f1", na)])
 
 
 def on_device(
     sizes, tokens, doc_lengths, gain_one, query_weight, key_weight, value_weight, out_weight,
     gain_two, up_weight, down_weight, cotangent,
 ):
-    chips_x, fsdp = sizes
-    every = ("x", "core", "fsdp")
-    chips = ("x", "fsdp")
+    nx, na, nb = sizes
+    fsdp = na * nb
     core = lax.axis_index("core")
+    me = jnp.stack([lax.axis_index(a) for a in ("x", "f1", "f2", "core")]).astype(jnp.int32)
     swap = lambda a: lax.ppermute(a, "core", [(0, 1), (1, 0)])
     rows, model = tokens.shape
     shard = query_weight.shape[0]
     ff = up_weight.shape[1]
     chunks = down_weight.shape[0] // shard
     part = ff // (2 * chunks)
-    groups = chips_x * 2
 
     gain_block = jnp.zeros((shard, HEAD), bf16).at[:, 0].set(gain_one).at[:, 1].set(gain_two)
-    w_rows = jnp.concatenate([query_weight, key_weight, value_weight, gain_block], axis=1)
-    w = lax.all_gather(w_rows, every, axis=0, tiled=True)
-    wo = lax.all_gather(out_weight, every, axis=0, tiled=True)
+    w_rows = jnp.concatenate([query_weight, key_weight, value_weight, gain_block, out_weight], axis=1)
+    columns = w_rows.shape[1] - out_weight.shape[1]
+    along = spread(w_rows, "f1", na)
+    w_block = jnp.concatenate([a[:, :columns] for a in along], axis=0)
+    wo_block = jnp.concatenate([a[:, columns:] for a in along], axis=0)
+    w_pieces = gather_chips(sizes, w_block, True)
+    wo_pieces = gather_chips(sizes, wo_block, False)
+    w_pieces += [swap(p) for p in w_pieces]
+    wo_pieces += [swap(p) for p in wo_pieces]
 
     dy_p = swap(cotangent)
-    up = up_weight.reshape(shard, chips_x, 2, fsdp, chunks, shard).transpose(2, 0, 4, 1, 3, 5)
+    up = up_weight.reshape(shard, nx, 2, fsdp, chunks, shard).transpose(2, 0, 4, 1, 3, 5)
     up = up.reshape(2, shard, chunks, part)
     up_keep = jnp.where(core == 0, up[0], up[1])
     up_come = swap(jnp.where(core == 0, up[1], up[0]))
     up_pair = jnp.where(core == 0, jnp.stack([up_keep, up_come], 2), jnp.stack([up_come, up_keep], 2))
     up_pair = up_pair.reshape(shard, chunks, 2 * part)
     down = down_weight.reshape(chunks, shard, model)
-    per_call = 2
-    gathered = []
-    for first in range(0, chunks, per_call):
-        pieces = []
-        for c in range(first, first + per_call):
-            pieces += [up_pair[:, c], down[c]]
-        gathered.append(lax.all_gather(jnp.concatenate(pieces, axis=1), chips, axis=0, tiled=True))
-
-    qkv, att = attention_forward(doc_lengths, tokens, w)
-    hidden, nt_o = branch(tokens, att, wo, w)
+    f_rows = jnp.concatenate([p for c in range(chunks) for p in (up_pair[:, c], down[c])], axis=1)
+    along = spread(f_rows, "f1", na)
+    wide = 2 * model
+    pieces = []
+    for c in range(chunks):
+        block = jnp.concatenate([a[:, c * wide : (c + 1) * wide] for a in along], axis=0)
+        pieces.append(gather_chips(sizes, block, c % 2 == 0))
+
+    w, qkv, att = attention_forward(sizes, me, doc_lengths, tokens, w_pieces)
+    wo, hidden, nt_o = branch(sizes, me, tokens, att, w, wo_pieces)
     nt_p = swap(nt_o)
 
-    acts_o, acts_p, gis_o, gis_p, places, ffn_sums = [], [], [], [], [], []
-    for g in gathered:
-        act_o, act_p, gi_o, gi_p, grads = ffn(groups, nt_o, nt_p, cotangent, dy_p, g)
-        ffn_sums.append(lax.psum_scatter(grads, chips, scatter_dimension=0, tiled=True))
-        for c in range(per_call):
-            acts_o.append((act_o, c))
-            acts_p.append((act_p, c))
-            gis_o.append((gi_o, c))
-            gis_p.append((gi_p, c))
-            places.append((g, c))
-    out_p, gn_p = ffn_sum(groups, acts_p, gis_p, places)
+    acts_o, acts_p, gis_o, gis_p, ups, downs, sums = [], [], [], [], [], [], []
+    for c in range(chunks):
+        seen, up_c, down_c, grads = ffn(sizes, c % 2 == 0, me, nt_o, nt_p, cotangent, dy_p, pieces[c])
+        for kept, a in zip((acts_o, acts_p, gis_o, gis_p), seen):
+            kept.append(a)
+        ups.append(up_c)
+        downs.append(down_c)
+        sums.append(reduce_chips(sizes, grads, c % 2 == 0))
+    out_p, gn_p = ffn_sum(acts_p, gis_p, ups, downs)
     out_r, gn_r = swap(out_p), swap(gn_p)
-    out_o, gn_o = ffn_sum(groups, acts_o, gis_o, places)
-
-    output, gh, gatt, gwo, gg = branch_backward(hidden, gn_o, gn_r, out_o, out_r, cotangent, wo, w, att)
-    grad_out = lax.psum_scatter(gwo, every, scatter_dimension=0, tiled=True).astype(f32)
+    out_o, gn_o = ffn_sum(acts_o, gis_o, ups, downs)
+
+    output, gh, gatt, gg, keep, send = branch_backward(
+        sizes, False, me, hidden, gn_o, gn_r, out_o, out_r, cotangent, wo, w, att
+    )
+
+    def reduce_all(keep, send, x_outer):
+        come = swap(send)
+        n = nx if x_outer else nb
+        cut = keep.shape[0] // n
+        parts = [add([a[s * cut : (s + 1) * cut] for a in (keep, come)]).astype(bf16) for s in range(n)]
+        return reduce_chips(sizes, parts, x_outer)
+
+    grad_out = reduce_all(keep, send, False)
     gqkv = attention_backward(doc_lengths, qkv, gatt)
-    grad_tokens, gw = input_backward(tokens, gqkv, w, gh, gg)
-    gw = lax.psum_scatter(gw, every, scatter_dimension=0, tiled=True).astype(f32)
-
-    sums = jnp.concatenate([s.reshape(shard, per_call, 2 * model) for s in ffn_sums], axis=1)
-    grad_down = sums[:, :, model:].transpose(1, 0, 2).reshape(chunks * shard, model).astype(f32)
-    g_up = sums[:, :, :model].reshape(shard, chunks, 2, part)
+    grad_tokens, keep, send = input_backward(sizes, True, me, tokens, gqkv, w, gh, gg)
+    gw = reduce_all(keep, send, True)
+
+    sums = jnp.stack(sums, axis=1)
+    grad_down = sums[:, :, model:].transpose(1, 0, 2).reshape(chunks * shard, model)
+    g_up = sums[:, :, :model].reshape(shard, chunks, 2, part).astype(bf16)
     keep = jnp.where(core == 0, g_up[:, :, 0], g_up[:, :, 1])
     come = swap(jnp.where(core == 0, g_up[:, :, 1], g_up[:, :, 0]))
     grad_up = jnp.where(core == 0, jnp.stack([keep, come], 0), jnp.stack([come, keep], 0))
-    grad_up = grad_up.reshape(2, shard, chunks, chips_x, fsdp, shard).transpose(1, 3, 0, 4, 2, 5)
+    grad_up = grad_up.reshape(2, shard, chunks, nx, fsdp, shard).transpose(1, 3, 0, 4, 2, 5)
     grad_up = grad_up.reshape(shard, ff).astype(f32)
 
     qw = query_weight.shape[1]
@@ -509,11 +630,12 @@
 
 def solution(mesh):
     dp, fsdp = mesh.shape["dp"], mesh.shape["fsdp"]
-    split = Mesh(mesh.devices.reshape(dp // 2, 2, fsdp), ("x", "core", "fsdp"))
-    rows = P(("x", "core", "fsdp"), None)
-    line = P(("x", "core", "fsdp"))
+    sizes = (dp // 2, 4, fsdp // 4)
+    names = ("x", "core", "f1", "f2")
+    split = Mesh(mesh.devices.reshape(sizes[0], 2, *sizes[1:]), names)
+    rows, line = P(names, None), P(names)
     return jax.shard_map(
-        functools.partial(on_device, (dp // 2, fsdp)),
+        functools.partial(on_device, sizes),
         mesh=split,
         in_specs=(rows, rows, line, rows, rows, rows, rows, line, rows, rows, rows),
         out_specs=(rows, rows, line, rows, rows, rows, rows, line, rows, rows),

time: 865 us -> 477 us (0.55)
  waiting for transfers between devices: 602 us -> 104 us
  starting transfers between devices: 2.16 us -> 85.2 us
  local copies, waits for them, and re-layouts: 39.9 us -> 61.5 us
  between operations: 14.7 us -> 1.81 us
  other arithmetic: 11.5 us -> 23.4 us
    reduce_scatter x4 -> x0, waiting for transfers between devices: 406 us -> none  [the longest x2 189 us: on_device(): lax.psum_scatter(grads, chips, scatter_dimension=0, tiled=True)]
    all_gather x4 -> x0, waiting for transfers between devices: 190 us -> none  [the longest x2 110 us: on_device(): lax.all_gather(jnp.concatenate(pieces, axis=1), chips, axis=0, tiled=True)]
    ppermute x0 -> x54, waiting for transfers between devices: none -> 103 us  [the longest x24 58.3 us: spread(): lax.ppermute(a, axis, [(i, (i + s) % n) for i in range(n)])]
    ppermute x0 -> x54, starting transfers between devices: none -> 81.5 us  [the longest x30 44.7 us: send_on(): lax.ppermute(parts[s], axis, [(i, (i + s) % n) for i in range(n)])]
    unnamed x48 -> x134, local copies, waits for them, and re-layouts: 27.4 us -> 44.7 us
    convert_element_type x3 -> x14, other arithmetic: 3.27 us -> 16.1 us  [the longest x6 9.26 us: reduce_chips(): parts = [add([cut(p, s, n2) for p in got]).astype(bf16) for s in range(n2)]]
    pallas_call x9 -> x11, Pallas kernels: 187 us -> 193 us  [call(): pl.pallas_call(kernel, out_shape=outs, in_specs=in_specs or [VM] * len(ar...]
  transfers between devices with their start and end apart: 14 -> 70, of which waited for: 10 -> 26; matrix products, arithmetic and copies ran while one was open for 2% -> 9% of each run, Pallas kernels for 15% -> 41%
where the time goes in v2:
time: 477 us; the launch traced here: 469 us
  Pallas kernels  193 us (40%)
  waiting for transfers between devices  104 us (22%)
  starting transfers between devices  85.2 us (18%)
  local copies, waits for them, and re-layouts  61.5 us (13%)
  other arithmetic  23.4 us (5%)
    pallas_call x11, Pallas kernels, call(): pl.pallas_call(kernel, out_shape=outs, in_specs=in_specs or [VM] * len(ar...  193 us
    ppermute x24, waiting for transfers between devices, spread(): lax.ppermute(a, axis, [(i, (i + s) % n) for i in range(n)])  58.3 us
    unnamed x134, local copies, waits for them, and re-layouts  44.7 us
    ppermute x30, starting transfers between devices, send_on(): lax.ppermute(parts[s], axis, [(i, (i + s) % n) for i in range(n)])  44.7 us
    ppermute x30, waiting for transfers between devices, send_on(): lax.ppermute(parts[s], axis, [(i, (i + s) % n) for i in range(n)])  44.3 us
    ppermute x24, starting transfers between devices, spread(): lax.ppermute(a, axis, [(i, (i + s) % n) for i in range(n)])  36.8 us
  transfers between devices with their start and end apart: 70, of which 26 were waited for; matrix products, arithmetic and copies ran while one was open for 9% of the time, Pallas kernels for 41%

profile of v2, /device:TPU:0, one launch (start us, length us, event | category | flops | bytes accessed | tf_op | source)
XLA Modules:
  0.0 468.7 jit_solution(15911421667036217457)
XLA Ops:
  21.2 4.7 collective-permute-done.1
  42.9 14.2 %collective-permute-done.10.refs_1_ = bf16[128,1024]{1,0:T(8,128)(2,1)S(1)} collective-permute-done((bf16[128,1024]{1,0:T(8,128)(2,1)S(1)}, bf16[128,1024]{1,0:T(8,128)(2,1)S(1)}, u32[]{:S(2)}, u32[]{:S(2)}) %collective-permute-start.10) | collective-permute-done | bytes 262176 | tf_op jit(solution)/shard_map/ppermute | solution.py:499
  61.6 4.3 collective-permute-done.12.refs_3_
  66.9 26.9 %attention_forward.1 = (bf16[1024,1408]{1,0:T(8,128)(2,1)S(1)}, bf16[1024,1280]{1,0:T(8,128)(2,1)S(1)}, bf16[1024,1024]{1,0:T(8,128)(2,1)S(1)}) custom-call(s32[4]{0:T(128)S(1)} %pad_add_fusion.me_ref, s32[1,8]{1,0:T(1,128)S(1)} %copy-done.7, bf16[1024,1024]{1,0:T(8,128)(2,1)S(1)} %copy-done.3, bf16[128,1408]{1,0:T(8,128)(2,1)S(1)} %pad_maximum_fusion.5.refs_0_, ...), custom_call_target="tpu_custom_call" | custom-call | flops 6979321856 | bytes 12582960 | tf_op jit(solution)/shard_map/attention_forward/pallas_call | solution.py:42
  97.3 6.7 %branch.1 = (bf16[1024,1024]{1,0:T(8,128)(2,1)S(1)}, f32[1024,1024]{1,0:T(8,128)}, bf16[1024,1024]{1,0:T(8,128)(2,1)S(1)}) custom-call(s32[4]{0:T(128)S(1)} %pad_add_fusion.me_ref, bf16[1024,1024]{1,0:T(8,128)(2,1)S(1)} %copy-done.3, bf16[1024,1024]{1,0:T(8,128)(2,1)S(1)} %get-tuple-element.85.att_ref, bf16[1024,1408]{1,0:T(8,128)(2,1)S(1)} %get-tuple-element.86.w_ref, ...), custom_call_target="tpu_custom_call" | custom-call | flops 2147483648 | bytes 17563664 | tf_op jit(solution)/shard_map/branch/pallas_call | solution.py:42
  104.3 5.8 %collective-permute-done.22 = bf16[32,8192]{1,0:T(8,128)(2,1)S(1)} collective-permute-done((bf16[32,8192]{1,0:T(8,128)(2,1)}, bf16[32,8192]{1,0:T(8,128)(2,1)S(1)}, u32[]{:S(2)}, u32[]{:S(2)}) %collective-permute-start.22) | collective-permute-done | bytes 524320 | tf_op jit(solution)/shard_map/ppermute | solution.py:499
  112.9 10.8 %collective-permute-done.24.refs_2_ = bf16[128,2048]{1,0:T(8,128)(2,1)S(1)} collective-permute-done((bf16[128,2048]{1,0:T(8,128)(2,1)S(1)}, bf16[128,2048]{1,0:T(8,128)(2,1)S(1)}, u32[]{:S(2)}, u32[]{:S(2)}) %collective-permute-start.24) | collective-permute-done | bytes 524320 | tf_op jit(solution)/shard_map/ppermute | solution.py:499
  127.1 9.7 %collective-permute-done.26.refs_1_ = bf16[128,2048]{1,0:T(8,128)(2,1)S(1)} collective-permute-done((bf16[128,2048]{1,0:T(8,128)(2,1)S(1)}, bf16[128,2048]{1,0:T(8,128)(2,1)S(1)}, u32[]{:S(2)}, u32[]{:S(2)}) %collective-permute-start.26) | collective-permute-done | bytes 524320 | tf_op jit(solution)/shard_map/ppermute | solution.py:499
  138.4 8.1 %collective-permute-done.25.refs_3_ = bf16[128,2048]{1,0:T(8,128)(2,1)S(1)} collective-permute-done((bf16[128,2048]{1,0:T(8,128)(2,1)S(1)}, bf16[128,2048]{1,0:T(8,128)(2,1)S(1)}, u32[]{:S(2)}, u32[]{:S(2)}) %collective-permute-start.25) | collective-permute-done | bytes 524320 | tf_op jit(solution)/shard_map/ppermute | solution.py:499
  150.0 15.5 %ffn.4 = (bf16[1024,512]{1,0:T(8,128)(2,1)S(1)}, bf16[1024,512]{1,0:T(8,128)(2,1)S(1)}, bf16[1024,512]{1,0:T(8,128)(2,1)S(1)}, bf16[1024,512]{1,0:T(8,128)(2,1)S...) custom-call(s32[4]{0:T(128)S(1)} %pad_add_fusion.me_ref, ...), custom_call_target="tpu_custom_call" | custom-call | flops 8589934592 | bytes 18874384 | tf_op jit(solution)/shard_map/ffn/pallas_call | solution.py:42
  172.9 15.9 %ffn.5 = (bf16[1024,512]{1,0:T(8,128)(2,1)S(1)}, bf16[1024,512]{1,0:T(8,128)(2,1)S(1)}, bf16[1024,512]{1,0:T(8,128)(2,1)S(1)}, bf16[1024,512]{1,0:T(8,128)(2,1)S...) custom-call(s32[4]{0:T(128)S(1)} %pad_add_fusion.me_ref, ...), custom_call_target="tpu_custom_call" | custom-call | flops 8589934592 | bytes 18874384 | tf_op jit(solution)/shard_map/ffn/pallas_call | solution.py:42
  196.7 15.5 %ffn.6 = (bf16[1024,512]{1,0:T(8,128)(2,1)S(1)}, bf16[1024,512]{1,0:T(8,128)(2,1)S(1)}, bf16[1024,512]{1,0:T(8,128)(2,1)S(1)}, bf16[1024,512]{1,0:T(8,128)(2,1)S...) custom-call(s32[4]{0:T(128)S(1)} %pad_add_fusion.me_ref, ...), custom_call_target="tpu_custom_call" | custom-call | flops 8589934592 | bytes 18874384 | tf_op jit(solution)/shard_map/ffn/pallas_call | solution.py:42
  220.2 15.8 %ffn.7 = (bf16[1024,512]{1,0:T(8,128)(2,1)S(1)}, bf16[1024,512]{1,0:T(8,128)(2,1)S(1)}, bf16[1024,512]{1,0:T(8,128)(2,1)S(1)}, bf16[1024,512]{1,0:T(8,128)(2,1)S...) custom-call(s32[4]{0:T(128)S(1)} %pad_add_fusion.me_ref, ...), custom_call_target="tpu_custom_call" | custom-call | flops 8589934592 | bytes 18874384 | tf_op jit(solution)/shard_map/ffn/pallas_call | solution.py:42
  249.3 12.1 %ffn_sum.3 = (bf16[1024,1024]{1,0:T(8,128)(2,1)}, bf16[1024,1024]{1,0:T(8,128)(2,1)}) custom-call(bf16[1024,512]{1,0:T(8,128)(2,1)S(1)} %get-tuple-element.106.refs_0_, bf16[1024,512]{1,0:T(8,128)(2,1)S(1)} %copy-done.21, bf16[1024,512]{1,0:T(8,128)(2,1)S(1)} %copy-done.31, bf16[1024,512]{1,0:T(8,128)(2,1)S(1)} %copy-done.41, ...), custom_call_target="tpu_custom_call" | custom-call | flops 8589934592 | bytes 20971520 | tf_op jit(solution)/shard_map/ffn_sum/pallas_call | solution.py:42
  265.1 12.0 %ffn_sum.2 = (bf16[1024,1024]{1,0:T(8,128)(2,1)}, bf16[1024,1024]{1,0:T(8,128)(2,1)}) custom-call(bf16[1024,512]{1,0:T(8,128)(2,1)S(1)} %get-tuple-element.89.refs_0_, bf16[1024,512]{1,0:T(8,128)(2,1)S(1)} %copy-done.15, bf16[1024,512]{1,0:T(8,128)(2,1)S(1)} %copy-done.25, bf16[1024,512]{1,0:T(8,128)(2,1)S(1)} %copy-done.35, ...), custom_call_target="tpu_custom_call" | custom-call | flops 8589934592 | bytes 20971520 | tf_op jit(solution)/shard_map/ffn_sum/pallas_call | solution.py:42
  286.4 7.7 %collective-permute-done.50 = bf16[128,2048]{1,0:T(8,128)(2,1)S(1)} collective-permute-done((bf16[128,2048]{1,0:T(8,128)(2,1)S(1)}, bf16[128,2048]{1,0:T(8,128)(2,1)S(1)}, u32[]{:S(2)}, u32[]{:S(2)}) %collective-permute-start.50) | collective-permute-done | bytes 524320 | tf_op jit(solution)/shard_map/ppermute | solution.py:519
  299.0 5.7 %collective-permute-done.60 = bf16[128,2048]{1,0:T(8,128)(2,1)S(1)} collective-permute-done((bf16[128,2048]{1,0:T(8,128)(2,1)S(1)}, bf16[128,2048]{1,0:T(8,128)(2,1)S(1)}, u32[]{:S(2)}, u32[]{:S(2)}) %collective-permute-start.60) | collective-permute-done | bytes 524320 | tf_op jit(solution)/shard_map/ppermute | solution.py:519
  315.3 4.7 collective-permute-start.58
  320.1 4.5 collective-permute-start.61
  333.4 20.1 %branch_backward.1 = (bf16[1024,1024]{1,0:T(8,128)(2,1)}, f32[1024,1024]{1,0:T(8,128)}, bf16[1024,1024]{1,0:T(8,128)(2,1)}, f32[8,1024]{1,0:T(8,128)}, bf16[512,...) custom-call(s32[4]{0:T(128)} %copy-done.4, f32[1024,1024]{1,0:T(8,128)} %get-tuple-element.87.hidden_ref, ...), custom_call_target="tpu_custom_call" | custom-call | flops 4294967296 | bytes 32276496 | tf_op jit(solution)/shard_map/branch_backward/pallas_call | solution.py:42
  355.1 33.0 %attention_backward.1.g_ref = bf16[1024,1280]{1,0:T(8,128)(2,1)S(1)} custom-call(s32[1,8]{1,0:T(1,128)S(1)} %copy-done.7, bf16[1024,1280]{1,0:T(8,128)(2,1)S(1)} %copy-done.10, bf16[1024,1024]{1,0:T(8,128)(2,1)S(1)} %copy-done.6), custom_call_target="tpu_custom_call" | custom-call | flops 10737418240 | bytes 7340064 | tf_op jit(solution)/shard_map/attention_backward/pallas_call | solution.py:42
  389.7 19.6 %input_backward.1 = (bf16[1024,1024]{1,0:T(8,128)(2,1)}, bf16[512,1408]{1,0:T(8,128)(2,1)}, bf16[512,1408]{1,0:T(8,128)(2,1)}) custom-call(s32[4]{0:T(128)} %copy-done.4, bf16[1024,1024]{1,0:T(8,128)(2,1)} %x_ref.5, bf16[1024,1280]{1,0:T(8,128)(2,1)} %copy-done.8, bf16[1024,1408]{1,0:T(8,128)(2,1)} %copy-done, f32[1024,1024]{1,0:T(8,128)} %get-tuple-element.121.gh_ref, ...), custom_call_target="tpu_custom_call" | custom-call | flops 5368709120 | bytes 16810000 | tf_op jit(solution)/shard_map/input_backward/pallas_call | solution.py:42
  428.9 5.9 %collective-permute-done.44 = bf16[256,1024]{1,0:T(8,128)(2,1)S(1)} collective-permute-done((bf16[256,1024]{1,0:T(8,128)(2,1)}, bf16[256,1024]{1,0:T(8,128)(2,1)S(1)}, u32[]{:S(2)}, u32[]{:S(2)}) %collective-permute-start.44) | collective-permute-done | bytes 524320 | tf_op jit(solution)/shard_map/ppermute | solution.py:519
  437.1 7.5 %collective-permute-done.38 = bf16[256,1408]{1,0:T(8,128)(2,1)} collective-permute-done((bf16[256,1408]{1,0:T(8,128)(2,1)}, bf16[256,1408]{1,0:T(8,128)(2,1)}, u32[]{:S(2)}, u32[]{:S(2)}) %collective-permute-start.38) | collective-permute-done | bytes 720928 | tf_op jit(solution)/shard_map/ppermute | solution.py:519
  (330 shorter events, 180.1 us)
Async XLA Ops:
  59.6 44.6 %collective-permute-start.21 = (bf16[32,8192]{1,0:T(8,128)(2,1)}, bf16[32,8192]{1,0:T(8,128)(2,1)S(1)}, u32[]{:S(2)}, u32[]{:S(2)}) collective-permute-start(bf16[32,8192]{1,0:T(8,128)(2,1)} %constant_dynamic-update-slice_fusion.5), channel_id=1, source_target_pairs={{0,4},{2,6},{4,0},{6,2},{1,5},{3,7},{5,1},{7,3},{8,12},{10,14},{12... | collective-permute-start | bytes 1572872 | tf_op jit(solution)/shard_map/ppermute | solution.py:499
  65.8 29.5 %collective-permute-start.13 = (bf16[128,1024]{1,0:T(8,128)(2,1)S(1)}, bf16[128,1024]{1,0:T(8,128)(2,1)S(1)}, u32[]{:S(2)}, u32[]{:S(2)}) collective-permute-start(bf16[128,1024]{1,0:T(8,128)(2,1)S(1)} %pad_maximum_fusion.6.refs_0_), channel_id=1, source_target_pairs={{0,8},{8,0},{1,9},{9,1},{2,10},{10,2},{3,11},{11,3},{4,12},{12,4},... | collective-permute-start | bytes 786440 | tf_op jit(solution)/shard_map/ppermute | solution.py:541
  65.9 29.5 %collective-permute-start.14 = (bf16[128,1024]{1,0:T(8,128)(2,1)S(1)}, bf16[128,1024]{1,0:T(8,128)(2,1)S(1)}, u32[]{:S(2)}, u32[]{:S(2)}) collective-permute-start(bf16[128,1024]{1,0:T(8,128)(2,1)S(1)} %collective-permute-done.10.refs_1_), channel_id=1, source_target_pairs={{0,8},{8,0},{1,9},{9,1},{2,10},{10,2},{3,11},{11,3},{4,12},{12,4},... | collective-permute-start | bytes 786440 | tf_op jit(solution)/shard_map/ppermute | solution.py:541
  66.4 30.9 %collective-permute-start.15 = (bf16[128,1024]{1,0:T(8,128)(2,1)S(1)}, bf16[128,1024]{1,0:T(8,128)(2,1)S(1)}, u32[]{:S(2)}, u32[]{:S(2)}) collective-permute-start(bf16[128,1024]{1,0:T(8,128)(2,1)S(1)} %collective-permute-done.11.refs_2_), channel_id=1, source_target_pairs={{0,8},{8,0},{1,9},{9,1},{2,10},{10,2},{3,11},{11,3},{4,12},{12,4},... | collective-permute-start | bytes 786440 | tf_op jit(solution)/shard_map/ppermute | solution.py:541
  66.4 30.9 %collective-permute-start.16 = (bf16[128,1024]{1,0:T(8,128)(2,1)S(1)}, bf16[128,1024]{1,0:T(8,128)(2,1)S(1)}, u32[]{:S(2)}, u32[]{:S(2)}) collective-permute-start(bf16[128,1024]{1,0:T(8,128)(2,1)S(1)} %collective-permute-done.12.refs_3_), channel_id=1, source_target_pairs={{0,8},{8,0},{1,9},{9,1},{2,10},{10,2},{3,11},{11,3},{4,12},{12,4},... | collective-permute-start | bytes 786440 | tf_op jit(solution)/shard_map/ppermute | solution.py:541
  95.3 52.6 %collective-permute-start.18 = (bf16[1024,1024]{1,0:T(8,128)(2,1)}, bf16[1024,1024]{1,0:T(8,128)(2,1)S(1)}, u32[]{:S(2)}, u32[]{:S(2)}) collective-permute-start(bf16[1024,1024]{1,0:T(8,128)(2,1)} %dy_ref.1), channel_id=1, source_target_pairs={{0,8},{8,0},{1,9},{9,1},{2,10},{10,2},{3,11},{11,3},{4,12},{12,4},... | collective-permute-start | bytes 6291464 | tf_op jit(solution)/shard_map/ppermute | solution.py:541
  104.0 44.5 %collective-permute-start.17 = (bf16[1024,1024]{1,0:T(8,128)(2,1)S(1)}, bf16[1024,1024]{1,0:T(8,128)(2,1)S(1)}, u32[]{:S(2)}, u32[]{:S(2)}) collective-permute-start(bf16[1024,1024]{1,0:T(8,128)(2,1)S(1)} %get-tuple-element.88.nt_o), channel_id=1, source_target_pairs={{0,8},{8,0},{1,9},{9,1},{2,10},{10,2},{3,11},{11,3},{4,12},{12,4},... | collective-permute-start | bytes 6291464 | tf_op jit(solution)/shard_map/ppermute | solution.py:541
  125.6 41.9 %collective-permute-start.27 = (bf16[128,2048]{1,0:T(8,128)(2,1)S(1)}, bf16[128,2048]{1,0:T(8,128)(2,1)S(1)}, u32[]{:S(2)}, u32[]{:S(2)}) collective-permute-start(bf16[128,2048]{1,0:T(8,128)(2,1)S(1)} %pad_maximum_fusion.2.refs_0_), channel_id=1, source_target_pairs={{0,16},{16,0},{1,17},{17,1},{2,18},{18,2},{3,19},{19,3},{4,20},{20... | collective-permute-start | bytes 1572872 | tf_op jit(solution)/shard_map/ppermute | solution.py:499
  136.9 32.1 %collective-permute-start.30 = (bf16[128,2048]{1,0:T(8,128)(2,1)S(1)}, bf16[128,2048]{1,0:T(8,128)(2,1)S(1)}, u32[]{:S(2)}, u32[]{:S(2)}) collective-permute-start(bf16[128,2048]{1,0:T(8,128)(2,1)S(1)} %pad_maximum_fusion.3.refs_0_), channel_id=1, source_target_pairs={{0,16},{16,0},{1,17},{17,1},{2,18},{18,2},{3,19},{19,3},{4,20},{20... | collective-permute-start | bytes 1572872 | tf_op jit(solution)/shard_map/ppermute | solution.py:499
  146.4 48.3 %collective-permute-start.29 = (bf16[128,2048]{1,0:T(8,128)(2,1)S(1)}, bf16[128,2048]{1,0:T(8,128)(2,1)S(1)}, u32[]{:S(2)}, u32[]{:S(2)}) collective-permute-start(bf16[128,2048]{1,0:T(8,128)(2,1)S(1)} %pad_maximum_fusion.3.refs_0_), channel_id=1, source_target_pairs={{0,1},{1,0},{2,3},{3,2},{4,5},{5,4},{6,7},{7,6},{8,9},{9,8},{10,11... | collective-permute-start | bytes 1572872 | tf_op jit(solution)/shard_map/ppermute | solution.py:499
  167.5 52.7 %collective-permute-start.33 = (bf16[128,2048]{1,0:T(8,128)(2,1)S(1)}, bf16[128,2048]{1,0:T(8,128)(2,1)S(1)}, u32[]{:S(2)}, u32[]{:S(2)}) collective-permute-start(bf16[128,2048]{1,0:T(8,128)(2,1)S(1)} %pad_maximum_fusion.4.refs_0_), channel_id=1, source_target_pairs={{0,16},{16,0},{1,17},{17,1},{2,18},{18,2},{3,19},{19,3},{4,20},{20... | collective-permute-start | bytes 1572872 | tf_op jit(solution)/shard_map/ppermute | solution.py:499
  169.0 27.8 %collective-permute-start.31 = (bf16[128,2048]{1,0:T(8,128)(2,1)S(1)}, bf16[128,2048]{1,0:T(8,128)(2,1)S(1)}, u32[]{:S(2)}, u32[]{:S(2)}) collective-permute-start(bf16[128,2048]{1,0:T(8,128)(2,1)S(1)} %collective-permute-done.30.refs_2_), channel_id=1, source_target_pairs={{0,1},{1,0},{2,3},{3,2},{4,5},{5,4},{6,7},{7,6},{8,9},{9,8},{10,11... | collective-permute-start | bytes 1572872 | tf_op jit(solution)/shard_map/ppermute | solution.py:499
  170.4 49.8 %collective-permute-start.34 = (bf16[128,2048]{1,0:T(8,128)(2,1)S(1)}, bf16[128,2048]{1,0:T(8,128)(2,1)S(1)}, u32[]{:S(2)}, u32[]{:S(2)}) collective-permute-start(bf16[128,2048]{1,0:T(8,128)(2,1)S(1)} %collective-permute-done.32.refs_1_), channel_id=1, source_target_pairs={{0,16},{16,0},{1,17},{17,1},{2,18},{18,2},{3,19},{19,3},{4,20},{20... | collective-permute-start | bytes 1572872 | tf_op jit(solution)/shard_map/ppermute | solution.py:499
  172.9 104.3 %collective-permute-start.49 = (bf16[256,2048]{1,0:T(8,128)(2,1)}, bf16[256,2048]{1,0:T(8,128)(2,1)}, u32[]{:S(2)}, u32[]{:S(2)}) collective-permute-start(bf16[256,2048]{1,0:T(8,128)(2,1)} %get-tuple-element.129), channel_id=1, source_target_pairs={{0,16},{16,0},{1,17},{17,1},{2,18},{18,2},{3,19},{19,3},{4,20},{20... | collective-permute-start | bytes 3145736 | tf_op jit(solution)/shard_map/ppermute | solution.py:519
  194.7 84.5 %collective-permute-start.54 = (bf16[256,2048]{1,0:T(8,128)(2,1)}, bf16[256,2048]{1,0:T(8,128)(2,1)}, u32[]{:S(2)}, u32[]{:S(2)}) collective-permute-start(bf16[256,2048]{1,0:T(8,128)(2,1)} %get-tuple-element.131), channel_id=1, source_target_pairs={{0,1},{1,0},{2,3},{3,2},{4,5},{5,4},{6,7},{7,6},{8,9},{9,8},{10,11... | collective-permute-start | bytes 3145736 | tf_op jit(solution)/shard_map/ppermute | solution.py:519
  218.2 64.7 %collective-permute-start.59 = (bf16[256,2048]{1,0:T(8,128)(2,1)}, bf16[256,2048]{1,0:T(8,128)(2,1)}, u32[]{:S(2)}, u32[]{:S(2)}) collective-permute-start(bf16[256,2048]{1,0:T(8,128)(2,1)} %get-tuple-element.133), channel_id=1, source_target_pairs={{0,16},{16,0},{1,17},{17,1},{2,18},{18,2},{3,19},{19,3},{4,20},{20... | collective-permute-start | bytes 3145736 | tf_op jit(solution)/shard_map/ppermute | solution.py:519
  241.9 42.8 %collective-permute-start.64 = (bf16[256,2048]{1,0:T(8,128)(2,1)}, bf16[256,2048]{1,0:T(8,128)(2,1)}, u32[]{:S(2)}, u32[]{:S(2)}) collective-permute-start(bf16[256,2048]{1,0:T(8,128)(2,1)} %get-tuple-element.135), channel_id=1, source_target_pairs={{0,1},{1,0},{2,3},{3,2},{4,5},{5,4},{6,7},{7,6},{8,9},{9,8},{10,11... | collective-permute-start | bytes 3145736 | tf_op jit(solution)/shard_map/ppermute | solution.py:519
  261.4 69.0 %collective-permute-start.35 = (bf16[1024,1024]{1,0:T(8,128)(2,1)}, bf16[1024,1024]{1,0:T(8,128)(2,1)S(1)}, u32[]{:S(2)}, u32[]{:S(2)}) collective-permute-start(bf16[1024,1024]{1,0:T(8,128)(2,1)} %get-tuple-element.114), channel_id=1, source_target_pairs={{0,8},{8,0},{1,9},{9,1},{2,10},{10,2},{3,11},{11,3},{4,12},{12,4},... | collective-permute-start | bytes 6291464 | tf_op jit(solution)/shard_map/ppermute | solution.py:541
  277.1 54.7 %collective-permute-start.36 = (bf16[1024,1024]{1,0:T(8,128)(2,1)S(1)}, bf16[1024,1024]{1,0:T(8,128)(2,1)S(1)}, u32[]{:S(2)}, u32[]{:S(2)}) collective-permute-start(bf16[1024,1024]{1,0:T(8,128)(2,1)S(1)} %copy-done.58), channel_id=1, source_target_pairs={{0,8},{8,0},{1,9},{9,1},{2,10},{10,2},{3,11},{11,3},{4,12},{12,4},... | collective-permute-start | bytes 6291464 | tf_op jit(solution)/shard_map/ppermute | solution.py:541
  320.1 89.3 %collective-permute-start.61 = (bf16[32,2048]{1,0:T(8,128)(2,1)}, bf16[32,2048]{1,0:T(8,128)(2,1)}, u32[]{:S(2)}, u32[]{:S(2)}) collective-permute-start(bf16[32,2048]{1,0:T(8,128)(2,1)} %get-tuple-element.158), channel_id=1, source_target_pairs={{0,2},{2,4},{4,6},{6,0},{1,3},{3,5},{5,7},{7,1},{8,10},{10,12},{12... | collective-permute-start | bytes 393224 | tf_op jit(solution)/shard_map/ppermute | solution.py:519
  328.3 84.1 %collective-permute-start.62 = (bf16[32,2048]{1,0:T(8,128)(2,1)}, bf16[32,2048]{1,0:T(8,128)(2,1)}, u32[]{:S(2)}, u32[]{:S(2)}) collective-permute-start(bf16[32,2048]{1,0:T(8,128)(2,1)} %get-tuple-element.160), channel_id=1, source_target_pairs={{0,4},{2,6},{4,0},{6,2},{1,5},{3,7},{5,1},{7,3},{8,12},{10,14},{12... | collective-permute-start | bytes 393224 | tf_op jit(solution)/shard_map/ppermute | solution.py:519
  328.4 84.0 %collective-permute-start.63 = (bf16[32,2048]{1,0:T(8,128)(2,1)}, bf16[32,2048]{1,0:T(8,128)(2,1)}, u32[]{:S(2)}, u32[]{:S(2)}) collective-permute-start(bf16[32,2048]{1,0:T(8,128)(2,1)} %get-tuple-element.159), channel_id=1, source_target_pairs={{0,6},{2,0},{4,2},{6,4},{1,7},{3,1},{5,3},{7,5},{8,14},{10,8},{12,... | collective-permute-start | bytes 393224 | tf_op jit(solution)/shard_map/ppermute | solution.py:519
  330.4 83.7 %collective-permute-start.66 = (bf16[32,2048]{1,0:T(8,128)(2,1)S(1)}, bf16[32,2048]{1,0:T(8,128)(2,1)S(1)}, u32[]{:S(2)}, u32[]{:S(2)}) collective-permute-start(bf16[32,2048]{1,0:T(8,128)(2,1)S(1)} %get-tuple-element.161), channel_id=1, source_target_pairs={{0,2},{2,4},{4,6},{6,0},{1,3},{3,5},{5,7},{7,1},{8,10},{10,12},{12... | collective-permute-start | bytes 393224 | tf_op jit(solution)/shard_map/ppermute | solution.py:519
  331.8 82.3 %collective-permute-start.67 = (bf16[32,2048]{1,0:T(8,128)(2,1)S(1)}, bf16[32,2048]{1,0:T(8,128)(2,1)S(1)}, u32[]{:S(2)}, u32[]{:S(2)}) collective-permute-start(bf16[32,2048]{1,0:T(8,128)(2,1)S(1)} %get-tuple-element.163), channel_id=1, source_target_pairs={{0,4},{2,6},{4,0},{6,2},{1,5},{3,7},{5,1},{7,3},{8,12},{10,14},{12... | collective-permute-start | bytes 393224 | tf_op jit(solution)/shard_map/ppermute | solution.py:519
  (108 other events, 1096.7 us)

commit v3 on v1

v3 whole, which is shorter than its diff:
```python
import functools
import math

import jax
import jax.numpy as jnp
from jax import lax
from jax.experimental import pallas as pl
from jax.experimental.pallas import tpu as pltpu
from jax.sharding import Mesh, PartitionSpec as P

EPS = 1e-06
HEAD = 128
MIB = 2**20
f32 = jnp.float32
bf16 = jnp.bfloat16
VM = pl.BlockSpec(memory_space=pltpu.VMEM)
SM = pl.BlockSpec(memory_space=pltpu.SMEM)
GELU_A = math.sqrt(2.0 / math.pi)
GELU_B = GELU_A * 0.044715
SCORE_SCALE = 1.0 / math.sqrt(HEAD)
LOG2E = math.log2(math.e)
MARKS = 64
GROUP = 2
VMEM_MIB = 60
HINT = 8


def nn(a, b):
    return lax.dot_general(a, b, (((1,), (0,)), ((), ())), preferred_element_type=f32)


def nt(a, b):
    return lax.dot_general(a, b, (((1,), (1,)), ((), ())), preferred_element_type=f32)


def tn(a, b):
    return lax.dot_general(a, b, (((0,), (0,)), ((), ())), preferred_element_type=f32)


def shape(dims, dtype):
    return jax.ShapeDtypeStruct(dims, dtype)


def call(kernel, outs, args, flops, exps=0, scratch=(), vmem=48, name=None, in_specs=None, **kw):
    moved = sum(math.prod(a.shape) * a.dtype.itemsize for a in (*args, *outs))
    return pl.pallas_call(
        kernel,
        out_shape=outs,
        in_specs=in_specs or [VM] * len(args),
        out_specs=kw.pop("out_specs", [VM] * len(outs)),
        scratch_shapes=list(scratch),
        compiler_params=pltpu.CompilerParams(vmem_limit_bytes=vmem * MIB),
        cost_estimate=pl.CostEstimate(flops=flops // HINT, bytes_accessed=moved // HINT, transcendentals=exps // HINT),
        name=name,
        **kw,
    )(*args)


def chip_at(sizes, order, me_ref, rx, rb, ra, sign):
    nx, na, nb = sizes
    x = lax.rem(me_ref[0] + (sign * rx) % nx, nx)
    a = lax.rem(me_ref[1] + (sign * ra) % na, na) if order[1] else ra
    b = lax.rem(me_ref[2] + (sign * rb) % nb, nb)
    return x, a * nb + b


def blocks_of(sizes, order):
    nx, na, nb = sizes
    for rx in range(nx):
        for rb in range(nb):
            for ra in range(na):
                yield (rx, rb, ra), (rx, rb) if order[0] else (rb, rx)


def seconds(sizes, order):
    return sizes[2] if order[0] else sizes[0]


def firsts(sizes, order):
    return sizes[0] if order[0] else sizes[2]


def row_of(sizes, x, f, core, shard):
    return pl.ds(pl.multiple_of(((x * 2 + core) * (sizes[1] * sizes[2]) + f) * shard, shard), shard)


def half_row_of(sizes, x, f, shard):
    return pl.ds(pl.multiple_of((x * (sizes[1] * sizes[2]) + f) * shard, shard), shard)


def assemble(sizes, me_ref, orders, refs, whole_ref):
    refs, column = list(refs), 0
    for order in orders:
        count = seconds(sizes, order)
        mine, refs = refs[: 2 * count], refs[2 * count :]
        width = mine[0].shape[1]
        shard = mine[0].shape[0] // (firsts(sizes, order) * sizes[1])
        for other in range(2):
            core = me_ref[3] if other == 0 else 1 - me_ref[3]
            for place, (first, second) in blocks_of(sizes, order):
                x, f = chip_at(sizes, order, me_ref, *place, -1)
                at = (first * sizes[1] + place[2]) * shard
                whole_ref[row_of(sizes, x, f, core, shard), column : column + width] = mine[other * count + second][at : at + shard, :]
        column += width


def hand_out(sizes, me_ref, orders, whole_ref, refs):
    nx, na, nb = sizes
    column = 0
    for n, order in enumerate(orders):
        for other, ref in enumerate(refs[2 * n : 2 * n + 2]):
            core = me_ref[3] if other == 0 else 1 - me_ref[3]
            shard = ref.shape[0] // (nx * na * nb)
            for place, (first, second) in blocks_of(sizes, order):
                x, f = chip_at(sizes, order, me_ref, *place, 1)
                at = ((first * seconds(sizes, order) + second) * na + place[2]) * shard
                ref[at : at + shard, :] = whole_ref[row_of(sizes, x, f, core, shard), column : column + ref.shape[1]]
        column += refs[2 * n].shape[1]


def gain_rows(block):
    return block.astype(f32).T


def norm_tile(x, gain):
    r = lax.rsqrt(jnp.mean(x * x, axis=-1, keepdims=True) + EPS)
    return x * r * gain


def position_ids(len_ref, pos):
    seg = jnp.zeros(pos.shape, jnp.int32)
    end = jnp.int32(0)
    slots = len_ref.shape[1]
    for slot in range(slots):
        end = end + len_ref[0, slot]
        seg = seg + (pos >= end).astype(jnp.int32)
    return jnp.where(pos >= end, slots + pos // 128, seg), pos >= end


def query_marks(len_ref, first):
    pos = first + lax.broadcasted_iota(jnp.int32, (128, 1), 0)
    ids, _ = position_ids(len_ref, pos)
    lane = lax.broadcasted_iota(jnp.int32, (128, 128), 1)
    return jnp.where(lane == ids, 1.0, 0.0)


def key_marks(len_ref, first):
    pos = first + lax.broadcasted_iota(jnp.int32, (128, 1), 0)
    ids, _ = position_ids(len_ref, pos)
    lane = lax.broadcasted_iota(jnp.int32, (128, 128), 1)
    return jnp.where(lane >= MARKS, 1.0, jnp.where(lane == ids, 0.0, -1e30)).astype(bf16)


def block_bias(len_ref, first):
    q_pos = first + lax.broadcasted_iota(jnp.int32, (128, 1), 0)
    k_pos = first + lax.broadcasted_iota(jnp.int32, (1, 128), 1)
    _, k_pad = position_ids(len_ref, k_pos)
    allowed = ((k_pos <= q_pos) & jnp.logical_not(k_pad)) | (k_pos == q_pos)
    return jnp.where(allowed, 0.0, -1e30)


def split3(v):
    hi = v.astype(bf16).astype(f32)
    mid = (v - hi).astype(bf16).astype(f32)
    return hi, mid, v - hi - mid


def at_lanes(base, first, values):
    lane = lax.broadcasted_iota(jnp.int32, base.shape, 1)
    for n, v in enumerate(values):
        base = jnp.where(lane == first + n, v, base)
    return base


def stack(a, heads):
    return jnp.concatenate([a[:, h * HEAD : (h + 1) * HEAD] for h in range(heads)], axis=0)


def project_kernel(sizes, orders, me_ref, x_ref, *refs):
    *pieces, w_ref, qkv_ref, gains_ref, normed = refs
    assemble(sizes, me_ref, orders, pieces, w_ref)
    rows = x_ref.shape[0]
    wide = qkv_ref.shape[1]
    key_at = wide - 2 * HEAD
    gains_ref[...] = gain_rows(w_ref[:, wide : wide + HEAD])[:8]

    @pl.loop(0, rows // 128, unroll=True)
    def _(t):
        at = pl.ds(pl.multiple_of(t * 128, 128), 128)
        normed[at, :] = norm_tile(x_ref[at, :].astype(f32), gains_ref[0:1, :]).astype(bf16)

    @pl.loop(0, key_at // 256, unroll=True)
    def _(j):
        at = pl.ds(pl.multiple_of(j * 256, 256), 256)
        qkv_ref[:, at] = (nn(normed[...], w_ref[:, at]) * (SCORE_SCALE * LOG2E)).astype(bf16)

    qkv_ref[:, key_at:] = nn(normed[...], w_ref[:, key_at:wide]).astype(bf16)


def project(sizes, orders, columns, me, x, pieces):
    rows, model = x.shape
    wide = columns - HEAD
    return call(
        functools.partial(project_kernel, sizes, orders),
        [shape((model, columns), bf16), shape((rows, wide), bf16), shape((8, model), f32)],
        (me, x, *pieces),
        2 * rows * model * wide,
        0,
        [pltpu.VMEM((rows, model), bf16)],
        VMEM_MIB,
        "project",
        [SM] + [VM] * (1 + len(pieces)),
    )


def marked(len_ref, qkv_ref, keys, values):
    rows, wide = qkv_ref.shape
    keys[:, :HEAD] = qkv_ref[:, wide - 2 * HEAD : wide - HEAD]
    values[:, :HEAD] = qkv_ref[:, wide - HEAD :]

    @pl.loop(0, rows // 128, unroll=True)
    def _(t):
        at = pl.ds(pl.multiple_of(t * 128, 128), 128)
        keys[at, HEAD:] = key_marks(len_ref, t * 128)
        values[at, HEAD:] = jnp.ones((128, HEAD), bf16)


def attention_forward_kernel(len_ref, qkv_ref, att_ref, lse_ref, keys, values):
    rows, wide = qkv_ref.shape
    heads = (wide - 2 * HEAD) // HEAD
    marked(len_ref, qkv_ref, keys, values)

    for i in range(rows // 128):
        ext = (i + 1) * 128
        q_at = slice(i * 128, ext)
        marks = query_marks(len_ref, i * 128).astype(bf16)
        bias = block_bias(len_ref, i * 128)
        lse = jnp.zeros((128, HEAD), f32)
        lane = lax.broadcasted_iota(jnp.int32, (128, HEAD), 1)
        for first in range(0, heads, GROUP):
            cols = slice(first * HEAD, (first + GROUP) * HEAD)
            q = stack(qkv_ref[q_at, cols], GROUP)
            q = jnp.concatenate([q, jnp.concatenate([marks] * GROUP, axis=0)], axis=1)
            s = nt(q, keys[:ext, :])
            last = s[:, ext - 128 :] + jnp.concatenate([bias] * GROUP, axis=0)
            s = jnp.concatenate([s[:, : ext - 128], last], axis=1) if i else last
            peak = jnp.max(s, axis=-1, keepdims=True)
            e = jnp.exp2(s - peak).astype(bf16)
            o = nn(e, values[:ext, :])
            total = o[:, HEAD:]
            low = peak + jnp.log2(total)
            o = (o[:, :HEAD] / total).astype(bf16)
            att_ref[q_at, cols] = jnp.concatenate([o[h * 128 : (h + 1) * 128] for h in range(GROUP)], axis=1)
            for h in range(GROUP):
                lse = jnp.where(lane == first + h, low[h * 128 : (h + 1) * 128], lse)
        lse_ref[q_at, :] = lse


def attention_forward(lengths, qkv):
    rows, wide = qkv.shape
    model = wide - 2 * HEAD
    return call(
        attention_forward_kernel,
        [shape((rows, model), bf16), shape((rows, HEAD), f32)],
        (lengths, qkv),
        4 * rows * rows * model,
        rows * rows * 4,
        [pltpu.VMEM((rows, 2 * HEAD), bf16), pltpu.VMEM((rows, 2 * HEAD), bf16)],
        VMEM_MIB,
        "attention_forward",
        [SM, VM],
    )


def branch_kernel(sizes, orders, me_ref, x_ref, att_ref, gains_ref, *refs):
    *pieces, wo_ref, hidden_ref, nt_ref = refs

    @pl.when(pl.program_id(0) == 0)
    def _():
        assemble(sizes, me_ref, orders, pieces, wo_ref)

    hidden_ref[...] = x_ref[...].astype(f32) + nn(att_ref[...], wo_ref[...])

    @pl.loop(0, x_ref.shape[0] // 128, unroll=True)
    def _(t):
        at = pl.ds(pl.multiple_of(t * 128, 128), 128)
        nt_ref[at, :] = norm_tile(hidden_ref[at, :], gains_ref[1:2, :]).astype(bf16)


def held(a):
    return pl.BlockSpec(a.shape, lambda i: (0, 0), pipeline_mode=pl.Buffered(1))


def branch(sizes, orders, me, x, att, gains, pieces):
    rows, model = x.shape
    tile = rows // 4
    wo = shape((model, model), bf16)
    strip = pl.BlockSpec((tile, model), lambda i: (i, 0))
    return call(
        functools.partial(branch_kernel, sizes, orders),
        [wo, shape((rows, model), f32), shape((rows, model), bf16)],
        (me, x, att, gains, *pieces),
        2 * rows * model * model,
        0,
        (),
        VMEM_MIB,
        "branch",
        [SM, strip, strip, held(gains), *map(held, pieces)],
        grid=(rows // tile,),
        out_specs=[held(wo), strip, strip],
    )


def gelu_both(v):
    v2 = v * v
    t = jnp.tanh(v * (GELU_A + GELU_B * v2))
    h = 0.5 + 0.5 * t
    a = v * h
    return a, h + (a - a * h) * ((2 * GELU_A) + (6 * GELU_B) * v2)


def ffn_kernel(sizes, order, me_ref, *refs):
    count, lines = seconds(sizes, order), firsts(sizes, order)
    take = lambda n: [refs.pop(0) for _ in range(n)]
    refs = list(refs)
    ins = take(4 + count)
    seen, whole, outs = take(4), take(2), take(lines)
    held_in = take(4 + count)
    acts, (up_ref, down_ref), (gu, gd), staged = take(4), take(2), take(2), take(lines)
    in_sem, out_sem = refs
    part, model = down_ref.shape
    shard = part // math.prod(sizes)
    tile = min(256, part)

    loads = [pltpu.make_async_copy(a, b, in_sem.at[n]) for n, (a, b) in enumerate(zip(ins, held_in))]
    for n in (*range(4, 4 + count), 0, 2, 1, 3):
        loads[n].start()
    started = []

    def store(src, dst):
        copy = pltpu.make_async_copy(src, dst, out_sem.at[len(started)])
        copy.start()
        started.append(copy)

    pieces = held_in[4:]
    for n in range(count):
        loads[4 + n].wait()
    for place, (first, second) in blocks_of(sizes, order):
        x, f = chip_at(sizes, order, me_ref, *place, -1)
        row = (first * sizes[1] + place[2]) * shard
        at = slice(row, row + shard)
        for core in range(2):
            up_ref[row_of(sizes, x, f, core, shard), :] = pieces[second][at, core * part : (core + 1) * part]
        down_ref[half_row_of(sizes, x, f, shard), :] = pieces[second][at, 2 * part :]
    store(up_ref, whole[0])
    store(down_ref, whole[1])

    nt_o, nt_p, dy_o, dy_p = held_in[:4]
    act_o, act_p, gi_o, gi_p = acts
    tiles = [slice(j * tile, (j + 1) * tile) for j in range(part // tile)]
    for j, cols in enumerate(tiles):
        for own, (n_ref, y_ref, a_ref, i_ref) in enumerate(((nt_o, dy_o, act_o, gi_o), (nt_p, dy_p, act_p, gi_p))):
            if j == 0:
                loads[own].wait()
            inner = nn(n_ref[...], up_ref[:, cols])
            if j == 0:
                loads[2 + own].wait()
            ga = nt(y_ref[...], down_ref[cols, :])
            a, slope = gelu_both(inner)
            a_ref[:, cols] = a.astype(bf16)
            i_ref[:, cols] = (ga * slope).astype(bf16)
    for n, a in enumerate(acts):
        store(a, seen[n])
    for cols in tiles:
        gu[:, cols] = (tn(nt_o[...], gi_o[:, cols]) + tn(nt_p[...], gi_p[:, cols])).astype(bf16)
    for cols in tiles:
        gd[cols, :] = (tn(act_o[:, cols], dy_o[...]) + tn(act_p[:, cols], dy_p[...])).astype(bf16)

    for line in reversed(range(lines)):
        for place, (first, second) in blocks_of(sizes, order):
            if first != line:
                continue
            x, f = chip_at(sizes, order, me_ref, *place, 1)
            row = (second * sizes[1] + place[2]) * shard
            at = slice(row, row + shard)
            for core in range(2):
                staged[line][at, core * part : (core + 1) * part] = gu[row_of(sizes, x, f, core, shard), :]
            staged[line][at, 2 * part :] = gd[half_row_of(sizes, x, f, shard), :]
        store(staged[line], outs[line])
    for copy in started:
        copy.wait()


def ffn(sizes, order, me, nt_o, nt_p, dy_o, dy_p, pieces):
    rows, model = nt_o.shape
    part = model // 2
    up, down = shape((model, part), bf16), shape((part, model), bf16)
    lines = firsts(sizes, order)
    grads = [shape((part // lines, 2 * model), bf16)] * lines
    ins = (nt_o, nt_p, dy_o, dy_p, *pieces)
    outs = [shape((rows, part), bf16)] * 4 + [up, down] + grads
    far = pl.BlockSpec(memory_space=pl.ANY)
    outs = call(
        functools.partial(ffn_kernel, sizes, order),
        outs,
        (me, *ins),
        16 * rows * model * part,
        2 * rows * part,
        [pltpu.VMEM(a.shape, bf16) for a in (*ins, *outs[:4], up, down, up, down, *grads)]
        + [pltpu.SemaphoreType.DMA((len(ins),)), pltpu.SemaphoreType.DMA((len(outs),))],
        VMEM_MIB,
        "ffn",
        [SM] + [far] * len(ins),
        out_specs=[far] * len(outs),
    )
    return outs[:4], outs[4], outs[5], outs[6:]


def hidden_backward_kernel(count, *refs):
    gis, ups, gn_ref = refs[:count], refs[count : 2 * count], refs[2 * count]
    total = None
    for i, u in zip(gis, ups):
        v = nt(i[...], u[...])
        total = v if total is None else total + v
    gn_ref[...] = total.astype(bf16)


def hidden_backward(gis, ups):
    rows, part = gis[0].shape
    model = ups[0].shape[0]
    count = len(gis)
    tile = model // 4
    return call(
        functools.partial(hidden_backward_kernel, count),
        [shape((rows, model), bf16)],
        (*gis, *ups),
        count * 2 * rows * part * model,
        0,
        (),
        VMEM_MIB,
        "hidden_backward",
        [pl.BlockSpec((tile, part), lambda g: (g, 0))] * count + [held(u) for u in ups],
        grid=(rows // tile,),
        out_specs=[pl.BlockSpec((tile, model), lambda g: (g, 0))],
    )[0]


def down_kernel(count, *refs):
    acts, downs, more, out_ref = refs[:count], refs[count : 2 * count], refs[2 * count : -1], refs[-1]
    total = None
    for a, d in zip(acts, downs):
        v = nn(a[...], d[...])
        total = v if total is None else total + v
    for m in more:
        total = total + m[...].astype(f32)
    out_ref[...] = total.astype(bf16)


def down(acts, downs, more):
    rows, part = acts[0].shape
    model = downs[0].shape[1]
    count = len(acts)
    tile = rows // 4
    strip = pl.BlockSpec((tile, model), lambda g: (g, 0))
    return call(
        functools.partial(down_kernel, count),
        [shape((rows, model), bf16)],
        (*acts, *downs, *more),
        count * 2 * rows * part * model,
        0,
        (),
        VMEM_MIB,
        "down",
        [pl.BlockSpec((tile, part), lambda g: (g, 0))] * count + [held(d) for d in downs] + [strip] * len(more),
        grid=(rows // tile,),
        out_specs=[strip],
    )[0]


def branch_backward_kernel(sizes, orders, count, me_ref, hidden_ref, gn_ref, dy_ref, att_ref, gains_ref, wo_ref, *refs):
    gis, ups, refs = refs[:count], refs[count : 2 * count], refs[2 * count :]
    gh_ref, gatt_ref, gg_ref, *halves, gn, gb, gwo, low = refs
    step = pl.program_id(0)
    rows = hidden_ref.shape[0]

    @pl.when(step == 0)
    def _():
        gg_ref[...] = jnp.zeros_like(gg_ref)
        gwo[...] = jnp.zeros_like(gwo)

    total = gn_ref[...].astype(f32)
    for i, u in zip(gis, ups):
        total = total + nt(i[...], u[...])
    gn[...] = total

    @pl.loop(0, rows // 64, unroll=True)
    def _(t):
        at = pl.ds(pl.multiple_of(t * 64, 64), 64)
        h, n = hidden_ref[at, :], gn[at, :]
        r = lax.rsqrt(jnp.mean(h * h, axis=-1, keepdims=True) + EPS)
        z = h * r
        gg_ref[1:2, :] += jnp.sum(n * z, axis=0, keepdims=True)
        g = n * gains_ref[1:2, :]
        gh = dy_ref[at, :].astype(f32) + r * (g - z * jnp.mean(g * z, axis=-1, keepdims=True))
        gh_ref[at, :] = gh
        gb[at, :] = gh.astype(bf16)

    gatt_ref[...] = nt(gb[...], wo_ref[...]).astype(bf16)
    gwo[...] += tn(att_ref[...], gb[...])

    @pl.when(step == pl.num_programs(0) - 1)
    def _():
        low[...] = gwo[...].astype(bf16)
        hand_out(sizes, me_ref, orders, low, halves)


def branch_backward(sizes, orders, me, hidden, gn, dy, att, gains, wo, gis, ups):
    rows, model = hidden.shape
    part = gis[0].shape[1]
    count = len(gis)
    tile = rows // 4
    strip = pl.BlockSpec((tile, model), lambda i: (i, 0))
    gg = shape((8, model), f32)
    halves = [shape((model // 2, model // len(orders)), bf16)] * (2 * len(orders))
    return call(
        functools.partial(branch_backward_kernel, sizes, orders, count),
        [shape((rows, model), f32), shape((rows, model), bf16), gg, *halves],
        (me, hidden, gn, dy, att, gains, wo, *gis, *ups),
        4 * rows * model * model + count * 2 * rows * part * model,
        0,
        [
            pltpu.VMEM((tile, model), f32),
            pltpu.VMEM((tile, model), bf16),
            pltpu.VMEM((model, model), f32),
            pltpu.VMEM((model, model), bf16),
        ],
        VMEM_MIB,
        "branch_backward",
        [SM, strip, strip, strip, strip, held(gains), held(wo)]
        + [pl.BlockSpec((tile, part), lambda i: (i, 0))] * count
        + [held(u) for u in ups],
        grid=(rows // tile,),
        out_specs=[strip, strip, held(gg), *map(held, halves)],
    )


def attention_backward_kernel(
    len_ref, qkv_ref, ga_ref, att_ref, lse_ref, g_ref, keys, values, probs, gscores, dk, dv
):
    rows, wide = qkv_ref.shape
    heads = (wide - 2 * HEAD) // HEAD
    key_at = heads * HEAD
    dk[...] = jnp.zeros_like(dk)
    dv[...] = jnp.zeros_like(dv)
    marked(len_ref, qkv_ref, keys, values)

    for i in range(rows // 128):
        ext = (i + 1) * 128
        q_at = slice(i * 128, ext)
        marks = query_marks(len_ref, i * 128)
        bias = block_bias(len_ref, i * 128)
        for first in range(0, heads, GROUP):
            cols = slice(first * HEAD, (first + GROUP) * HEAD)
            q = stack(qkv_ref[q_at, cols], GROUP)
            ga = stack(ga_ref[q_at, cols], GROUP)
            q_more, ga_more = [], []
            for h in range(first, first + GROUP):
                at = slice(h * HEAD, (h + 1) * HEAD)
                q_more.append(at_lanes(marks, MARKS, split3(-lse_ref[q_at, h : h + 1])).astype(bf16))
                delta = jnp.sum(ga_ref[q_at, at].astype(f32) * att_ref[q_at, at].astype(f32), axis=-1, keepdims=True)
                ga_more.append(at_lanes(jnp.zeros((128, HEAD), f32), 0, split3(-delta)).astype(bf16))
            s = nt(jnp.concatenate([q, jnp.concatenate(q_more, axis=0)], axis=1), keys[:ext, :])
            gp = nt(jnp.concatenate([ga, jnp.concatenate(ga_more, axis=0)], axis=1), values[:ext, :])
            last = s[:, ext - 128 :] + jnp.concatenate([bias] * GROUP, axis=0)
            s = jnp.concatenate([s[:, : ext - 128], last], axis=1) if i else last
            p = jnp.exp2(s)
            out = slice(first * 128, (first + GROUP) * 128)
            probs[out, :ext] = p.astype(bf16)
            gscores[out, :ext] = (p * gp).astype(bf16)
        dv[:ext, :] += tn(probs[:, :ext], stack(ga_ref[q_at, :], heads))
        dk[:ext, :] += tn(gscores[:, :ext], stack(qkv_ref[q_at, :key_at], heads))
        gq = (nn(gscores[:, :ext], keys[:ext, :HEAD]) * SCORE_SCALE).astype(bf16)
        g_ref[q_at, :key_at] = jnp.concatenate([gq[h * 128 : (h + 1) * 128] for h in range(heads)], axis=1)

    g_ref[:, key_at : key_at + HEAD] = (dk[...] * (1.0 / LOG2E)).astype(bf16)
    g_ref[:, key_at + HEAD :] = dv[...].astype(bf16)


def attention_backward(lengths, qkv, ga, att, lse):
    rows, wide = qkv.shape
    model = ga.shape[1]
    return call(
        attention_backward_kernel,
        [shape(qkv.shape, bf16)],
        (lengths, qkv, ga, att, lse),
        10 * rows * rows * model,
        rows * rows * 4,
        [
            pltpu.VMEM((rows, 2 * HEAD), bf16),
            pltpu.VMEM((rows, 2 * HEAD), bf16),
            pltpu.VMEM((model, rows), bf16),
            pltpu.VMEM((model, rows), bf16),
            pltpu.VMEM((rows, HEAD), f32),
            pltpu.VMEM((rows, HEAD), f32),
        ],
        VMEM_MIB,
        "attention_backward",
        [SM] + [VM] * 4,
    )[0]


def projection_grads_kernel(sizes, orders, me_ref, x_ref, g_ref, w_ref, gains_ref, gg_ref, *refs):
    *halves, normed, gw = refs
    rows, model = x_ref.shape
    wide = g_ref.shape[1]

    @pl.loop(0, rows // 128, unroll=True)
    def _(t):
        at = pl.ds(pl.multiple_of(t * 128, 128), 128)
        normed[at, :] = norm_tile(x_ref[at, :].astype(f32), gains_ref[0:1, :]).astype(bf16)

    dots = jnp.zeros((model, HEAD), f32)
    for j in range(wide // 256):
        at = slice(j * 256, (j + 1) * 256)
        v = tn(normed[...], g_ref[:, at])
        gw[:, at] = v.astype(bf16)
        v = v * w_ref[:, at].astype(f32)
        dots = dots + (v[:, :HEAD] + v[:, HEAD:])
    one = jnp.sum(dots, axis=-1, keepdims=True) / w_ref[:, wide : wide + 1].astype(f32)
    two = jnp.concatenate([gg_ref[...], jnp.zeros((HEAD - 8, model), f32)], axis=0).T
    lane = lax.broadcasted_iota(jnp.int32, (model, HEAD), 1)
    gw[:, wide : wide + HEAD] = jnp.where(lane == 0, one, two).astype(bf16)
    hand_out(sizes, me_ref, orders, gw, halves)


def projection_grads(sizes, orders, widths, me, x, g, w, gains, gg):
    rows, model = x.shape
    halves = [shape((w.shape[0] // 2, width), bf16) for width in widths for _ in range(2)]
    return call(
        functools.partial(projection_grads_kernel, sizes, orders),
        halves,
        (me, x, g, w, gains, gg),
        2 * rows * model * g.shape[1],
        0,
        [pltpu.VMEM((rows, model), bf16), pltpu.VMEM(w.shape, bf16)],
        VMEM_MIB,
        "projection_grads",
        [SM] + [VM] * 5,
    )


def input_backward_kernel(x_ref, g_ref, gh_ref, w_ref, gains_ref, gx_ref, gn):
    rows = x_ref.shape[0]
    gn[...] = nt(g_ref[...], w_ref[:, : g_ref.shape[1]])

    @pl.loop(0, rows // 64, unroll=True)
    def _(t):
        at = pl.ds(pl.multiple_of(t * 64, 64), 64)
        x = x_ref[at, :].astype(f32)
        r = lax.rsqrt(jnp.mean(x * x, axis=-1, keepdims=True) + EPS)
        z = x * r
        g = gn[at, :] * gains_ref[0:1, :]
        gx_ref[at, :] = (gh_ref[at, :] + r * (g - z * jnp.mean(g * z, axis=-1, keepdims=True))).astype(bf16)


def input_backward(x, g, gh, w, gains):
    rows, model = x.shape
    tile = rows // 4
    strip = lambda a: pl.BlockSpec((tile, a.shape[1]), lambda i: (i, 0))
    return call(
        input_backward_kernel,
        [shape(x.shape, bf16)],
        (x, g, gh, w, gains),
        2 * rows * model * g.shape[1],
        0,
        [pltpu.VMEM((tile, model), f32)],
        VMEM_MIB,
        "input_backward",
        [strip(x), strip(g), strip(gh), held(w), held(gains)],
        grid=(rows // tile,),
        out_specs=[strip(x)],
    )[0]


def after(a, *first):
    return lax.optimization_barrier((a, *first))[0]


def spread(a, axis, n):
    return [a] + [lax.ppermute(a, axis, [(i, (i + s) % n) for i in range(n)]) for s in range(1, n)]


def add(parts):
    total = parts[0].astype(f32)
    for p in parts[1:]:
        total = total + p.astype(f32)
    return total


def send_on(parts, axis, n):
    return [lax.ppermute(parts[s], axis, [(i, (i + s) % n) for i in range(n)]) for s in range(1, n)]


def cut(a, s, n):
    rows = a.shape[0] // n
    return a[s * rows : (s + 1) * rows]


def cut_columns(a, s, n):
    columns = a.shape[1] // n
    return a[:, s * columns : (s + 1) * columns]


class Hops:
    def __init__(self, sizes, order):
        x, b = ("x", sizes[0]), ("f2", sizes[2])
        self.axes = (x, b) if order[0] else (b, x)

    def gather_one(self, block):
        self.lines = spread(block, *self.axes[0])
        return self.lines[1:]

    def gather_two(self):
        self.pieces = spread(jnp.concatenate(self.lines, axis=0), *self.axes[1])
        return self.pieces

    def reduce_one(self, parts):
        self.got = [parts[0], *send_on(parts, *self.axes[0])]

    def reduce_two(self):
        n = self.axes[1][1]
        parts = [add([cut(p, s, n) for p in self.got]).astype(bf16) for s in range(n)]
        self.got = [parts[0], *send_on(parts, *self.axes[1])]
        return parts

    def sum_two(self, n=1):
        return [add([cut(p, s, n) for p in self.got]).astype(bf16) for s in range(n)]


def on_device(
    sizes, tokens, doc_lengths, gain_one, query_weight, key_weight, value_weight, out_weight,
    gain_two, up_weight, down_weight, cotangent,
):
    nx, na, nb = sizes
    fsdp = na * nb
    core = lax.axis_index("core")
    me = jnp.stack([lax.axis_index(a) for a in ("x", "f1", "f2", "core")]).astype(jnp.int32)
    swap = lambda a: lax.ppermute(a, "core", [(0, 1), (1, 0)])
    rows, model = tokens.shape
    shard = query_weight.shape[0]
    ff = up_weight.shape[1]
    chunks = down_weight.shape[0] // shard
    part = ff // (2 * chunks)
    wide = 2 * model
    x_then, b_then = (True, True), (False, True)
    by_index = [(c % 2 == 0, False) for c in range(chunks)]

    lane = lax.broadcasted_iota(jnp.int32, (shard, HEAD), 1)
    gain_block = jnp.where(lane == 0, gain_one[:, None], jnp.where(lane == 1, gain_two[:, None], jnp.zeros((), bf16)))
    w_rows = jnp.concatenate([query_weight, key_weight, value_weight, gain_block], axis=1)
    columns = w_rows.shape[1]
    first_share = columns // 256 * HEAD
    w_orders, w_widths = (x_then, b_then), (first_share, columns - first_share)
    w_along = spread(w_rows, "f1", na)

    up = up_weight.reshape(shard, nx, 2, fsdp, chunks, shard).transpose(2, 0, 4, 1, 3, 5)
    up = up.reshape(2, shard, chunks, part)
    up_keep = jnp.where(core == 0, up[0], up[1])
    up_come = swap(jnp.where(core == 0, up[1], up[0]))
    up_pair = jnp.where(core == 0, jnp.stack([up_keep, up_come], 2), jnp.stack([up_come, up_keep], 2))
    up_pair = up_pair.reshape(shard, chunks, wide // 2)
    down_rows = down_weight.reshape(chunks, shard, model)
    f_along = []
    for first in range(0, chunks, 2):
        mine = jnp.concatenate([p for c in (first, first + 1) for p in (up_pair[:, c], down_rows[c])], axis=1)
        f_along.append(lax.all_gather(after(mine, *w_along[1:]), "f1", axis=0, tiled=True))

    w_block = jnp.concatenate(w_along, axis=0)
    w_hops = [Hops(sizes, order) for order in w_orders]
    lines = w_hops[0].gather_one(w_block[:, :first_share]) + w_hops[1].gather_one(w_block[:, first_share:])
    wo_along = spread(after(out_weight, *lines), "f1", na)
    w_pieces = []
    for h in w_hops:
        p = h.gather_two()
        w_pieces += p + [swap(a) for a in p]
    wo_orders = (x_then, b_then)
    wo_block = jnp.concatenate(wo_along, axis=0)
    wo_hops = [Hops(sizes, order) for order in wo_orders]
    for n, h in enumerate(wo_hops):
        h.gather_one(cut_columns(wo_block, n, 2))
    wo_pieces = []
    for h in wo_hops:
        p = h.gather_two()
        wo_pieces += p + [swap(a) for a in p]
    hops = [Hops(sizes, order) for order in by_index]
    f_lines = lambda c: hops[c].gather_one(cut_columns(f_along[c // 2], c % 2, 2))

    w, qkv, gains = project(sizes, w_orders, columns, me, tokens, w_pieces)
    lines = [p for c in (0, 1) for p in f_lines(c)]
    att, lse = attention_forward(doc_lengths, after(qkv, *lines))
    pieces = {c: hops[c].gather_two() for c in (0, 1)}
    dy_p = swap(after(cotangent, qkv))
    wo, hidden, nt_o = branch(sizes, wo_orders, me, tokens, att, gains, wo_pieces)
    nt_p = swap(nt_o)

    acts_o, acts_p, gis_o, gis_p, ups, downs = [], [], [], [], [], []

    def run_ffn(c, *first):
        seen, up_c, down_c, grads = ffn(sizes, by_index[c], me, after(nt_o, *first), nt_p, cotangent, dy_p, pieces[c])
        for kept, a in zip((acts_o, acts_p, gis_o, gis_p), seen):
            kept.append(a)
        ups.append(up_c)
        downs.append(down_c)
        hops[c].reduce_one(grads)

    def sum_cores(keep, come, order):
        n = firsts(sizes, order)
        return [add([cut(a, s, n) for a in (keep, come)]).astype(bf16) for s in range(n)]

    f_along[1] = after(f_along[1], att)
    lines = [p for c in (2, 3) for p in f_lines(c)]
    run_ffn(0, *pieces[1])
    run_ffn(1, *lines, ups[0])
    for c in (2, 3):
        pieces[c] = hops[c].gather_two()
    run_ffn(2, ups[1])
    ready = hops[0].reduce_two()
    run_ffn(3, *ready, ups[2])
    ready = hops[1].reduce_two()
    gn_p = hidden_backward([after(gis_p[0], *ready), *gis_p[1:]], ups)
    gn_r = swap(gn_p)
    ready = hops[2].reduce_two()
    out_p = down([after(acts_p[0], gn_p, *ready), *acts_p[1:]], downs, [])
    out_r = swap(out_p)
    last = lambda a: lax.psum_scatter(a, "f1", scatter_dimension=0, tiled=True)
    pair = jnp.concatenate([hops[c].sum_two()[0] for c in (0, 1)], axis=1)
    sums = [last(pair)]
    gh, gatt, gg, *halves = branch_backward(
        sizes, wo_orders[:1], me, hidden, gn_r, cotangent, att, gains, wo, [after(gis_o[0], out_p, pair), *gis_o[1:]], ups
    )
    come = swap(halves[1])
    ready = hops[3].reduce_two()
    wo_reduce = Hops(sizes, x_then)
    ready += sum_cores(halves[0], come, x_then)
    wo_reduce.reduce_one(ready[-firsts(sizes, x_then) :])
    g = attention_backward(doc_lengths, after(qkv, *ready), gatt, att, lse)
    ready = wo_reduce.reduce_two()
    pair = jnp.concatenate([hops[c].sum_two()[0] for c in (2, 3)], axis=1)
    sums.append(last(pair))
    halves = projection_grads(sizes, w_orders, w_widths, me, after(tokens, *ready, pair), g, w, gains, gg)
    come = [swap(h) for h in halves[1::2]]
    wo_parts = wo_reduce.sum_two(na)
    wo_got = send_on(wo_parts, "f1", na)
    ready = [sum_cores(k, c, o) for k, c, o in zip(halves[0::2], come, w_orders)]
    w_reduce = [Hops(sizes, order) for order in w_orders]
    for h, r in zip(w_reduce, ready):
        h.reduce_one(r)
    ready = [r for rs in ready for r in rs]
    grad_tokens = input_backward(after(tokens, *ready), g, gh, w, gains)
    for h in w_reduce:
        h.got = [after(p, grad_tokens) for p in h.got]
        h.reduce_two()
    grad_out = add([wo_parts[0], *wo_got])
    output = down([after(acts_o[0], grad_tokens), *acts_o[1:]], downs, [hidden, out_r])
    for h in w_reduce:
        h.got = [after(p, output) for p in h.got]
    w_parts = [jnp.concatenate(p, axis=1) for p in zip(*[h.sum_two(na) for h in w_reduce])]
    gw = add([w_parts[0], *send_on(w_parts, "f1", na)])

    sums = jnp.stack([s.reshape(shard, 2, wide) for s in sums], axis=1).reshape(shard, chunks, wide)
    grad_down = sums[:, :, model:].transpose(1, 0, 2).reshape(chunks * shard, model).astype(f32)
    g_up = sums[:, :, :model].reshape(shard, chunks, 2, part)
    keep = jnp.where(core == 0, g_up[:, :, 0], g_up[:, :, 1])
    come = swap(jnp.where(core == 0, g_up[:, :, 1], g_up[:, :, 0]))
    grad_up = jnp.where(core == 0, jnp.stack([keep, come], 0), jnp.stack([come, keep], 0))
    grad_up = grad_up.reshape(2, shard, chunks, nx, fsdp, shard).transpose(1, 3, 0, 4, 2, 5)
    grad_up = grad_up.reshape(shard, ff).astype(f32)

    qw = query_weight.shape[1]
    return (
        output,
        grad_tokens,
        gw[:, qw + 2 * HEAD],
        gw[:, :qw],
        gw[:, qw : qw + HEAD],
        gw[:, qw + HEAD : qw + 2 * HEAD],
        grad_out,
        gw[:, qw + 2 * HEAD + 1],
        grad_up,
        grad_down,
    )


def solution(mesh):
    dp, fsdp = mesh.shape["dp"], mesh.shape["fsdp"]
    sizes = (dp // 2, 4, fsdp // 4)
    names = ("x", "core", "f1", "f2")
    split = Mesh(mesh.devices.reshape(sizes[0], 2, *sizes[1:]), names)
    rows, line = P(names, None), P(names)
    return jax.shard_map(
        functools.partial(on_device, sizes),
        mesh=split,
        in_specs=(rows, rows, line, rows, rows, rows, rows, line, rows, rows, rows),
        out_specs=(rows, rows, line, rows, rows, rows, rows, line, rows, rows),
        check_vma=False,
    )
```

time: 865 us -> 405 us (0.47)
  waiting for transfers between devices: 602 us -> 95.3 us
  starting transfers between devices: 2.16 us -> 57.8 us
  other arithmetic: 11.5 us -> 32.1 us
  local copies, waits for them, and re-layouts: 39.9 us -> 20.8 us
    reduce_scatter x4 -> x2, waiting for transfers between devices: 406 us -> 0.01 us  [on_device(): last = lambda a: lax.psum_scatter(a, 'f1', scatter_dimension=0, tiled=True)]
    all_gather x4 -> x2, waiting for transfers between devices: 190 us -> 0.97 us  [on_device(): lax.all_gather(after(mine, *w_along[1:]), 'f1', axis=0, tiled=True)]
    ppermute x0 -> x42, waiting for transfers between devices: none -> 91.5 us  [the longest x22 55.7 us: spread(): lax.ppermute(a, axis, [(i, (i + s) % n) for i in range(n)])]
    ppermute x0 -> x42, starting transfers between devices: none -> 54 us  [the longest x22 30.1 us: spread(): lax.ppermute(a, axis, [(i, (i + s) % n) for i in range(n)])]
    unnamed x48 -> x73, local copies, waits for them, and re-layouts: 27.4 us -> 4.77 us
    convert_element_type x2 -> x17, other arithmetic: 2.41 us -> 17.6 us  [the longest x7 6.95 us: sum_two(): add([cut(p, s, n) for p in self.got]).astype(bf16)]
    pallas_call x9 -> x14, Pallas kernels: 187 us -> 179 us  [call(): pl.pallas_call(kernel, out_shape=outs, in_specs=in_specs or [VM] * len(ar...]
  transfers between devices with their start and end apart: 14 -> 63, of which waited for: 10 -> 23; matrix products, arithmetic and copies ran while one was open for 2% -> 11% of each run, Pallas kernels for 15% -> 45%
where the time goes in v3:
time: 405 us; the launch traced here: 400 us
  Pallas kernels  179 us (44%)
  waiting for transfers between devices  95.3 us (24%)
  starting transfers between devices  57.8 us (14%)
  other arithmetic  32.1 us (8%)
  local copies, waits for them, and re-layouts  20.8 us (5%)
  between operations  14.9 us (4%)
    pallas_call x14, Pallas kernels, call(): pl.pallas_call(kernel, out_shape=outs, in_specs=in_specs or [VM] * len(ar...  179 us
    ppermute x22, waiting for transfers between devices, spread(): lax.ppermute(a, axis, [(i, (i + s) % n) for i in range(n)])  55.7 us
    ppermute x20, waiting for transfers between devices, send_on(): lax.ppermute(parts[s], axis, [(i, (i + s) % n) for i in range(n)])  35.8 us
    ppermute x22, starting transfers between devices, spread(): lax.ppermute(a, axis, [(i, (i + s) % n) for i in range(n)])  30.1 us
    ppermute x20, starting transfers between devices, send_on(): lax.ppermute(parts[s], axis, [(i, (i + s) % n) for i in range(n)])  24 us
  transfers between devices with their start and end apart: 63, of which 23 were waited for; matrix products, arithmetic and copies ran while one was open for 11% of the time, Pallas kernels for 45%

profile of v3, /device:TPU:0, one launch (start us, length us, event | category | flops | bytes accessed | tf_op | source)
XLA Modules:
  0.0 399.6 jit_solution(13520918345913162707)
XLA Ops:
  8.9 5.1 %collective-permute-start.2 = (bf16[32,1408]{1,0:T(8,128)(2,1)S(1)}, bf16[32,1408]{1,0:T(8,128)(2,1)S(1)}, u32[]{:S(2)}, u32[]{:S(2)}) collective-permute-start(bf16[32,1408]{1,0:T(8,128)(2,1)S(1)} %pad_maximum_fusion.20), channel_id=1, source_target_pairs={{0,6},{2,0},{4,2},{6,4},{1,7},{3,1},{5,3},{7,5},{8,14},{10,8},{12,... | collective-permute-start | bytes 270344 | tf_op jit(solution)/shard_map/ppermute | solution.py:690
  25.4 3.9 collective-permute-done.3
  46.1 6.6 %collective-permute-done.21 = bf16[128,512]{1,0:T(8,128)(2,1)S(1)} collective-permute-done((bf16[128,512]{1,0:T(8,128)(2,1)S(1)}, bf16[128,512]{1,0:T(8,128)(2,1)S(1)}, u32[]{:S(2)}, u32[]{:S(2)}) %collective-permute-start.21) | collective-permute-done | bytes 131104 | tf_op jit(solution)/shard_map/ppermute | solution.py:690
  61.5 15.1 %collective-permute-done.22.refs_5_ = bf16[256,512]{1,0:T(8,128)(2,1)} collective-permute-done((bf16[256,512]{1,0:T(8,128)(2,1)}, bf16[256,512]{1,0:T(8,128)(2,1)}, u32[]{:S(2)}, u32[]{:S(2)}) %collective-permute-start.22) | collective-permute-done | bytes 262176 | tf_op jit(solution)/shard_map/ppermute | solution.py:690
  80.0 7.5 %project.1 = (bf16[1024,1408]{1,0:T(8,128)(2,1)}, bf16[1024,1280]{1,0:T(8,128)(2,1)}, f32[8,1024]{1,0:T(8,128)}) custom-call(s32[4]{0:T(128)} %pad_add_fusion.me_ref, bf16[1024,1024]{1,0:T(8,128)(2,1)} %x_ref.5, bf16[256,640]{1,0:T(8,128)(2,1)} %copy-done.12, bf16[256,640]{1,0:T(8,128)(2,1)} %copy-done.28, bf16[256,640]{1,0:T(8,128)(2,1)} %copy-done.29, ...), custom_call_target="tpu_custom_call" | custom-call | flops 335544320 | bytes 1314818 | tf_op jit(solution)/shard_map/project/pallas_call | solution.py:46
  88.0 10.5 %attention_forward.1 = (bf16[1024,1024]{1,0:T(8,128)(2,1)}, f32[1024,128]{1,0:T(8,128)}) custom-call(s32[1,8]{1,0:T(1,128)} %len_ref.3, bf16[1024,1280]{1,0:T(8,128)(2,1)} %get-tuple-element.135.qkv_ref), custom_call_target="tpu_custom_call" | custom-call | flops 536870912 | bytes 655364 | tf_op jit(solution)/shard_map/attention_forward/pallas_call | solution.py:46
  98.6 7.9 %branch.1 = (bf16[1024,1024]{1,0:T(8,128)(2,1)}, f32[1024,1024]{1,0:T(8,128)}, bf16[1024,1024]{1,0:T(8,128)(2,1)}) custom-call(s32[4]{0:T(128)} %pad_add_fusion.me_ref, bf16[1024,1024]{1,0:T(8,128)(2,1)} %x_ref.5, bf16[1024,1024]{1,0:T(8,128)(2,1)} %get-tuple-element.87.att_ref, f32[8,1024]{1,0:T(8,128)} %get-tuple-element.88.gains_ref, ...), custom_call_target="tpu_custom_call" | custom-call | flops 268435456 | bytes 1839106 | tf_op jit(solution)/shard_map/branch/pallas_call | solution.py:46
  114.4 19.6 %collective-permute-done.25.refs_5_ = bf16[256,2048]{1,0:T(8,128)(2,1)} collective-permute-done((bf16[256,2048]{1,0:T(8,128)(2,1)S(1)}, bf16[256,2048]{1,0:T(8,128)(2,1)}, u32[]{:S(2)}, u32[]{:S(2)}) %collective-permute-start.25) | collective-permute-done | bytes 1048608 | tf_op jit(solution)/shard_map/ppermute | solution.py:690
  136.2 16.9 %ffn.4 = (bf16[1024,512]{1,0:T(8,128)(2,1)}, bf16[1024,512]{1,0:T(8,128)(2,1)}, bf16[1024,512]{1,0:T(8,128)(2,1)}, bf16[1024,512]{1,0:T(8,128)(2,1)}, bf16[1024,...) custom-call(s32[4]{0:T(128)} %pad_add_fusion.me_ref, ...), custom_call_target="tpu_custom_call" | custom-call | flops 1073741824 | bytes 2359298 | tf_op jit(solution)/shard_map/ffn/pallas_call | solution.py:46
  156.1 17.2 %ffn.5 = (bf16[1024,512]{1,0:T(8,128)(2,1)}, bf16[1024,512]{1,0:T(8,128)(2,1)}, bf16[1024,512]{1,0:T(8,128)(2,1)}, bf16[1024,512]{1,0:T(8,128)(2,1)}, bf16[1024,...) custom-call(s32[4]{0:T(128)} %pad_add_fusion.me_ref, ...), custom_call_target="tpu_custom_call" | custom-call | flops 1073741824 | bytes 2359298 | tf_op jit(solution)/shard_map/ffn/pallas_call | solution.py:46
  181.3 17.6 %ffn.6 = (bf16[1024,512]{1,0:T(8,128)(2,1)}, bf16[1024,512]{1,0:T(8,128)(2,1)}, bf16[1024,512]{1,0:T(8,128)(2,1)}, bf16[1024,512]{1,0:T(8,128)(2,1)}, bf16[1024,...) custom-call(s32[4]{0:T(128)} %pad_add_fusion.me_ref, ...), custom_call_target="tpu_custom_call" | custom-call | flops 1073741824 | bytes 2359298 | tf_op jit(solution)/shard_map/ffn/pallas_call | solution.py:46
  207.2 5.5 %collective-permute-done.37 = bf16[128,2048]{1,0:T(8,128)(2,1)} collective-permute-done((bf16[128,2048]{1,0:T(8,128)(2,1)S(1)}, bf16[128,2048]{1,0:T(8,128)(2,1)}, u32[]{:S(2)}, u32[]{:S(2)}) %collective-permute-start.37) | collective-permute-done | bytes 524320 | tf_op jit(solution)/shard_map/ppermute | solution.py:701
  214.2 17.3 %ffn.7 = (bf16[1024,512]{1,0:T(8,128)(2,1)}, bf16[1024,512]{1,0:T(8,128)(2,1)}, bf16[1024,512]{1,0:T(8,128)(2,1)}, bf16[1024,512]{1,0:T(8,128)(2,1)}, bf16[1024,...) custom-call(s32[4]{0:T(128)} %pad_add_fusion.me_ref, ...), custom_call_target="tpu_custom_call" | custom-call | flops 1073741824 | bytes 2359298 | tf_op jit(solution)/shard_map/ffn/pallas_call | solution.py:46
  234.9 8.7 %hidden_backward.1 = bf16[1024,1024]{1,0:T(8,128)(2,1)} custom-call(bf16[1024,512]{1,0:T(8,128)(2,1)} %get-tuple-element.102.refs_0_, bf16[1024,512]{1,0:T(8,128)(2,1)} %get-tuple-element.103.refs_1_, bf16[1024,512]{1,0:T(8,128)(2,1)} %get-tuple-element.106.refs_2_, bf16[1024,512]{1,0:T(8,128)(2,1)} %get-tuple-element.111.refs_3_, ...), custom_call_target="tpu_custom_call" | custom-call | flops 536870912 | bytes 1310720 | tf_op jit(solution)/shard_map/hidden_backward/pallas_call | solution.py:46
  247.3 10.7 %collective-permute-done.42 = bf16[256,2048]{1,0:T(8,128)(2,1)} collective-permute-done((bf16[256,2048]{1,0:T(8,128)(2,1)}, bf16[256,2048]{1,0:T(8,128)(2,1)}, u32[]{:S(2)}, u32[]{:S(2)}) %collective-permute-start.42) | collective-permute-done | bytes 1048608 | tf_op jit(solution)/shard_map/ppermute | solution.py:701
  260.9 5.1 %collective-permute-done.41 = bf16[128,2048]{1,0:T(8,128)(2,1)} collective-permute-done((bf16[128,2048]{1,0:T(8,128)(2,1)S(1)}, bf16[128,2048]{1,0:T(8,128)(2,1)}, u32[]{:S(2)}, u32[]{:S(2)}) %collective-permute-start.41) | collective-permute-done | bytes 524320 | tf_op jit(solution)/shard_map/ppermute | solution.py:701
  267.5 8.6 %down.2 = bf16[1024,1024]{1,0:T(8,128)(2,1)} custom-call(bf16[1024,512]{1,0:T(8,128)(2,1)} %get-tuple-element.118.refs_0_, bf16[1024,512]{1,0:T(8,128)(2,1)} %get-tuple-element.119.refs_1_, bf16[1024,512]{1,0:T(8,128)(2,1)} %get-tuple-element.120.refs_2_, bf16[1024,512]{1,0:T(8,128)(2,1)} %get-tuple-element.121.refs_3_, ...), custom_call_target="tpu_custom_call" | custom-call | flops 536870912 | bytes 1310720 | tf_op jit(solution)/shard_map/down/pallas_call | solution.py:46
  279.2 18.6 %branch_backward.1 = (f32[1024,1024]{1,0:T(8,128)}, bf16[1024,1024]{1,0:T(8,128)(2,1)}, f32[8,1024]{1,0:T(8,128)}, bf16[512,1024]{1,0:T(8,128)(2,1)}, bf16[512,1024]{1,0:T(8,128)(2,1)}) custom-call(s32[4]{0:T(128)} %pad_add_fusion.me_ref, f32[1024,1024]{1,0:T(8,128)} %get-tuple-element.94.hidden_ref.refs_8_, bf16[1024,1024]{1,0:T(8,128)(2,1)} %copy-done.4, ...), custom_call_target="tpu_custom_call" | custom-call | flops 1073741824 | bytes 3678210 | tf_op jit(solution)/shard_map/branch_backward/pallas_call | solution.py:46
  305.3 20.6 %attention_backward.1.g_ref = bf16[1024,1280]{1,0:T(8,128)(2,1)} custom-call(s32[1,8]{1,0:T(1,128)} %len_ref.3, bf16[1024,1280]{1,0:T(8,128)(2,1)} %get-tuple-element.135.qkv_ref, bf16[1024,1024]{1,0:T(8,128)(2,1)} %get-tuple-element.136.ga_ref, bf16[1024,1024]{1,0:T(8,128)(2,1)} %get-tuple-element.87.att_ref, f32[1024,128]{1,0:T(8,128)} %get-tuple-element.137.lse_ref), custom_call_target="tpu_custom_call" | custom-call | flops 1342177280 | bytes 1245188 | tf_op jit(solution)/shard_map/attention_backward/pallas_call | solution.py:46
  326.9 8.8 %projection_grads.1 = (bf16[512,640]{1,0:T(8,128)(2,1)}, bf16[512,640]{1,0:T(8,128)(2,1)}, bf16[512,768]{1,0:T(8,128)(2,1)}, bf16[512,768]{1,0:T(8,128)(2,1)}) custom-call(s32[4]{0:T(128)} %pad_add_fusion.me_ref, bf16[1024,1024]{1,0:T(8,128)(2,1)} %x_ref.5, bf16[1024,1280]{1,0:T(8,128)(2,1)} %attention_backward.1.g_ref, ...), custom_call_target="tpu_custom_call" | custom-call | flops 335544320 | bytes 1318914 | tf_op jit(solution)/shard_map/projection_grads/pallas_call | solution.py:46
  349.7 8.7 %input_backward.1 = bf16[1024,1024]{1,0:T(8,128)(2,1)} custom-call(bf16[1024,1024]{1,0:T(8,128)(2,1)} %x_ref.5, bf16[1024,1280]{1,0:T(8,128)(2,1)} %attention_backward.1.g_ref, f32[1024,1024]{1,0:T(8,128)} %get-tuple-element.145.gh_ref, bf16[1024,1408]{1,0:T(8,128)(2,1)} %get-tuple-element.138.w_ref, f32[8,1024]{1,0:T(8,128)} %get-tuple-element.88.gains_ref), custom_call_target="tpu_custom_call" | custom-call | flops 335544320 | bytes 1740800 | tf_op jit(solution)/shard_map/input_backward/pallas_call | solution.py:46
  364.6 9.8 %down.3 = bf16[1024,1024]{1,0:T(8,128)(2,1)} custom-call(bf16[1024,512]{1,0:T(8,128)(2,1)} %get-tuple-element.146.refs_0_, bf16[1024,512]{1,0:T(8,128)(2,1)} %get-tuple-element.147.refs_1_, bf16[1024,512]{1,0:T(8,128)(2,1)} %get-tuple-element.148.refs_2_, bf16[1024,512]{1,0:T(8,128)(2,1)} %get-tuple-element.149.refs_3_, ...), custom_call_target="tpu_custom_call" | custom-call | flops 536870912 | bytes 2097152 | tf_op jit(solution)/shard_map/down/pallas_call | solution.py:46
  375.6 4.7 %collective-permute-done.50 = bf16[128,768]{1,0:T(8,128)(2,1)S(1)} collective-permute-done((bf16[128,768]{1,0:T(8,128)(2,1)S(1)}, bf16[128,768]{1,0:T(8,128)(2,1)S(1)}, u32[]{:S(2)}, u32[]{:S(2)}) %collective-permute-start.50) | collective-permute-done | bytes 196640 | tf_op jit(solution)/shard_map/ppermute | solution.py:701
  380.3 3.8 collective-permute-start.53
  (262 shorter events, 126.0 us)
Async XLA Ops:
  7.2 47.8 %all-gather.3.cloned.1.call-start = ((), (), s32[]{:S(2)}) async-start(), calls=%async_computation.2 | async-start | bytes 1310720 | tf_op jit(solution)/shard_map/all_gather | solution.py:776
  22.1 89.6 %all-gather.5.cloned.1.call-start = ((), (), s32[]{:S(2)}) async-start(), calls=%async_computation.3 | async-start | bytes 1310720 | tf_op jit(solution)/shard_map/all_gather | solution.py:776
  59.0 28.5 %collective-permute-start.13 = (bf16[128,2048]{1,0:T(8,128)(2,1)S(1)}, bf16[128,2048]{1,0:T(8,128)(2,1)}, u32[]{:S(2)}, u32[]{:S(2)}) collective-permute-start(bf16[128,2048]{1,0:T(8,128)(2,1)S(1)} %get-tuple-element.178), channel_id=1, source_target_pairs={{0,1},{1,0},{2,3},{3,2},{4,5},{5,4},{6,7},{7,6},{8,9},{9,8},{10,11... | collective-permute-start | bytes 1572872 | tf_op jit(solution)/shard_map/ppermute | solution.py:690
  78.8 225.3 %reduce-scatter.3.cloned.1.call-start = ((), (), s32[]{:S(2)}) async-start(), calls=%async_computation.4 | async-start | bytes 1310720 | tf_op jit(solution)/shard_map/reduce_scatter | solution.py:835
  87.5 47.7 %collective-permute-start.27 = (bf16[1024,1024]{1,0:T(8,128)(2,1)S(1)}, bf16[1024,1024]{1,0:T(8,128)(2,1)}, u32[]{:S(2)}, u32[]{:S(2)}) collective-permute-start(bf16[1024,1024]{1,0:T(8,128)(2,1)S(1)} %copy-done), channel_id=1, source_target_pairs={{0,8},{8,0},{1,9},{9,1},{2,10},{10,2},{3,11},{11,3},{4,12},{12,4},... | collective-permute-start | bytes 6291464 | tf_op jit(solution)/shard_map/ppermute | solution.py:748
  106.5 29.7 %collective-permute-start.26 = (bf16[1024,1024]{1,0:T(8,128)(2,1)}, bf16[1024,1024]{1,0:T(8,128)(2,1)}, u32[]{:S(2)}, u32[]{:S(2)}) collective-permute-start(bf16[1024,1024]{1,0:T(8,128)(2,1)} %get-tuple-element.110.refs_0_), channel_id=1, source_target_pairs={{0,8},{8,0},{1,9},{9,1},{2,10},{10,2},{3,11},{11,3},{4,12},{12,4},... | collective-permute-start | bytes 6291464 | tf_op jit(solution)/shard_map/ppermute | solution.py:748
  107.9 26.1 %collective-permute-start.25 = (bf16[256,2048]{1,0:T(8,128)(2,1)S(1)}, bf16[256,2048]{1,0:T(8,128)(2,1)}, u32[]{:S(2)}, u32[]{:S(2)}) collective-permute-start(bf16[256,2048]{1,0:T(8,128)(2,1)S(1)} %pad_maximum_fusion.refs_4_), channel_id=1, source_target_pairs={{0,16},{16,0},{1,17},{17,1},{2,18},{18,2},{3,19},{19,3},{4,20},{20... | collective-permute-start | bytes 3145736 | tf_op jit(solution)/shard_map/ppermute | solution.py:690
  110.5 25.6 %collective-permute-start.28 = (bf16[256,2048]{1,0:T(8,128)(2,1)}, bf16[256,2048]{1,0:T(8,128)(2,1)}, u32[]{:S(2)}, u32[]{:S(2)}) collective-permute-start(bf16[256,2048]{1,0:T(8,128)(2,1)} %pad_maximum_fusion.1.refs_4_), channel_id=1, source_target_pairs={{0,1},{1,0},{2,3},{3,2},{4,5},{5,4},{6,7},{7,6},{8,9},{9,8},{10,11... | collective-permute-start | bytes 3145736 | tf_op jit(solution)/shard_map/ppermute | solution.py:690
  113.8 39.9 %collective-permute-start.29 = (bf16[128,2048]{1,0:T(8,128)(2,1)}, bf16[128,2048]{1,0:T(8,128)(2,1)}, u32[]{:S(2)}, u32[]{:S(2)}) collective-permute-start(bf16[128,2048]{1,0:T(8,128)(2,1)} %get-tuple-element.177), channel_id=1, source_target_pairs={{0,16},{16,0},{1,17},{17,1},{2,18},{18,2},{3,19},{19,3},{4,20},{20... | collective-permute-start | bytes 1572872 | tf_op jit(solution)/shard_map/ppermute | solution.py:690
  134.0 22.1 %collective-permute-start.30 = (bf16[128,2048]{1,0:T(8,128)(2,1)S(1)}, bf16[128,2048]{1,0:T(8,128)(2,1)S(1)}, u32[]{:S(2)}, u32[]{:S(2)}) collective-permute-start(bf16[128,2048]{1,0:T(8,128)(2,1)S(1)} %get-tuple-element.176), channel_id=1, source_target_pairs={{0,1},{1,0},{2,3},{3,2},{4,5},{5,4},{6,7},{7,6},{8,9},{9,8},{10,11... | collective-permute-start | bytes 1572872 | tf_op jit(solution)/shard_map/ppermute | solution.py:690
  153.1 25.3 %collective-permute-start.33 = (bf16[256,2048]{1,0:T(8,128)(2,1)}, bf16[256,2048]{1,0:T(8,128)(2,1)S(1)}, u32[]{:S(2)}, u32[]{:S(2)}) collective-permute-start(bf16[256,2048]{1,0:T(8,128)(2,1)} %get-tuple-element.108), channel_id=1, source_target_pairs={{0,16},{16,0},{1,17},{17,1},{2,18},{18,2},{3,19},{19,3},{4,20},{20... | collective-permute-start | bytes 3145736 | tf_op jit(solution)/shard_map/ppermute | solution.py:701
  155.1 26.3 %collective-permute-start.32 = (bf16[256,2048]{1,0:T(8,128)(2,1)S(1)}, bf16[256,2048]{1,0:T(8,128)(2,1)}, u32[]{:S(2)}, u32[]{:S(2)}) collective-permute-start(bf16[256,2048]{1,0:T(8,128)(2,1)S(1)} %pad_maximum_fusion.2.refs_4_), channel_id=1, source_target_pairs={{0,1},{1,0},{2,3},{3,2},{4,5},{5,4},{6,7},{7,6},{8,9},{9,8},{10,11... | collective-permute-start | bytes 3145736 | tf_op jit(solution)/shard_map/ppermute | solution.py:690
  173.3 30.5 %collective-permute-start.31 = (bf16[256,2048]{1,0:T(8,128)(2,1)}, bf16[256,2048]{1,0:T(8,128)(2,1)}, u32[]{:S(2)}, u32[]{:S(2)}) collective-permute-start(bf16[256,2048]{1,0:T(8,128)(2,1)} %get-tuple-element.101), channel_id=1, source_target_pairs={{0,1},{1,0},{2,3},{3,2},{4,5},{5,4},{6,7},{7,6},{8,9},{9,8},{10,11... | collective-permute-start | bytes 3145736 | tf_op jit(solution)/shard_map/ppermute | solution.py:701
  175.7 38.5 %collective-permute-start.34 = (bf16[256,2048]{1,0:T(8,128)(2,1)S(1)}, bf16[256,2048]{1,0:T(8,128)(2,1)}, u32[]{:S(2)}, u32[]{:S(2)}) collective-permute-start(bf16[256,2048]{1,0:T(8,128)(2,1)S(1)} %pad_maximum_fusion.3.refs_4_), channel_id=1, source_target_pairs={{0,16},{16,0},{1,17},{17,1},{2,18},{18,2},{3,19},{19,3},{4,20},{20... | collective-permute-start | bytes 3145736 | tf_op jit(solution)/shard_map/ppermute | solution.py:690
  179.5 33.2 %collective-permute-start.37 = (bf16[128,2048]{1,0:T(8,128)(2,1)S(1)}, bf16[128,2048]{1,0:T(8,128)(2,1)}, u32[]{:S(2)}, u32[]{:S(2)}) collective-permute-start(bf16[128,2048]{1,0:T(8,128)(2,1)S(1)} %add_convert_fusion.10), channel_id=1, source_target_pairs={{0,1},{1,0},{2,3},{3,2},{4,5},{5,4},{6,7},{7,6},{8,9},{9,8},{10,11... | collective-permute-start | bytes 1572872 | tf_op jit(solution)/shard_map/ppermute | solution.py:701
  198.9 44.6 %collective-permute-start.36 = (bf16[256,2048]{1,0:T(8,128)(2,1)}, bf16[256,2048]{1,0:T(8,128)(2,1)}, u32[]{:S(2)}, u32[]{:S(2)}) collective-permute-start(bf16[256,2048]{1,0:T(8,128)(2,1)} %get-tuple-element.117), channel_id=1, source_target_pairs={{0,16},{16,0},{1,17},{17,1},{2,18},{18,2},{3,19},{19,3},{4,20},{20... | collective-permute-start | bytes 3145736 | tf_op jit(solution)/shard_map/ppermute | solution.py:701
  205.8 27.8 %collective-permute-start.38 = (bf16[128,2048]{1,0:T(8,128)(2,1)}, bf16[128,2048]{1,0:T(8,128)(2,1)S(1)}, u32[]{:S(2)}, u32[]{:S(2)}) collective-permute-start(bf16[128,2048]{1,0:T(8,128)(2,1)} %add_convert_fusion.12), channel_id=1, source_target_pairs={{0,16},{16,0},{1,17},{17,1},{2,18},{18,2},{3,19},{19,3},{4,20},{20... | collective-permute-start | bytes 1572872 | tf_op jit(solution)/shard_map/ppermute | solution.py:701
  231.5 26.5 %collective-permute-start.42 = (bf16[256,2048]{1,0:T(8,128)(2,1)}, bf16[256,2048]{1,0:T(8,128)(2,1)}, u32[]{:S(2)}, u32[]{:S(2)}) collective-permute-start(bf16[256,2048]{1,0:T(8,128)(2,1)} %get-tuple-element.133), channel_id=1, source_target_pairs={{0,1},{1,0},{2,3},{3,2},{4,5},{5,4},{6,7},{7,6},{8,9},{9,8},{10,11... | collective-permute-start | bytes 3145736 | tf_op jit(solution)/shard_map/ppermute | solution.py:701
  243.6 34.2 %collective-permute-start.35 = (bf16[1024,1024]{1,0:T(8,128)(2,1)}, bf16[1024,1024]{1,0:T(8,128)(2,1)S(1)}, u32[]{:S(2)}, u32[]{:S(2)}) collective-permute-start(bf16[1024,1024]{1,0:T(8,128)(2,1)} %hidden_backward.1), channel_id=1, source_target_pairs={{0,8},{8,0},{1,9},{9,1},{2,10},{10,2},{3,11},{11,3},{4,12},{12,4},... | collective-permute-start | bytes 6291464 | tf_op jit(solution)/shard_map/ppermute | solution.py:748
  247.3 88.9 %reduce-scatter.5.cloned.1.call-start = ((), (), s32[]{:S(2)}) async-start(), calls=%async_computation.5 | async-start | bytes 1310720 | tf_op jit(solution)/shard_map/reduce_scatter | solution.py:835
  302.5 23.4 %collective-permute-start.40 = (bf16[256,1024]{1,0:T(8,128)(2,1)S(1)}, bf16[256,1024]{1,0:T(8,128)(2,1)S(1)}, u32[]{:S(2)}, u32[]{:S(2)}) collective-permute-start(bf16[256,1024]{1,0:T(8,128)(2,1)S(1)} %get-tuple-element.169), channel_id=1, source_target_pairs={{0,16},{16,0},{1,17},{17,1},{2,18},{18,2},{3,19},{19,3},{4,20},{20... | collective-permute-start | bytes 1572872 | tf_op jit(solution)/shard_map/ppermute | solution.py:701
  304.1 60.5 %collective-permute-start.46 = (bf16[1024,1024]{1,0:T(8,128)(2,1)}, bf16[1024,1024]{1,0:T(8,128)(2,1)}, u32[]{:S(2)}, u32[]{:S(2)}) collective-permute-start(bf16[1024,1024]{1,0:T(8,128)(2,1)} %down.2), channel_id=1, source_target_pairs={{0,8},{8,0},{1,9},{9,1},{2,10},{10,2},{3,11},{11,3},{4,12},{12,4},... | collective-permute-start | bytes 6291464 | tf_op jit(solution)/shard_map/ppermute | solution.py:748
  348.9 25.4 %collective-permute-start.49 = (bf16[256,768]{1,0:T(8,128)(2,1)S(1)}, bf16[256,768]{1,0:T(8,128)(2,1)S(1)}, u32[]{:S(2)}, u32[]{:S(2)}) collective-permute-start(bf16[256,768]{1,0:T(8,128)(2,1)S(1)} %get-tuple-element.170), channel_id=1, source_target_pairs={{0,1},{1,0},{2,3},{3,2},{4,5},{5,4},{6,7},{7,6},{8,9},{9,8},{10,11... | collective-permute-start | bytes 1179656 | tf_op jit(solution)/shard_map/ppermute | solution.py:701
  361.8 22.6 %collective-permute-start.57 = (bf16[32,1024]{1,0:T(8,128)(2,1)S(1)}, bf16[32,1024]{1,0:T(8,128)(2,1)S(1)}, u32[]{:S(2)}, u32[]{:S(2)}) collective-permute-start(bf16[32,1024]{1,0:T(8,128)(2,1)S(1)} %get-tuple-element.191), channel_id=1, source_target_pairs={{0,6},{2,0},{4,2},{6,4},{1,7},{3,1},{5,3},{7,5},{8,14},{10,8},{12,... | collective-permute-start | bytes 196616 | tf_op jit(solution)/shard_map/ppermute | solution.py:701
  (74 other events, 939.8 us)
Sparse Core Ops, SparseCore 0:
  22.2 32.6 all-gather.2
  78.9 26.3 all-gather.4
  247.4 25.2 reduce-scatter.2
  299.1 25.7 reduce-scatter.4

commit v4 on v3

--- a/solution.py
+++ b/solution.py
@@ -14,6 +14,7 @@
 f32 = jnp.float32
 bf16 = jnp.bfloat16
 VM = pl.BlockSpec(memory_space=pltpu.VMEM)
+NEAR = pl.BlockSpec(memory_space=pltpu.VMEM)
 SM = pl.BlockSpec(memory_space=pltpu.SMEM)
 GELU_A = math.sqrt(2.0 / math.pi)
 GELU_B = GELU_A * 0.044715
@@ -23,6 +24,7 @@
 GROUP = 2
 VMEM_MIB = 60
 HINT = 8
+FFN_MIB = 44
 
 
 def nn(a, b):
@@ -43,10 +45,16 @@
 
 def call(kernel, outs, args, flops, exps=0, scratch=(), vmem=48, name=None, in_specs=None, **kw):
     moved = sum(math.prod(a.shape) * a.dtype.itemsize for a in (*args, *outs))
+    specs = in_specs or [VM] * len(args)
+    args = [
+        a if s is SM else pltpu.with_memory_space_constraint(a, pltpu.VMEM if s is NEAR else pltpu.HBM)
+        for a, s in zip(args, specs)
+    ]
+    outs = [pltpu.HBM(a.shape, a.dtype) for a in outs]
     return pl.pallas_call(
         kernel,
         out_shape=outs,
-        in_specs=in_specs or [VM] * len(args),
+        in_specs=specs,
         out_specs=kw.pop("out_specs", [VM] * len(outs)),
         scratch_shapes=list(scratch),
         compiler_params=pltpu.CompilerParams(vmem_limit_bytes=vmem * MIB),
@@ -323,18 +331,18 @@
     count, lines = seconds(sizes, order), firsts(sizes, order)
     take = lambda n: [refs.pop(0) for _ in range(n)]
     refs = list(refs)
-    ins = take(4 + count)
+    near, ins = take(4), take(count)
     seen, whole, outs = take(4), take(2), take(lines)
-    held_in = take(4 + count)
+    pieces = take(count)
     acts, (up_ref, down_ref), (gu, gd), staged = take(4), take(2), take(2), take(lines)
     in_sem, out_sem = refs
     part, model = down_ref.shape
     shard = part // math.prod(sizes)
     tile = min(256, part)
 
-    loads = [pltpu.make_async_copy(a, b, in_sem.at[n]) for n, (a, b) in enumerate(zip(ins, held_in))]
-    for n in (*range(4, 4 + count), 0, 2, 1, 3):
-        loads[n].start()
+    loads = [pltpu.make_async_copy(a, b, in_sem.at[n]) for n, (a, b) in enumerate(zip(ins, pieces))]
+    for load in loads:
+        load.start()
     started = []
 
     def store(src, dst):
@@ -342,9 +350,8 @@
         copy.start()
         started.append(copy)
 
-    pieces = held_in[4:]
-    for n in range(count):
-        loads[4 + n].wait()
+    for load in loads:
+        load.wait()
     for place, (first, second) in blocks_of(sizes, order):
         x, f = chip_at(sizes, order, me_ref, *place, -1)
         row = (first * sizes[1] + place[2]) * shard
@@ -352,25 +359,22 @@
         for core in range(2):
             up_ref[row_of(sizes, x, f, core, shard), :] = pieces[second][at, core * part : (core + 1) * part]
         down_ref[half_row_of(sizes, x, f, shard), :] = pieces[second][at, 2 * part :]
-    store(up_ref, whole[0])
-    store(down_ref, whole[1])
-
-    nt_o, nt_p, dy_o, dy_p = held_in[:4]
+
+    nt_o, nt_p, dy_o, dy_p = near
     act_o, act_p, gi_o, gi_p = acts
     tiles = [slice(j * tile, (j + 1) * tile) for j in range(part // tile)]
     for j, cols in enumerate(tiles):
         for own, (n_ref, y_ref, a_ref, i_ref) in enumerate(((nt_o, dy_o, act_o, gi_o), (nt_p, dy_p, act_p, gi_p))):
-            if j == 0:
-                loads[own].wait()
             inner = nn(n_ref[...], up_ref[:, cols])
-            if j == 0:
-                loads[2 + own].wait()
             ga = nt(y_ref[...], down_ref[cols, :])
             a, slope = gelu_both(inner)
             a_ref[:, cols] = a.astype(bf16)
             i_ref[:, cols] = (ga * slope).astype(bf16)
-    for n, a in enumerate(acts):
-        store(a, seen[n])
+            if j == len(tiles) - 1:
+                store(a_ref, seen[own])
+                store(i_ref, seen[2 + own])
+    store(up_ref, whole[0])
+    store(down_ref, whole[1])
     for cols in tiles:
         gu[:, cols] = (tn(nt_o[...], gi_o[:, cols]) + tn(nt_p[...], gi_p[:, cols])).astype(bf16)
     for cols in tiles:
@@ -399,18 +403,18 @@
     grads = [shape((part // lines, 2 * model), bf16)] * lines
     ins = (nt_o, nt_p, dy_o, dy_p, *pieces)
     outs = [shape((rows, part), bf16)] * 4 + [up, down] + grads
-    far = pl.BlockSpec(memory_space=pl.ANY)
+    far = pl.BlockSpec(memory_space=pltpu.HBM)
     outs = call(
         functools.partial(ffn_kernel, sizes, order),
         outs,
         (me, *ins),
         16 * rows * model * part,
         2 * rows * part,
-        [pltpu.VMEM(a.shape, bf16) for a in (*ins, *outs[:4], up, down, up, down, *grads)]
-        + [pltpu.SemaphoreType.DMA((len(ins),)), pltpu.SemaphoreType.DMA((len(outs),))],
-        VMEM_MIB,
+        [pltpu.VMEM(a.shape, bf16) for a in (*pieces, *outs[:4], up, down, up, down, *grads)]
+        + [pltpu.SemaphoreType.DMA((len(pieces),)), pltpu.SemaphoreType.DMA((len(outs),))],
+        FFN_MIB,
         "ffn",
-        [SM] + [far] * len(ins),
+        [SM] + [NEAR] * 4 + [far] * len(pieces),
         out_specs=[far] * len(outs),
     )
     return outs[:4], outs[4], outs[5], outs[6:]
@@ -727,6 +731,9 @@
     def reduce_one(self, parts):
         self.got = [parts[0], *send_on(parts, *self.axes[0])]
 
+    def hold(self, *first):
+        self.got[1:] = [after(p, *first) for p in self.got[1:]]
+
     def reduce_two(self):
         n = self.axes[1][1]
         parts = [add([cut(p, s, n) for p in self.got]).astype(bf16) for s in range(n)]
@@ -772,35 +779,39 @@
     down_rows = down_weight.reshape(chunks, shard, model)
     f_along = []
     for first in range(0, chunks, 2):
-        mine = jnp.concatenate([p for c in (first, first + 1) for p in (up_pair[:, c], down_rows[c])], axis=1)
+        mine = [p for c in (first, first + 1) for p in (up_pair[:, c], down_rows[c])]
+        mine = jnp.concatenate(mine + ([] if first else [out_weight]), axis=1)
         f_along.append(lax.all_gather(after(mine, *w_along[1:]), "f1", axis=0, tiled=True))
 
+    dy_p = swap(after(cotangent, *w_along[1:]))
     w_block = jnp.concatenate(w_along, axis=0)
     w_hops = [Hops(sizes, order) for order in w_orders]
     lines = w_hops[0].gather_one(w_block[:, :first_share]) + w_hops[1].gather_one(w_block[:, first_share:])
-    wo_along = spread(after(out_weight, *lines), "f1", na)
     w_pieces = []
     for h in w_hops:
         p = h.gather_two()
         w_pieces += p + [swap(a) for a in p]
-    wo_orders = (x_then, b_then)
-    wo_block = jnp.concatenate(wo_along, axis=0)
+    wo_orders, wo_back = ((True, False), (False, False)), (x_then,)
+    hops = [Hops(sizes, order) for order in by_index]
+    f_lines = lambda c: hops[c].gather_one(cut_columns(f_along[c // 2], c % 2, 2))
+
+    w, qkv, gains = project(sizes, w_orders, columns, me, tokens, w_pieces)
+    f_along[0] = after(f_along[0], qkv)
+    wo_block, f_along[0] = f_along[0][:, 2 * wide :], f_along[0][:, : 2 * wide]
     wo_hops = [Hops(sizes, order) for order in wo_orders]
     for n, h in enumerate(wo_hops):
         h.gather_one(cut_columns(wo_block, n, 2))
-    wo_pieces = []
+    lines = [p for c in (0, 1) for p in f_lines(c)]
+    att, lse = attention_forward(doc_lengths, after(qkv, dy_p))
     for h in wo_hops:
-        p = h.gather_two()
-        wo_pieces += p + [swap(a) for a in p]
-    hops = [Hops(sizes, order) for order in by_index]
-    f_lines = lambda c: hops[c].gather_one(cut_columns(f_along[c // 2], c % 2, 2))
-
-    w, qkv, gains = project(sizes, w_orders, columns, me, tokens, w_pieces)
-    lines = [p for c in (0, 1) for p in f_lines(c)]
-    att, lse = attention_forward(doc_lengths, after(qkv, *lines))
+        h.lines[1:] = [after(p, att) for p in h.lines[1:]]
+    wo_pieces = [h.gather_two() for h in wo_hops]
+    wo_pieces = [a for p in wo_pieces for a in (*p, *[swap(b) for b in p])]
+    for c in (0, 1):
+        hops[c].lines[1:] = [after(p, att, *[h.pieces[1] for h in wo_hops]) for p in hops[c].lines[1:]]
     pieces = {c: hops[c].gather_two() for c in (0, 1)}
-    dy_p = swap(after(cotangent, qkv))
     wo, hidden, nt_o = branch(sizes, wo_orders, me, tokens, att, gains, wo_pieces)
+    nt_o = after(nt_o, *pieces[0], *pieces[1], f_along[1])
     nt_p = swap(nt_o)
 
     acts_o, acts_p, gis_o, gis_p, ups, downs = [], [], [], [], [], []
@@ -811,63 +822,76 @@
             kept.append(a)
         ups.append(up_c)
         downs.append(down_c)
-        hops[c].reduce_one(grads)
+        return grads
 
     def sum_cores(keep, come, order):
         n = firsts(sizes, order)
         return [add([cut(a, s, n) for a in (keep, come)]).astype(bf16) for s in range(n)]
 
-    f_along[1] = after(f_along[1], att)
+    f_along[1] = after(f_along[1], nt_p)
     lines = [p for c in (2, 3) for p in f_lines(c)]
-    run_ffn(0, *pieces[1])
-    run_ffn(1, *lines, ups[0])
+    grads = [run_ffn(0)]
+    grads.append(run_ffn(1, *lines, ups[0]))
     for c in (2, 3):
+        hops[c].lines[1:] = [after(p, ups[0]) for p in hops[c].lines[1:]]
         pieces[c] = hops[c].gather_two()
-    run_ffn(2, ups[1])
-    ready = hops[0].reduce_two()
-    run_ffn(3, *ready, ups[2])
-    ready = hops[1].reduce_two()
+    late = [*pieces[2], *pieces[3], ups[1]]
+    grads.append(run_ffn(2, *late))
+    for c in (0, 1):
+        hops[c].reduce_one([after(g, *late) for g in grads[c]])
+    grads.append(run_ffn(3, ups[2]))
+    for c in (0, 1):
+        hops[c].hold(ups[3])
+    ready = [p for c in (0, 1) for p in hops[c].reduce_two()]
+    for c in (2, 3):
+        hops[c].reduce_one([after(g, *ready) for g in grads[c]])
     gn_p = hidden_backward([after(gis_p[0], *ready), *gis_p[1:]], ups)
     gn_r = swap(gn_p)
-    ready = hops[2].reduce_two()
-    out_p = down([after(acts_p[0], gn_p, *ready), *acts_p[1:]], downs, [])
-    out_r = swap(out_p)
+    out_p = down([after(acts_p[0], gn_p), *acts_p[1:]], downs, [])
     last = lambda a: lax.psum_scatter(a, "f1", scatter_dimension=0, tiled=True)
+    for c in (0, 1):
+        hops[c].hold(out_p)
     pair = jnp.concatenate([hops[c].sum_two()[0] for c in (0, 1)], axis=1)
     sums = [last(pair)]
     gh, gatt, gg, *halves = branch_backward(
-        sizes, wo_orders[:1], me, hidden, gn_r, cotangent, att, gains, wo, [after(gis_o[0], out_p, pair), *gis_o[1:]], ups
+        sizes, wo_back, me, hidden, gn_r, cotangent, att, gains, wo, [after(gis_o[0], pair), *gis_o[1:]], ups
     )
-    come = swap(halves[1])
-    ready = hops[3].reduce_two()
+    for c in (2, 3):
+        hops[c].hold(gatt)
+    ready = [p for c in (2, 3) for p in hops[c].reduce_two()]
+    come = swap(after(halves[1], *ready))
     wo_reduce = Hops(sizes, x_then)
-    ready += sum_cores(halves[0], come, x_then)
-    wo_reduce.reduce_one(ready[-firsts(sizes, x_then) :])
+    ready = sum_cores(halves[0], come, x_then)
+    wo_reduce.reduce_one(ready)
     g = attention_backward(doc_lengths, after(qkv, *ready), gatt, att, lse)
-    ready = wo_reduce.reduce_two()
+    for h in (hops[2], hops[3], wo_reduce):
+        h.hold(g)
     pair = jnp.concatenate([hops[c].sum_two()[0] for c in (2, 3)], axis=1)
     sums.append(last(pair))
+    ready = wo_reduce.reduce_two()
+    out_r = swap(after(out_p, g))
     halves = projection_grads(sizes, w_orders, w_widths, me, after(tokens, *ready, pair), g, w, gains, gg)
-    come = [swap(h) for h in halves[1::2]]
-    wo_parts = wo_reduce.sum_two(na)
-    wo_got = send_on(wo_parts, "f1", na)
+    wo_reduce.hold(halves[0])
+    wo_last = wo_reduce.sum_two()[0]
+    come = [swap(after(h, wo_last)) for h in halves[1::2]]
     ready = [sum_cores(k, c, o) for k, c, o in zip(halves[0::2], come, w_orders)]
     w_reduce = [Hops(sizes, order) for order in w_orders]
     for h, r in zip(w_reduce, ready):
         h.reduce_one(r)
     ready = [r for rs in ready for r in rs]
     grad_tokens = input_backward(after(tokens, *ready), g, gh, w, gains)
+    ready = []
     for h in w_reduce:
-        h.got = [after(p, grad_tokens) for p in h.got]
-        h.reduce_two()
-    grad_out = add([wo_parts[0], *wo_got])
-    output = down([after(acts_o[0], grad_tokens), *acts_o[1:]], downs, [hidden, out_r])
+        h.hold(grad_tokens)
+        ready += h.reduce_two()
+    output = down([after(acts_o[0], *ready), *acts_o[1:]], downs, [hidden, out_r])
     for h in w_reduce:
-        h.got = [after(p, output) for p in h.got]
-    w_parts = [jnp.concatenate(p, axis=1) for p in zip(*[h.sum_two(na) for h in w_reduce])]
-    gw = add([w_parts[0], *send_on(w_parts, "f1", na)])
-
-    sums = jnp.stack([s.reshape(shard, 2, wide) for s in sums], axis=1).reshape(shard, chunks, wide)
+        h.hold(output)
+    w_parts = [jnp.concatenate([*p, cut(wo_last, n, na)], axis=1) for n, p in enumerate(zip(*[h.sum_two(na) for h in w_reduce]))]
+    got = send_on(w_parts, "f1", na)
+
+    sums = [after(a, *w_parts) for a in sums]
+    sums = jnp.stack([a.reshape(shard, 2, wide) for a in sums], axis=1).reshape(shard, chunks, wide)
     grad_down = sums[:, :, model:].transpose(1, 0, 2).reshape(chunks * shard, model).astype(f32)
     g_up = sums[:, :, :model].reshape(shard, chunks, 2, part)
     keep = jnp.where(core == 0, g_up[:, :, 0], g_up[:, :, 1])
@@ -875,6 +899,8 @@
     grad_up = jnp.where(core == 0, jnp.stack([keep, come], 0), jnp.stack([come, keep], 0))
     grad_up = grad_up.reshape(2, shard, chunks, nx, fsdp, shard).transpose(1, 3, 0, 4, 2, 5)
     grad_up = grad_up.reshape(shard, ff).astype(f32)
+    gw = add([w_parts[0], *got])
+    grad_out = gw[:, columns:]
 
     qw = query_weight.shape[1]
     return (

time: 405 us -> 361 us (0.89)
  waiting for transfers between devices: 95.3 us -> 56.3 us
  starting transfers between devices: 57.8 us -> 49.6 us
    ppermute x20 -> x17, waiting for transfers between devices: 35.8 us -> 7.81 us  [send_on(): lax.ppermute(parts[s], axis, [(i, (i + s) % n) for i in range(n)])]
    ppermute x22 -> x19, waiting for transfers between devices: 55.7 us -> 31.9 us  [spread(): lax.ppermute(a, axis, [(i, (i + s) % n) for i in range(n)])]
    ppermute x17, waiting for transfers between devices: 2.77 us -> 10.8 us  [on_device(): swap = lambda a: lax.ppermute(a, 'core', [(0, 1), (1, 0)])]
    ppermute x22 -> x19, starting transfers between devices: 30.1 us -> 25.3 us  [spread(): lax.ppermute(a, axis, [(i, (i + s) % n) for i in range(n)])]
    all_gather x2, waiting for transfers between devices: 0.97 us -> 5.63 us  [on_device(): lax.all_gather(after(mine, *w_along[1:]), 'f1', axis=0, tiled=True)]
    ppermute x20 -> x17, starting transfers between devices: 24 us -> 21.3 us  [send_on(): lax.ppermute(parts[s], axis, [(i, (i + s) % n) for i in range(n)])]
  transfers between devices with their start and end apart: 63 -> 57, of which waited for: 23 -> 20; matrix products, arithmetic and copies ran while one was open for 11% -> 11% of each run, Pallas kernels for 45% -> 47%
where the time goes in v4:
time: 361 us; the launch traced here: 356 us
  Pallas kernels  177 us (49%)
  waiting for transfers between devices  56.3 us (16%)
  starting transfers between devices  49.6 us (14%)
  other arithmetic  35.8 us (10%)
  local copies, waits for them, and re-layouts  22.7 us (6%)
  between operations  14.9 us (4%)
    pallas_call x14, Pallas kernels, call(): pl.pallas_call(kernel, out_shape=outs, in_specs=specs, out_specs=kw.pop('...  177 us
    ppermute x19, waiting for transfers between devices, spread(): lax.ppermute(a, axis, [(i, (i + s) % n) for i in range(n)])  31.9 us
    ppermute x19, starting transfers between devices, spread(): lax.ppermute(a, axis, [(i, (i + s) % n) for i in range(n)])  25.3 us
    ppermute x17, starting transfers between devices, send_on(): lax.ppermute(parts[s], axis, [(i, (i + s) % n) for i in range(n)])  21.3 us
    ppermute x17, waiting for transfers between devices, on_device(): swap = lambda a: lax.ppermute(a, 'core', [(0, 1), (1, 0)])  10.8 us
    convert_element_type x7, other arithmetic, reduce_two(): add([cut(p, s, n) for p in self.got]).astype(bf16)  10.7 us
    ppermute x17, waiting for transfers between devices, send_on(): lax.ppermute(parts[s], axis, [(i, (i + s) % n) for i in range(n)])  7.81 us
  transfers between devices with their start and end apart: 57, of which 20 were waited for; matrix products, arithmetic and copies ran while one was open for 11% of the time, Pallas kernels for 47%

profile of v4, /device:TPU:0, one launch (start us, length us, event | category | flops | bytes accessed | tf_op | source)
XLA Modules:
  0.0 356.3 jit_solution(7339063636351555586)
XLA Ops:
  11.0 4.6 %collective-permute-start.2 = (bf16[32,1408]{1,0:T(8,128)(2,1)}, bf16[32,1408]{1,0:T(8,128)(2,1)}, u32[]{:S(2)}, u32[]{:S(2)}) collective-permute-start(bf16[32,1408]{1,0:T(8,128)(2,1)} %pad_maximum_fusion.23), channel_id=1, source_target_pairs={{0,6},{2,0},{4,2},{6,4},{1,7},{3,1},{5,3},{7,5},{8,14},{10,8},{12,... | collective-permute-start | bytes 270344 | tf_op jit(solution)/shard_map/ppermute | solution.py:694
  20.4 4.6 %collective-permute-done.1 = bf16[32,1408]{1,0:T(8,128)(2,1)} collective-permute-done((bf16[32,1408]{1,0:T(8,128)(2,1)}, bf16[32,1408]{1,0:T(8,128)(2,1)}, u32[]{:S(2)}, u32[]{:S(2)}) %collective-permute-start.1) | collective-permute-done | bytes 90144 | tf_op jit(solution)/shard_map/ppermute | solution.py:694
  30.3 3.4 collective-permute-done.7
  36.9 7.6 %collective-permute-done.8.refs_5_ = bf16[256,768]{1,0:T(8,128)(2,1)S(1)} collective-permute-done((bf16[256,768]{1,0:T(8,128)(2,1)S(1)}, bf16[256,768]{1,0:T(8,128)(2,1)S(1)}, u32[]{:S(2)}, u32[]{:S(2)}) %collective-permute-start.8) | collective-permute-done | bytes 393248 | tf_op jit(solution)/shard_map/ppermute | solution.py:694
  47.5 7.4 %project.1 = (bf16[1024,1408]{1,0:T(8,128)(2,1)}, bf16[1024,1280]{1,0:T(8,128)(2,1)}, f32[8,1024]{1,0:T(8,128)}) custom-call(s32[4]{0:T(128)} %pad_add_fusion.me_ref, bf16[1024,1024]{1,0:T(8,128)(2,1)} %x_ref.5, bf16[256,640]{1,0:T(8,128)(2,1)} %copy-done.12, bf16[256,640]{1,0:T(8,128)(2,1)} %collective-permute-done.4.refs_1_, bf16[256,640]{1,0:T(8,128)(2,1)} %copy-done.24, ...), custom_call_target="tpu_custom_call" | custom-call | flops 335544320 | bytes 1314818 | tf_op jit(solution)/shard_map/project/pallas_call | solution.py:54
  63.9 10.5 %attention_forward.1 = (bf16[1024,1024]{1,0:T(8,128)(2,1)}, f32[1024,128]{1,0:T(8,128)}) custom-call(s32[1,8]{1,0:T(1,128)} %len_ref.3, bf16[1024,1280]{1,0:T(8,128)(2,1)} %get-tuple-element.182.qkv_ref), custom_call_target="tpu_custom_call" | custom-call | flops 536870912 | bytes 655364 | tf_op jit(solution)/shard_map/attention_forward/pallas_call | solution.py:54
  81.6 2.9 collective-permute-done.14.refs_1_
  95.6 8.0 %branch.1 = (bf16[1024,1024]{1,0:T(8,128)(2,1)}, f32[1024,1024]{1,0:T(8,128)}, bf16[1024,1024]{1,0:T(8,128)(2,1)}) custom-call(s32[4]{0:T(128)} %pad_add_fusion.me_ref, bf16[1024,1024]{1,0:T(8,128)(2,1)} %x_ref.5, bf16[1024,1024]{1,0:T(8,128)(2,1)} %get-tuple-element.113.att_ref, f32[8,1024]{1,0:T(8,128)} %get-tuple-element.114.gains_ref, ...), custom_call_target="tpu_custom_call" | custom-call | flops 268435456 | bytes 1839106 | tf_op jit(solution)/shard_map/branch/pallas_call | solution.py:54
  103.7 3.1 all-gather.5.cloned.1.call-done
  106.8 5.1 %collective-permute-done.22.refs_5_ = bf16[256,2048]{1,0:T(8,128)(2,1)} collective-permute-done((bf16[256,2048]{1,0:T(8,128)(2,1)}, bf16[256,2048]{1,0:T(8,128)(2,1)}, u32[]{:S(2)}, u32[]{:S(2)}) %collective-permute-start.22) | collective-permute-done | bytes 1048608 | tf_op jit(solution)/shard_map/ppermute | solution.py:694
  111.9 4.4 %collective-permute-done.25.refs_1_ = bf16[1024,1024]{1,0:T(8,128)(2,1)S(1)} collective-permute-done((bf16[1024,1024]{1,0:T(8,128)(2,1)}, bf16[1024,1024]{1,0:T(8,128)(2,1)S(1)}, u32[]{:S(2)}, u32[]{:S(2)}) %collective-permute-start.25) | collective-permute-done | bytes 2097184 | tf_op jit(solution)/shard_map/ppermute | solution.py:755
  120.6 16.5 %ffn.4 = (bf16[1024,512]{1,0:T(8,128)(2,1)}, bf16[1024,512]{1,0:T(8,128)(2,1)}, bf16[1024,512]{1,0:T(8,128)(2,1)}, bf16[1024,512]{1,0:T(8,128)(2,1)}, bf16[1024,...) custom-call(s32[4]{0:T(128)S(1)} %copy-done.2, ...), custom_call_target="tpu_custom_call" | custom-call | flops 1073741824 | bytes 2359298 | tf_op jit(solution)/shard_map/ffn/pallas_call | solution.py:54
  138.5 16.8 %ffn.5 = (bf16[1024,512]{1,0:T(8,128)(2,1)}, bf16[1024,512]{1,0:T(8,128)(2,1)}, bf16[1024,512]{1,0:T(8,128)(2,1)}, bf16[1024,512]{1,0:T(8,128)(2,1)}, bf16[1024,...) custom-call(s32[4]{0:T(128)S(1)} %copy-done.2, ...), custom_call_target="tpu_custom_call" | custom-call | flops 1073741824 | bytes 2359298 | tf_op jit(solution)/shard_map/ffn/pallas_call | solution.py:54
  155.3 6.8 %collective-permute-done.27.refs_5_ = bf16[256,2048]{1,0:T(8,128)(2,1)S(1)} collective-permute-done((bf16[256,2048]{1,0:T(8,128)(2,1)S(1)}, bf16[256,2048]{1,0:T(8,128)(2,1)S(1)}, u32[]{:S(2)}, u32[]{:S(2)}) %collective-permute-start.27) | collective-permute-done | bytes 1048608 | tf_op jit(solution)/shard_map/ppermute | solution.py:694
  164.4 16.8 %ffn.6 = (bf16[1024,512]{1,0:T(8,128)(2,1)}, bf16[1024,512]{1,0:T(8,128)(2,1)}, bf16[1024,512]{1,0:T(8,128)(2,1)}, bf16[1024,512]{1,0:T(8,128)(2,1)}, bf16[1024,...) custom-call(s32[4]{0:T(128)S(1)} %copy-done.2, ...), custom_call_target="tpu_custom_call" | custom-call | flops 1073741824 | bytes 2359298 | tf_op jit(solution)/shard_map/ffn/pallas_call | solution.py:54
  181.2 17.0 %ffn.7 = (bf16[1024,512]{1,0:T(8,128)(2,1)}, bf16[1024,512]{1,0:T(8,128)(2,1)}, bf16[1024,512]{1,0:T(8,128)(2,1)}, bf16[1024,512]{1,0:T(8,128)(2,1)}, bf16[1024,...) custom-call(s32[4]{0:T(128)S(1)} %copy-done.2, ...), custom_call_target="tpu_custom_call" | custom-call | flops 1073741824 | bytes 2359298 | tf_op jit(solution)/shard_map/ffn/pallas_call | solution.py:54
  200.7 8.7 %hidden_backward.1 = bf16[1024,1024]{1,0:T(8,128)(2,1)} custom-call(bf16[1024,512]{1,0:T(8,128)(2,1)} %get-tuple-element.147.refs_0_, bf16[1024,512]{1,0:T(8,128)(2,1)} %get-tuple-element.148.refs_1_, bf16[1024,512]{1,0:T(8,128)(2,1)} %get-tuple-element.149.refs_2_, bf16[1024,512]{1,0:T(8,128)(2,1)} %get-tuple-element.150.refs_3_, ...), custom_call_target="tpu_custom_call" | custom-call | flops 536870912 | bytes 1310720 | tf_op jit(solution)/shard_map/hidden_backward/pallas_call | solution.py:54
  213.5 8.6 %down.2 = bf16[1024,1024]{1,0:T(8,128)(2,1)} custom-call(bf16[1024,512]{1,0:T(8,128)(2,1)} %get-tuple-element.154.refs_0_, bf16[1024,512]{1,0:T(8,128)(2,1)} %get-tuple-element.155.refs_1_, bf16[1024,512]{1,0:T(8,128)(2,1)} %get-tuple-element.156.refs_2_, bf16[1024,512]{1,0:T(8,128)(2,1)} %get-tuple-element.157.refs_3_, ...), custom_call_target="tpu_custom_call" | custom-call | flops 536870912 | bytes 1310720 | tf_op jit(solution)/shard_map/down/pallas_call | solution.py:54
  228.7 18.2 %branch_backward.1 = (f32[1024,1024]{1,0:T(8,128)}, bf16[1024,1024]{1,0:T(8,128)(2,1)}, f32[8,1024]{1,0:T(8,128)}, bf16[512,1024]{1,0:T(8,128)(2,1)}, bf16[512,1024]{1,0:T(8,128)(2,1)}) custom-call(s32[4]{0:T(128)} %pad_add_fusion.me_ref, f32[1024,1024]{1,0:T(8,128)} %get-tuple-element.125.hidden_ref.refs_8_, bf16[1024,1024]{1,0:T(8,128)(2,1)} %copy-done.7, ...), custom_call_target="tpu_custom_call" | custom-call | flops 1073741824 | bytes 3678210 | tf_op jit(solution)/shard_map/branch_backward/pallas_call | solution.py:54
  257.7 21.0 %attention_backward.1.g_ref = bf16[1024,1280]{1,0:T(8,128)(2,1)} custom-call(s32[1,8]{1,0:T(1,128)} %len_ref.3, bf16[1024,1280]{1,0:T(8,128)(2,1)} %get-tuple-element.182.qkv_ref, bf16[1024,1024]{1,0:T(8,128)(2,1)} %get-tuple-element.174.ga_ref, bf16[1024,1024]{1,0:T(8,128)(2,1)} %get-tuple-element.113.att_ref, f32[1024,128]{1,0:T(8,128)} %get-tuple-element.183.lse_ref), custom_call_target="tpu_custom_call" | custom-call | flops 1342177280 | bytes 1245188 | tf_op jit(solution)/shard_map/attention_backward/pallas_call | solution.py:54
  285.7 8.8 %projection_grads.1 = (bf16[512,640]{1,0:T(8,128)(2,1)}, bf16[512,640]{1,0:T(8,128)(2,1)}, bf16[512,768]{1,0:T(8,128)(2,1)}, bf16[512,768]{1,0:T(8,128)(2,1)}) custom-call(s32[4]{0:T(128)} %pad_add_fusion.me_ref, bf16[1024,1024]{1,0:T(8,128)(2,1)} %x_ref.5, bf16[1024,1280]{1,0:T(8,128)(2,1)} %attention_backward.1.g_ref, ...), custom_call_target="tpu_custom_call" | custom-call | flops 335544320 | bytes 1318914 | tf_op jit(solution)/shard_map/projection_grads/pallas_call | solution.py:54
  304.5 9.0 %input_backward.1 = bf16[1024,1024]{1,0:T(8,128)(2,1)} custom-call(bf16[1024,1024]{1,0:T(8,128)(2,1)} %x_ref.5, bf16[1024,1280]{1,0:T(8,128)(2,1)} %attention_backward.1.g_ref, f32[1024,1024]{1,0:T(8,128)} %get-tuple-element.198.gh_ref, bf16[1024,1408]{1,0:T(8,128)(2,1)} %get-tuple-element.188.w_ref, f32[8,1024]{1,0:T(8,128)} %get-tuple-element.114.gains_ref), custom_call_target="tpu_custom_call" | custom-call | flops 335544320 | bytes 1740800 | tf_op jit(solution)/shard_map/input_backward/pallas_call | solution.py:54
  317.4 9.8 %down.3 = bf16[1024,1024]{1,0:T(8,128)(2,1)} custom-call(bf16[1024,512]{1,0:T(8,128)(2,1)} %get-tuple-element.201.refs_0_, bf16[1024,512]{1,0:T(8,128)(2,1)} %get-tuple-element.202.refs_1_, bf16[1024,512]{1,0:T(8,128)(2,1)} %get-tuple-element.203.refs_2_, bf16[1024,512]{1,0:T(8,128)(2,1)} %get-tuple-element.204.refs_3_, ...), custom_call_target="tpu_custom_call" | custom-call | flops 536870912 | bytes 2097152 | tf_op jit(solution)/shard_map/down/pallas_call | solution.py:54
  342.5 4.9 %collective-permute-done.50 = bf16[32,2432]{1,0:T(8,128)(2,1)S(1)} collective-permute-done((bf16[32,2432]{1,0:T(8,128)(2,1)S(1)}, bf16[32,2432]{1,0:T(8,128)(2,1)S(1)}, u32[]{:S(2)}, u32[]{:S(2)}) %collective-permute-start.50) | collective-permute-done | bytes 155680 | tf_op jit(solution)/shard_map/ppermute | solution.py:705
  (254 shorter events, 117.0 us)
Async XLA Ops:
  7.2 50.2 %all-gather.3.cloned.1.call-start = ((), (), s32[]{:S(2)}) async-start(), calls=%async_computation.2 | async-start | bytes 1638400 | tf_op jit(solution)/shard_map/all_gather | solution.py:784
  25.1 81.7 %all-gather.5.cloned.1.call-start = ((), (), s32[]{:S(2)}) async-start(), calls=%async_computation.3 | async-start | bytes 1310720 | tf_op jit(solution)/shard_map/all_gather | solution.py:784
  25.3 38.6 %collective-permute-start.11 = (bf16[1024,1024]{1,0:T(8,128)(2,1)S(1)}, bf16[1024,1024]{1,0:T(8,128)(2,1)}, u32[]{:S(2)}, u32[]{:S(2)}) collective-permute-start(bf16[1024,1024]{1,0:T(8,128)(2,1)S(1)} %copy-done), channel_id=1, source_target_pairs={{0,8},{8,0},{1,9},{9,1},{2,10},{10,2},{3,11},{11,3},{4,12},{12,4},... | collective-permute-start | bytes 6291464 | tf_op jit(solution)/shard_map/ppermute | solution.py:755
  58.4 16.0 %collective-permute-start.17 = (bf16[128,512]{1,0:T(8,128)(2,1)S(1)}, bf16[128,512]{1,0:T(8,128)(2,1)S(1)}, u32[]{:S(2)}, u32[]{:S(2)}) collective-permute-start(bf16[128,512]{1,0:T(8,128)(2,1)S(1)} %get-tuple-element.228), channel_id=1, source_target_pairs={{0,1},{1,0},{2,3},{3,2},{4,5},{5,4},{6,7},{7,6},{8,9},{9,8},{10,11... | collective-permute-start | bytes 393224 | tf_op jit(solution)/shard_map/ppermute | solution.py:694
  62.8 22.9 %collective-permute-start.23 = (bf16[128,2048]{1,0:T(8,128)(2,1)S(1)}, bf16[128,2048]{1,0:T(8,128)(2,1)}, u32[]{:S(2)}, u32[]{:S(2)}) collective-permute-start(bf16[128,2048]{1,0:T(8,128)(2,1)S(1)} %get-tuple-element.226), channel_id=1, source_target_pairs={{0,1},{1,0},{2,3},{3,2},{4,5},{5,4},{6,7},{7,6},{8,9},{9,8},{10,11... | collective-permute-start | bytes 1572872 | tf_op jit(solution)/shard_map/ppermute | solution.py:694
  63.4 22.4 %collective-permute-start.21 = (bf16[128,2048]{1,0:T(8,128)(2,1)S(1)}, bf16[128,2048]{1,0:T(8,128)(2,1)}, u32[]{:S(2)}, u32[]{:S(2)}) collective-permute-start(bf16[128,2048]{1,0:T(8,128)(2,1)S(1)} %get-tuple-element.227), channel_id=1, source_target_pairs={{0,16},{16,0},{1,17},{17,1},{2,18},{18,2},{3,19},{19,3},{4,20},{20... | collective-permute-start | bytes 1572872 | tf_op jit(solution)/shard_map/ppermute | solution.py:694
  81.5 246.5 %reduce-scatter.3.cloned.1.call-start = ((), (), s32[]{:S(2)}) async-start(), calls=%async_computation.4 | async-start | bytes 1310720 | tf_op jit(solution)/shard_map/reduce_scatter | solution.py:851
  89.6 22.3 %collective-permute-start.22 = (bf16[256,2048]{1,0:T(8,128)(2,1)}, bf16[256,2048]{1,0:T(8,128)(2,1)}, u32[]{:S(2)}, u32[]{:S(2)}) collective-permute-start(bf16[256,2048]{1,0:T(8,128)(2,1)} %pad_maximum_fusion.refs_4_), channel_id=1, source_target_pairs={{0,1},{1,0},{2,3},{3,2},{4,5},{5,4},{6,7},{7,6},{8,9},{9,8},{10,11... | collective-permute-start | bytes 3145736 | tf_op jit(solution)/shard_map/ppermute | solution.py:694
  90.2 21.7 %collective-permute-start.24 = (bf16[256,2048]{1,0:T(8,128)(2,1)S(1)}, bf16[256,2048]{1,0:T(8,128)(2,1)}, u32[]{:S(2)}, u32[]{:S(2)}) collective-permute-start(bf16[256,2048]{1,0:T(8,128)(2,1)S(1)} %pad_maximum_fusion.1.refs_4_), channel_id=1, source_target_pairs={{0,16},{16,0},{1,17},{17,1},{2,18},{18,2},{3,19},{19,3},{4,20},{20... | collective-permute-start | bytes 3145736 | tf_op jit(solution)/shard_map/ppermute | solution.py:694
  117.5 19.6 %collective-permute-start.28 = (bf16[128,2048]{1,0:T(8,128)(2,1)S(1)}, bf16[128,2048]{1,0:T(8,128)(2,1)S(1)}, u32[]{:S(2)}, u32[]{:S(2)}) collective-permute-start(bf16[128,2048]{1,0:T(8,128)(2,1)S(1)} %get-tuple-element.232), channel_id=1, source_target_pairs={{0,1},{1,0},{2,3},{3,2},{4,5},{5,4},{6,7},{7,6},{8,9},{9,8},{10,11... | collective-permute-start | bytes 1572872 | tf_op jit(solution)/shard_map/ppermute | solution.py:694
  119.1 18.1 %collective-permute-start.26 = (bf16[128,2048]{1,0:T(8,128)(2,1)S(1)}, bf16[128,2048]{1,0:T(8,128)(2,1)S(1)}, u32[]{:S(2)}, u32[]{:S(2)}) collective-permute-start(bf16[128,2048]{1,0:T(8,128)(2,1)S(1)} %get-tuple-element.233), channel_id=1, source_target_pairs={{0,16},{16,0},{1,17},{17,1},{2,18},{18,2},{3,19},{19,3},{4,20},{20... | collective-permute-start | bytes 1572872 | tf_op jit(solution)/shard_map/ppermute | solution.py:694
  137.4 24.7 %collective-permute-start.27 = (bf16[256,2048]{1,0:T(8,128)(2,1)S(1)}, bf16[256,2048]{1,0:T(8,128)(2,1)S(1)}, u32[]{:S(2)}, u32[]{:S(2)}) collective-permute-start(bf16[256,2048]{1,0:T(8,128)(2,1)S(1)} %pad_maximum_fusion.2.refs_4_), channel_id=1, source_target_pairs={{0,1},{1,0},{2,3},{3,2},{4,5},{5,4},{6,7},{7,6},{8,9},{9,8},{10,11... | collective-permute-start | bytes 3145736 | tf_op jit(solution)/shard_map/ppermute | solution.py:694
  138.0 24.4 %collective-permute-start.29 = (bf16[256,2048]{1,0:T(8,128)(2,1)S(1)}, bf16[256,2048]{1,0:T(8,128)(2,1)S(1)}, u32[]{:S(2)}, u32[]{:S(2)}) collective-permute-start(bf16[256,2048]{1,0:T(8,128)(2,1)S(1)} %pad_maximum_fusion.3.refs_4_), channel_id=1, source_target_pairs={{0,16},{16,0},{1,17},{17,1},{2,18},{18,2},{3,19},{19,3},{4,20},{20... | collective-permute-start | bytes 3145736 | tf_op jit(solution)/shard_map/ppermute | solution.py:694
  162.4 35.9 %collective-permute-start.31 = (bf16[256,2048]{1,0:T(8,128)(2,1)}, bf16[256,2048]{1,0:T(8,128)(2,1)S(1)}, u32[]{:S(2)}, u32[]{:S(2)}) collective-permute-start(bf16[256,2048]{1,0:T(8,128)(2,1)} %get-tuple-element.145), channel_id=1, source_target_pairs={{0,1},{1,0},{2,3},{3,2},{4,5},{5,4},{6,7},{7,6},{8,9},{9,8},{10,11... | collective-permute-start | bytes 3145736 | tf_op jit(solution)/shard_map/ppermute | solution.py:705
  163.9 34.4 %collective-permute-start.30 = (bf16[256,2048]{1,0:T(8,128)(2,1)S(1)}, bf16[256,2048]{1,0:T(8,128)(2,1)S(1)}, u32[]{:S(2)}, u32[]{:S(2)}) collective-permute-start(bf16[256,2048]{1,0:T(8,128)(2,1)S(1)} %copy-done.36), channel_id=1, source_target_pairs={{0,16},{16,0},{1,17},{17,1},{2,18},{18,2},{3,19},{19,3},{4,20},{20... | collective-permute-start | bytes 3145736 | tf_op jit(solution)/shard_map/ppermute | solution.py:705
  209.3 18.0 %collective-permute-start.32 = (bf16[1024,1024]{1,0:T(8,128)(2,1)}, bf16[1024,1024]{1,0:T(8,128)(2,1)S(1)}, u32[]{:S(2)}, u32[]{:S(2)}) collective-permute-start(bf16[1024,1024]{1,0:T(8,128)(2,1)} %hidden_backward.1), channel_id=1, source_target_pairs={{0,8},{8,0},{1,9},{9,1},{2,10},{10,2},{3,11},{11,3},{4,12},{12,4},... | collective-permute-start | bytes 6291464 | tf_op jit(solution)/shard_map/ppermute | solution.py:755
  209.9 15.1 %collective-permute-start.34 = (bf16[128,2048]{1,0:T(8,128)(2,1)}, bf16[128,2048]{1,0:T(8,128)(2,1)}, u32[]{:S(2)}, u32[]{:S(2)}) collective-permute-start(bf16[128,2048]{1,0:T(8,128)(2,1)} %get-tuple-element.218), channel_id=1, source_target_pairs={{0,16},{16,0},{1,17},{17,1},{2,18},{18,2},{3,19},{19,3},{4,20},{20... | collective-permute-start | bytes 1572872 | tf_op jit(solution)/shard_map/ppermute | solution.py:705
  211.3 35.5 %collective-permute-start.35 = (bf16[256,2048]{1,0:T(8,128)(2,1)}, bf16[256,2048]{1,0:T(8,128)(2,1)}, u32[]{:S(2)}, u32[]{:S(2)}) collective-permute-start(bf16[256,2048]{1,0:T(8,128)(2,1)} %get-tuple-element.173), channel_id=1, source_target_pairs={{0,16},{16,0},{1,17},{17,1},{2,18},{18,2},{3,19},{19,3},{4,20},{20... | collective-permute-start | bytes 3145736 | tf_op jit(solution)/shard_map/ppermute | solution.py:705
  211.9 35.0 %collective-permute-start.36 = (bf16[256,2048]{1,0:T(8,128)(2,1)}, bf16[256,2048]{1,0:T(8,128)(2,1)}, u32[]{:S(2)}, u32[]{:S(2)}) collective-permute-start(bf16[256,2048]{1,0:T(8,128)(2,1)} %get-tuple-element.179), channel_id=1, source_target_pairs={{0,1},{1,0},{2,3},{3,2},{4,5},{5,4},{6,7},{7,6},{8,9},{9,8},{10,11... | collective-permute-start | bytes 3145736 | tf_op jit(solution)/shard_map/ppermute | solution.py:705
  252.2 26.6 %collective-permute-start.40 = (bf16[128,2048]{1,0:T(8,128)(2,1)}, bf16[128,2048]{1,0:T(8,128)(2,1)}, u32[]{:S(2)}, u32[]{:S(2)}) collective-permute-start(bf16[128,2048]{1,0:T(8,128)(2,1)} %get-tuple-element.214), channel_id=1, source_target_pairs={{0,16},{16,0},{1,17},{17,1},{2,18},{18,2},{3,19},{19,3},{4,20},{20... | collective-permute-start | bytes 1572872 | tf_op jit(solution)/shard_map/ppermute | solution.py:705
  253.6 75.6 %reduce-scatter.5.cloned.1.call-start = ((), (), s32[]{:S(2)}) async-start(), calls=%async_computation.5 | async-start | bytes 1310720 | tf_op jit(solution)/shard_map/reduce_scatter | solution.py:851
  253.9 26.0 %collective-permute-start.39 = (bf16[128,2048]{1,0:T(8,128)(2,1)}, bf16[128,2048]{1,0:T(8,128)(2,1)}, u32[]{:S(2)}, u32[]{:S(2)}) collective-permute-start(bf16[128,2048]{1,0:T(8,128)(2,1)} %get-tuple-element.216), channel_id=1, source_target_pairs={{0,1},{1,0},{2,3},{3,2},{4,5},{5,4},{6,7},{7,6},{8,9},{9,8},{10,11... | collective-permute-start | bytes 1572872 | tf_op jit(solution)/shard_map/ppermute | solution.py:705
  256.7 24.5 %collective-permute-start.38 = (bf16[256,1024]{1,0:T(8,128)(2,1)}, bf16[256,1024]{1,0:T(8,128)(2,1)}, u32[]{:S(2)}, u32[]{:S(2)}) collective-permute-start(bf16[256,1024]{1,0:T(8,128)(2,1)} %get-tuple-element.212), channel_id=1, source_target_pairs={{0,16},{16,0},{1,17},{17,1},{2,18},{18,2},{3,19},{19,3},{4,20},{20... | collective-permute-start | bytes 1572872 | tf_op jit(solution)/shard_map/ppermute | solution.py:705
  279.9 37.4 %collective-permute-start.46 = (bf16[1024,1024]{1,0:T(8,128)(2,1)S(1)}, bf16[1024,1024]{1,0:T(8,128)(2,1)}, u32[]{:S(2)}, u32[]{:S(2)}) collective-permute-start(bf16[1024,1024]{1,0:T(8,128)(2,1)S(1)} %copy-done.6), channel_id=1, source_target_pairs={{0,8},{8,0},{1,9},{9,1},{2,10},{10,2},{3,11},{11,3},{4,12},{12,4},... | collective-permute-start | bytes 6291464 | tf_op jit(solution)/shard_map/ppermute | solution.py:755
  (70 other events, 627.0 us)
Sparse Core Ops, SparseCore 0:
  25.2 32.1 all-gather.2
  81.6 25.0 all-gather.4
  253.8 26.4 reduce-scatter.2
  296.9 25.7 reduce-scatter.4

commit v5 on v4

--- a/solution.py
+++ b/solution.py
@@ -22,7 +22,7 @@
 LOG2E = math.log2(math.e)
 MARKS = 64
 GROUP = 2
-VMEM_MIB = 60
+VMEM_MIB = 40
 HINT = 8
 FFN_MIB = 44
 
@@ -327,18 +327,22 @@
     return a, h + (a - a * h) * ((2 * GELU_A) + (6 * GELU_B) * v2)
 
 
-def ffn_kernel(sizes, order, me_ref, *refs):
+def ffn_kernel(sizes, order, chunk, joined, me_ref, *refs):
     count, lines = seconds(sizes, order), firsts(sizes, order)
     take = lambda n: [refs.pop(0) for _ in range(n)]
     refs = list(refs)
     near, ins = take(4), take(count)
+    take(joined)
     seen, whole, outs = take(4), take(2), take(lines)
     pieces = take(count)
     acts, (up_ref, down_ref), (gu, gd), staged = take(4), take(2), take(2), take(lines)
     in_sem, out_sem = refs
     part, model = down_ref.shape
     shard = part // math.prod(sizes)
-    tile = min(256, part)
+    share = slice(chunk * part, (chunk + 1) * part)
+    seen = [a.at[:, share] for a in seen]
+    whole = [whole[0].at[:, share], whole[1].at[share, :]]
+    tile = min(512, part)
 
     loads = [pltpu.make_async_copy(a, b, in_sem.at[n]) for n, (a, b) in enumerate(zip(ins, pieces))]
     for load in loads:
@@ -395,94 +399,86 @@
         copy.wait()
 
 
-def ffn(sizes, order, me, nt_o, nt_p, dy_o, dy_p, pieces):
+def ffn(sizes, order, chunk, chunks, me, nt_o, nt_p, dy_o, dy_p, pieces, joint):
     rows, model = nt_o.shape
     part = model // 2
     up, down = shape((model, part), bf16), shape((part, model), bf16)
     lines = firsts(sizes, order)
     grads = [shape((part // lines, 2 * model), bf16)] * lines
-    ins = (nt_o, nt_p, dy_o, dy_p, *pieces)
-    outs = [shape((rows, part), bf16)] * 4 + [up, down] + grads
+    ins = (nt_o, nt_p, dy_o, dy_p, *pieces, *joint)
+    seen = [shape((rows, part), bf16)] * 4
+    outs = [shape((rows, chunks * part), bf16)] * 4
+    outs += [shape((model, chunks * part), bf16), shape((chunks * part, model), bf16), *grads]
     far = pl.BlockSpec(memory_space=pltpu.HBM)
     outs = call(
-        functools.partial(ffn_kernel, sizes, order),
+        functools.partial(ffn_kernel, sizes, order, chunk, len(joint)),
         outs,
         (me, *ins),
         16 * rows * model * part,
         2 * rows * part,
-        [pltpu.VMEM(a.shape, bf16) for a in (*pieces, *outs[:4], up, down, up, down, *grads)]
+        [pltpu.VMEM(a.shape, bf16) for a in (*pieces, *seen, up, down, up, down, *grads)]
         + [pltpu.SemaphoreType.DMA((len(pieces),)), pltpu.SemaphoreType.DMA((len(outs),))],
         FFN_MIB,
         "ffn",
-        [SM] + [NEAR] * 4 + [far] * len(pieces),
+        [SM] + [NEAR] * 4 + [far] * (len(pieces) + len(joint)),
         out_specs=[far] * len(outs),
+        input_output_aliases={5 + len(pieces) + n: n for n in range(len(joint))},
     )
-    return outs[:4], outs[4], outs[5], outs[6:]
-
-
-def hidden_backward_kernel(count, *refs):
-    gis, ups, gn_ref = refs[:count], refs[count : 2 * count], refs[2 * count]
-    total = None
-    for i, u in zip(gis, ups):
-        v = nt(i[...], u[...])
-        total = v if total is None else total + v
-    gn_ref[...] = total.astype(bf16)
-
-
-def hidden_backward(gis, ups):
-    rows, part = gis[0].shape
-    model = ups[0].shape[0]
-    count = len(gis)
-    tile = model // 4
+    return outs[:6], outs[6:]
+
+
+def hidden_backward_kernel(gi_ref, up_ref, gn_ref):
+    gn_ref[...] = nt(gi_ref[...], up_ref[...]).astype(bf16)
+
+
+def hidden_backward(gi, up):
+    rows, inner = gi.shape
+    model = up.shape[0]
+    tile = rows // 4
     return call(
-        functools.partial(hidden_backward_kernel, count),
+        hidden_backward_kernel,
         [shape((rows, model), bf16)],
-        (*gis, *ups),
-        count * 2 * rows * part * model,
+        (gi, up),
+        2 * rows * inner * model,
         0,
         (),
         VMEM_MIB,
         "hidden_backward",
-        [pl.BlockSpec((tile, part), lambda g: (g, 0))] * count + [held(u) for u in ups],
+        [pl.BlockSpec((tile, inner), lambda g: (g, 0)), held(up)],
         grid=(rows // tile,),
         out_specs=[pl.BlockSpec((tile, model), lambda g: (g, 0))],
     )[0]
 
 
-def down_kernel(count, *refs):
-    acts, downs, more, out_ref = refs[:count], refs[count : 2 * count], refs[2 * count : -1], refs[-1]
-    total = None
-    for a, d in zip(acts, downs):
-        v = nn(a[...], d[...])
-        total = v if total is None else total + v
+def down_kernel(a_ref, d_ref, *refs):
+    *more, out_ref = refs
+    total = nn(a_ref[...], d_ref[...])
     for m in more:
         total = total + m[...].astype(f32)
     out_ref[...] = total.astype(bf16)
 
 
-def down(acts, downs, more):
-    rows, part = acts[0].shape
-    model = downs[0].shape[1]
-    count = len(acts)
+def down(act, weight, more):
+    rows, inner = act.shape
+    model = weight.shape[1]
     tile = rows // 4
     strip = pl.BlockSpec((tile, model), lambda g: (g, 0))
     return call(
-        functools.partial(down_kernel, count),
+        down_kernel,
         [shape((rows, model), bf16)],
-        (*acts, *downs, *more),
-        count * 2 * rows * part * model,
+        (act, weight, *more),
+        2 * rows * inner * model,
         0,
         (),
         VMEM_MIB,
         "down",
-        [pl.BlockSpec((tile, part), lambda g: (g, 0))] * count + [held(d) for d in downs] + [strip] * len(more),
+        [pl.BlockSpec((tile, inner), lambda g: (g, 0)), held(weight)] + [strip] * len(more),
         grid=(rows // tile,),
         out_specs=[strip],
     )[0]
 
 
-def branch_backward_kernel(sizes, orders, count, me_ref, hidden_ref, gn_ref, dy_ref, att_ref, gains_ref, wo_ref, *refs):
-    gis, ups, refs = refs[:count], refs[count : 2 * count], refs[2 * count :]
+def branch_backward_kernel(sizes, orders, me_ref, hidden_ref, gn_ref, dy_ref, att_ref, gains_ref, wo_ref, gi_ref, up_ref, *refs):
     gh_ref, gatt_ref, gg_ref, *halves, gn, gb, gwo, low = refs
     step = pl.program_id(0)
     rows = hidden_ref.shape[0]
@@ -492,10 +488,7 @@
         gg_ref[...] = jnp.zeros_like(gg_ref)
         gwo[...] = jnp.zeros_like(gwo)
 
-    total = gn_ref[...].astype(f32)
-    for i, u in zip(gis, ups):
-        total = total + nt(i[...], u[...])
-    gn[...] = total
+    gn[...] = gn_ref[...].astype(f32) + nt(gi_ref[...], up_ref[...])
 
     @pl.loop(0, rows // 64, unroll=True)
     def _(t):
@@ -518,19 +511,18 @@
         hand_out(sizes, me_ref, orders, low, halves)
 
 
-def branch_backward(sizes, orders, me, hidden, gn, dy, att, gains, wo, gis, ups):
+def branch_backward(sizes, orders, me, hidden, gn, dy, att, gains, wo, gi, up):
     rows, model = hidden.shape
-    part = gis[0].shape[1]
-    count = len(gis)
+    inner = gi.shape[1]
     tile = rows // 4
     strip = pl.BlockSpec((tile, model), lambda i: (i, 0))
     gg = shape((8, model), f32)
     halves = [shape((model // 2, model // len(orders)), bf16)] * (2 * len(orders))
     return call(
-        functools.partial(branch_backward_kernel, sizes, orders, count),
+        functools.partial(branch_backward_kernel, sizes, orders),
         [shape((rows, model), f32), shape((rows, model), bf16), gg, *halves],
-        (me, hidden, gn, dy, att, gains, wo, *gis, *ups),
-        4 * rows * model * model + count * 2 * rows * part * model,
+        (me, hidden, gn, dy, att, gains, wo, gi, up),
+        4 * rows * model * model + 2 * rows * inner * model,
         0,
         [
             pltpu.VMEM((tile, model), f32),
@@ -541,8 +533,7 @@
         VMEM_MIB,
         "branch_backward",
         [SM, strip, strip, strip, strip, held(gains), held(wo)]
-        + [pl.BlockSpec((tile, part), lambda i: (i, 0))] * count
-        + [held(u) for u in ups],
+        + [pl.BlockSpec((tile, inner), lambda i: (i, 0)), held(up)],
         grid=(rows // tile,),
         out_specs=[strip, strip, held(gg), *map(held, halves)],
     )
@@ -814,15 +805,13 @@
     nt_o = after(nt_o, *pieces[0], *pieces[1], f_along[1])
     nt_p = swap(nt_o)
 
-    acts_o, acts_p, gis_o, gis_p, ups, downs = [], [], [], [], [], []
+    grads, joint = [], []
 
     def run_ffn(c, *first):
-        seen, up_c, down_c, grads = ffn(sizes, by_index[c], me, after(nt_o, *first), nt_p, cotangent, dy_p, pieces[c])
-        for kept, a in zip((acts_o, acts_p, gis_o, gis_p), seen):
-            kept.append(a)
-        ups.append(up_c)
-        downs.append(down_c)
-        return grads
+        joint[:], sent = ffn(
+            sizes, by_index[c], c, chunks, me, after(nt_o, *first), nt_p, cotangent, dy_p, pieces[c], joint
+        )
+        grads.append(sent)
 
     def sum_cores(keep, come, order):
         n = firsts(sizes, order)
@@ -830,31 +819,32 @@
 
     f_along[1] = after(f_along[1], nt_p)
     lines = [p for c in (2, 3) for p in f_lines(c)]
-    grads = [run_ffn(0)]
-    grads.append(run_ffn(1, *lines, ups[0]))
+    run_ffn(0)
+    run_ffn(1, *lines)
     for c in (2, 3):
-        hops[c].lines[1:] = [after(p, ups[0]) for p in hops[c].lines[1:]]
+        hops[c].lines[1:] = [after(p, grads[0][0]) for p in hops[c].lines[1:]]
         pieces[c] = hops[c].gather_two()
-    late = [*pieces[2], *pieces[3], ups[1]]
-    grads.append(run_ffn(2, *late))
+    late = [*pieces[2], *pieces[3], grads[1][0]]
+    run_ffn(2, *late)
     for c in (0, 1):
         hops[c].reduce_one([after(g, *late) for g in grads[c]])
-    grads.append(run_ffn(3, ups[2]))
+    run_ffn(3)
     for c in (0, 1):
-        hops[c].hold(ups[3])
+        hops[c].hold(grads[3][0])
+    act_o, act_p, gi_o, gi_p, up, down_whole = joint
     ready = [p for c in (0, 1) for p in hops[c].reduce_two()]
     for c in (2, 3):
         hops[c].reduce_one([after(g, *ready) for g in grads[c]])
-    gn_p = hidden_backward([after(gis_p[0], *ready), *gis_p[1:]], ups)
+    gn_p = hidden_backward(after(gi_p, *ready), up)
     gn_r = swap(gn_p)
-    out_p = down([after(acts_p[0], gn_p), *acts_p[1:]], downs, [])
+    out_p = down(after(act_p, gn_p), down_whole, [])
     last = lambda a: lax.psum_scatter(a, "f1", scatter_dimension=0, tiled=True)
     for c in (0, 1):
         hops[c].hold(out_p)
     pair = jnp.concatenate([hops[c].sum_two()[0] for c in (0, 1)], axis=1)
     sums = [last(pair)]
     gh, gatt, gg, *halves = branch_backward(
-        sizes, wo_back, me, hidden, gn_r, cotangent, att, gains, wo, [after(gis_o[0], pair), *gis_o[1:]], ups
+        sizes, wo_back, me, hidden, gn_r, cotangent, att, gains, wo, after(gi_o, pair), up
     )
     for c in (2, 3):
         hops[c].hold(gatt)
@@ -884,7 +874,7 @@
     for h in w_reduce:
         h.hold(grad_tokens)
         ready += h.reduce_two()
-    output = down([after(acts_o[0], *ready), *acts_o[1:]], downs, [hidden, out_r])
+    output = down(after(act_o, *ready), down_whole, [hidden, out_r])
     for h in w_reduce:
         h.hold(output)
     w_parts = [jnp.concatenate([*p, cut(wo_last, n, na)], axis=1) for n, p in enumerate(zip(*[h.sum_two(na) for h in w_reduce]))]

time: 361 us -> 349 us (0.967)
  other arithmetic: 35.8 us -> 24.5 us
    convert_element_type x7, other arithmetic: 10.7 us -> 6.58 us  [reduce_two(): add([cut(p, s, n) for p in self.got]).astype(bf16)]
  transfers between devices with their start and end apart: 57 -> 57, of which waited for: 20 -> 22; matrix products, arithmetic and copies ran while one was open for 11% -> 9% of each run, Pallas kernels for 47% -> 48%
where the time goes in v5:
time: 349 us; the launch traced here: 344 us
  Pallas kernels  175 us (50%)
  waiting for transfers between devices  58 us (17%)
  starting transfers between devices  46.8 us (13%)
  local copies, waits for them, and re-layouts  25.3 us (7%)
  other arithmetic  24.5 us (7%)
  between operations  14.9 us (4%)
    pallas_call x14, Pallas kernels, call(): pl.pallas_call(kernel, out_shape=outs, in_specs=specs, out_specs=kw.pop('...  175 us
    ppermute x19, waiting for transfers between devices, spread(): lax.ppermute(a, axis, [(i, (i + s) % n) for i in range(n)])  33 us
    ppermute x19, starting transfers between devices, spread(): lax.ppermute(a, axis, [(i, (i + s) % n) for i in range(n)])  25.3 us
    ppermute x17, starting transfers between devices, send_on(): lax.ppermute(parts[s], axis, [(i, (i + s) % n) for i in range(n)])  18.5 us
    ppermute x17, waiting for transfers between devices, on_device(): swap = lambda a: lax.ppermute(a, 'core', [(0, 1), (1, 0)])  12.1 us
    ppermute x17, waiting for transfers between devices, send_on(): lax.ppermute(parts[s], axis, [(i, (i + s) % n) for i in range(n)])  8.38 us
  transfers between devices with their start and end apart: 57, of which 22 were waited for; matrix products, arithmetic and copies ran while one was open for 9% of the time, Pallas kernels for 48%

profile of v5, /device:TPU:0, one launch (start us, length us, event | category | flops | bytes accessed | tf_op | source)
XLA Modules:
  0.0 343.9 jit_solution(2520226903282491567)
XLA Ops:
  11.0 4.6 %collective-permute-start.2 = (bf16[32,1408]{1,0:T(8,128)(2,1)}, bf16[32,1408]{1,0:T(8,128)(2,1)}, u32[]{:S(2)}, u32[]{:S(2)}) collective-permute-start(bf16[32,1408]{1,0:T(8,128)(2,1)} %pad_maximum_fusion.23), channel_id=1, source_target_pairs={{0,6},{2,0},{4,2},{6,4},{1,7},{3,1},{5,3},{7,5},{8,14},{10,8},{12,... | collective-permute-start | bytes 270344 | tf_op jit(solution)/shard_map/ppermute | solution.py:685
  20.5 4.6 %collective-permute-done.1 = bf16[32,1408]{1,0:T(8,128)(2,1)} collective-permute-done((bf16[32,1408]{1,0:T(8,128)(2,1)}, bf16[32,1408]{1,0:T(8,128)(2,1)}, u32[]{:S(2)}, u32[]{:S(2)}) %collective-permute-start.1) | collective-permute-done | bytes 90144 | tf_op jit(solution)/shard_map/ppermute | solution.py:685
  30.3 3.4 collective-permute-done.7
  36.9 7.6 %collective-permute-done.8.refs_5_ = bf16[256,768]{1,0:T(8,128)(2,1)S(1)} collective-permute-done((bf16[256,768]{1,0:T(8,128)(2,1)S(1)}, bf16[256,768]{1,0:T(8,128)(2,1)S(1)}, u32[]{:S(2)}, u32[]{:S(2)}) %collective-permute-start.8) | collective-permute-done | bytes 393248 | tf_op jit(solution)/shard_map/ppermute | solution.py:685
  48.1 7.4 %project.1 = (bf16[1024,1408]{1,0:T(8,128)(2,1)}, bf16[1024,1280]{1,0:T(8,128)(2,1)}, f32[8,1024]{1,0:T(8,128)}) custom-call(s32[4]{0:T(128)S(1)} %pad_add_fusion.me_ref, bf16[1024,1024]{1,0:T(8,128)(2,1)} %x_ref.5, bf16[256,640]{1,0:T(8,128)(2,1)} %copy-done.12, bf16[256,640]{1,0:T(8,128)(2,1)} %collective-permute-done.4.refs_1_, ...), custom_call_target="tpu_custom_call" | custom-call | flops 335544320 | bytes 1314818 | tf_op jit(solution)/shard_map/project/pallas_call | solution.py:54
  64.0 10.5 %attention_forward.1 = (bf16[1024,1024]{1,0:T(8,128)(2,1)}, f32[1024,128]{1,0:T(8,128)}) custom-call(s32[1,8]{1,0:T(1,128)S(1)} %copy-done.2, bf16[1024,1280]{1,0:T(8,128)(2,1)} %get-tuple-element.183.qkv_ref), custom_call_target="tpu_custom_call" | custom-call | flops 536870912 | bytes 655364 | tf_op jit(solution)/shard_map/attention_forward/pallas_call | solution.py:54
  79.1 2.9 collective-permute-done.14.refs_1_
  93.7 8.1 %branch.1 = (bf16[1024,1024]{1,0:T(8,128)(2,1)}, f32[1024,1024]{1,0:T(8,128)}, bf16[1024,1024]{1,0:T(8,128)(2,1)}) custom-call(s32[4]{0:T(128)S(1)} %pad_add_fusion.me_ref, bf16[1024,1024]{1,0:T(8,128)(2,1)} %x_ref.5, bf16[1024,1024]{1,0:T(8,128)(2,1)} %get-tuple-element.112.att_ref, f32[8,1024]{1,0:T(8,128)} %get-tuple-element.113.gains_ref, ...), custom_call_target="tpu_custom_call" | custom-call | flops 268435456 | bytes 1839106 | tf_op jit(solution)/shard_map/branch/pallas_call | solution.py:54
  104.3 5.1 %collective-permute-done.22.refs_5_ = bf16[256,2048]{1,0:T(8,128)(2,1)} collective-permute-done((bf16[256,2048]{1,0:T(8,128)(2,1)}, bf16[256,2048]{1,0:T(8,128)(2,1)}, u32[]{:S(2)}, u32[]{:S(2)}) %collective-permute-start.22) | collective-permute-done | bytes 1048608 | tf_op jit(solution)/shard_map/ppermute | solution.py:685
  109.9 4.4 %collective-permute-done.25.refs_1_ = bf16[1024,1024]{1,0:T(8,128)(2,1)S(1)} collective-permute-done((bf16[1024,1024]{1,0:T(8,128)(2,1)}, bf16[1024,1024]{1,0:T(8,128)(2,1)S(1)}, u32[]{:S(2)}, u32[]{:S(2)}) %collective-permute-start.25) | collective-permute-done | bytes 2097184 | tf_op jit(solution)/shard_map/ppermute | solution.py:746
  118.2 16.2 %ffn.4 = (bf16[1024,2048]{1,0:T(8,128)(2,1)}, bf16[1024,2048]{1,0:T(8,128)(2,1)}, bf16[1024,2048]{1,0:T(8,128)(2,1)}, bf16[1024,2048]{1,0:T(8,128)(2,1)}, bf16[1...) custom-call(s32[4]{0:T(128)S(1)} %pad_add_fusion.me_ref, ...), custom_call_target="tpu_custom_call" | custom-call | flops 1073741824 | bytes 4718594 | tf_op jit(solution)/shard_map/ffn/pallas_call | solution.py:54
  136.2 15.8 %ffn.5 = (bf16[1024,2048]{1,0:T(8,128)(2,1)}, bf16[1024,2048]{1,0:T(8,128)(2,1)}, bf16[1024,2048]{1,0:T(8,128)(2,1)}, bf16[1024,2048]{1,0:T(8,128)(2,1)}, bf16[1...) custom-call(s32[4]{0:T(128)S(1)} %pad_add_fusion.me_ref, ...), custom_call_target="tpu_custom_call", output_to_operand_aliasing={{0}: (7, {}), {1}: (8, {}), {2}: (9, {}), {3}: (10, {}), {4... | custom-call | flops 1073741824 | bytes 7864322 | tf_op jit(solution)/shard_map/ffn/pallas_call | solution.py:54
  152.1 7.3 %collective-permute-done.27.refs_5_ = bf16[256,2048]{1,0:T(8,128)(2,1)S(1)} collective-permute-done((bf16[256,2048]{1,0:T(8,128)(2,1)S(1)}, bf16[256,2048]{1,0:T(8,128)(2,1)S(1)}, u32[]{:S(2)}, u32[]{:S(2)}) %collective-permute-start.27) | collective-permute-done | bytes 1048608 | tf_op jit(solution)/shard_map/ppermute | solution.py:685
  161.6 15.7 %ffn.6 = (bf16[1024,2048]{1,0:T(8,128)(2,1)}, bf16[1024,2048]{1,0:T(8,128)(2,1)}, bf16[1024,2048]{1,0:T(8,128)(2,1)}, bf16[1024,2048]{1,0:T(8,128)(2,1)}, bf16[1...) custom-call(s32[4]{0:T(128)S(1)} %pad_add_fusion.me_ref, ...), custom_call_target="tpu_custom_call", output_to_operand_aliasing={{0}: (7, {}), {1}: (8, {}), {2}: (9, {}), {3}: (10, {}), {4... | custom-call | flops 1073741824 | bytes 7864322 | tf_op jit(solution)/shard_map/ffn/pallas_call | solution.py:54
  177.4 16.1 %ffn.7 = (bf16[1024,2048]{1,0:T(8,128)(2,1)}, bf16[1024,2048]{1,0:T(8,128)(2,1)}, bf16[1024,2048]{1,0:T(8,128)(2,1)}, bf16[1024,2048]{1,0:T(8,128)(2,1)}, bf16[1...) custom-call(s32[4]{0:T(128)S(1)} %pad_add_fusion.me_ref, ...), custom_call_target="tpu_custom_call", output_to_operand_aliasing={{0}: (7, {}), {1}: (8, {}), {2}: (9, {}), {3}: (10, {}), {4... | custom-call | flops 1073741824 | bytes 7864322 | tf_op jit(solution)/shard_map/ffn/pallas_call | solution.py:54
  195.1 8.7 %hidden_backward.1 = bf16[1024,1024]{1,0:T(8,128)(2,1)} custom-call(bf16[1024,2048]{1,0:T(8,128)(2,1)} %get-tuple-element.160.gi_ref, bf16[1024,2048]{1,0:T(8,128)(2,1)} %get-tuple-element.161.up_ref), custom_call_target="tpu_custom_call" | custom-call | flops 536870912 | bytes 1310720 | tf_op jit(solution)/shard_map/hidden_backward/pallas_call | solution.py:54
  207.9 8.5 %down.2 = bf16[1024,1024]{1,0:T(8,128)(2,1)} custom-call(bf16[1024,2048]{1,0:T(8,128)(2,1)} %get-tuple-element.165.a_ref, bf16[2048,1024]{1,0:T(8,128)(2,1)} %get-tuple-element.166.d_ref), custom_call_target="tpu_custom_call" | custom-call | flops 536870912 | bytes 1310720 | tf_op jit(solution)/shard_map/down/pallas_call | solution.py:54
  222.8 18.4 %branch_backward.1 = (f32[1024,1024]{1,0:T(8,128)}, bf16[1024,1024]{1,0:T(8,128)(2,1)}, f32[8,1024]{1,0:T(8,128)}, bf16[512,1024]{1,0:T(8,128)(2,1)}, bf16[512,1024]{1,0:T(8,128)(2,1)}) custom-call(s32[4]{0:T(128)S(1)} %pad_add_fusion.me_ref, f32[1024,1024]{1,0:T(8,128)} %get-tuple-element.149.hidden_ref.refs_0_, bf16[1024,1024]{1,0:T(8,128)(2,1)} %copy-done.7, ...), custom_call_target="tpu_custom_call" | custom-call | flops 1073741824 | bytes 3678210 | tf_op jit(solution)/shard_map/branch_backward/pallas_call | solution.py:54
  250.8 21.0 %attention_backward.1.g_ref = bf16[1024,1280]{1,0:T(8,128)(2,1)} custom-call(s32[1,8]{1,0:T(1,128)S(1)} %copy-done.2, bf16[1024,1280]{1,0:T(8,128)(2,1)} %get-tuple-element.183.qkv_ref, bf16[1024,1024]{1,0:T(8,128)(2,1)} %get-tuple-element.176.ga_ref, bf16[1024,1024]{1,0:T(8,128)(2,1)} %get-tuple-element.112.att_ref, f32[1024,128]{1,0:T(8,128)} %get-tuple-element.184.lse_ref), custom_call_target="tpu_custom_call" | custom-call | flops 1342177280 | bytes 1245188 | tf_op jit(solution)/shard_map/attention_backward/pallas_call | solution.py:54
  276.0 8.8 %projection_grads.1 = (bf16[512,640]{1,0:T(8,128)(2,1)}, bf16[512,640]{1,0:T(8,128)(2,1)}, bf16[512,768]{1,0:T(8,128)(2,1)}, bf16[512,768]{1,0:T(8,128)(2,1)}) custom-call(s32[4]{0:T(128)S(1)} %pad_add_fusion.me_ref, bf16[1024,1024]{1,0:T(8,128)(2,1)} %x_ref.5, bf16[1024,1280]{1,0:T(8,128)(2,1)} %attention_backward.1.g_ref, ...), custom_call_target="tpu_custom_call" | custom-call | flops 335544320 | bytes 1318914 | tf_op jit(solution)/shard_map/projection_grads/pallas_call | solution.py:54
  294.6 9.0 %input_backward.1 = bf16[1024,1024]{1,0:T(8,128)(2,1)} custom-call(bf16[1024,1024]{1,0:T(8,128)(2,1)} %x_ref.5, bf16[1024,1280]{1,0:T(8,128)(2,1)} %attention_backward.1.g_ref, f32[1024,1024]{1,0:T(8,128)} %get-tuple-element.199.gh_ref, bf16[1024,1408]{1,0:T(8,128)(2,1)} %get-tuple-element.189.w_ref, f32[8,1024]{1,0:T(8,128)} %get-tuple-element.113.gains_ref), custom_call_target="tpu_custom_call" | custom-call | flops 335544320 | bytes 1740800 | tf_op jit(solution)/shard_map/input_backward/pallas_call | solution.py:54
  305.4 10.3 %down.3 = bf16[1024,1024]{1,0:T(8,128)(2,1)} custom-call(bf16[1024,2048]{1,0:T(8,128)(2,1)} %get-tuple-element.202.a_ref, bf16[2048,1024]{1,0:T(8,128)(2,1)} %get-tuple-element.166.d_ref, f32[1024,1024]{1,0:T(8,128)} %get-tuple-element.149.hidden_ref.refs_0_, bf16[1024,1024]{1,0:T(8,128)(2,1)} %collective-permute-done.46.refs_1_), custom_call_target="tpu_custom_call" | custom-call | flops 536870912 | bytes 2097152 | tf_op jit(solution)/shard_map/down/pallas_call | solution.py:54
  327.6 2.8 reshape.110
  330.4 4.6 %collective-permute-done.50 = bf16[32,2432]{1,0:T(8,128)(2,1)S(1)} collective-permute-done((bf16[32,2432]{1,0:T(8,128)(2,1)S(1)}, bf16[32,2432]{1,0:T(8,128)(2,1)S(1)}, u32[]{:S(2)}, u32[]{:S(2)}) %collective-permute-start.50) | collective-permute-done | bytes 155680 | tf_op jit(solution)/shard_map/ppermute | solution.py:696
  (264 shorter events, 107.2 us)
Async XLA Ops:
  7.2 50.3 %all-gather.3.cloned.1.call-start = ((), (), s32[]{:S(2)}) async-start(), calls=%async_computation.2 | async-start | bytes 1638400 | tf_op jit(solution)/shard_map/all_gather | solution.py:775
  25.1 79.2 %all-gather.5.cloned.1.call-start = ((), (), s32[]{:S(2)}) async-start(), calls=%async_computation.3 | async-start | bytes 1310720 | tf_op jit(solution)/shard_map/all_gather | solution.py:775
  25.4 38.6 %collective-permute-start.11 = (bf16[1024,1024]{1,0:T(8,128)(2,1)S(1)}, bf16[1024,1024]{1,0:T(8,128)(2,1)}, u32[]{:S(2)}, u32[]{:S(2)}) collective-permute-start(bf16[1024,1024]{1,0:T(8,128)(2,1)S(1)} %copy-done), channel_id=1, source_target_pairs={{0,8},{8,0},{1,9},{9,1},{2,10},{10,2},{3,11},{11,3},{4,12},{12,4},... | collective-permute-start | bytes 6291464 | tf_op jit(solution)/shard_map/ppermute | solution.py:746
  58.4 16.1 %collective-permute-start.17 = (bf16[128,512]{1,0:T(8,128)(2,1)S(1)}, bf16[128,512]{1,0:T(8,128)(2,1)S(1)}, u32[]{:S(2)}, u32[]{:S(2)}) collective-permute-start(bf16[128,512]{1,0:T(8,128)(2,1)S(1)} %get-tuple-element.226), channel_id=1, source_target_pairs={{0,1},{1,0},{2,3},{3,2},{4,5},{5,4},{6,7},{7,6},{8,9},{9,8},{10,11... | collective-permute-start | bytes 393224 | tf_op jit(solution)/shard_map/ppermute | solution.py:685
  62.8 20.5 %collective-permute-start.23 = (bf16[128,2048]{1,0:T(8,128)(2,1)S(1)}, bf16[128,2048]{1,0:T(8,128)(2,1)}, u32[]{:S(2)}, u32[]{:S(2)}) collective-permute-start(bf16[128,2048]{1,0:T(8,128)(2,1)S(1)} %get-tuple-element.224), channel_id=1, source_target_pairs={{0,1},{1,0},{2,3},{3,2},{4,5},{5,4},{6,7},{7,6},{8,9},{9,8},{10,11... | collective-permute-start | bytes 1572872 | tf_op jit(solution)/shard_map/ppermute | solution.py:685
  63.4 19.9 %collective-permute-start.21 = (bf16[128,2048]{1,0:T(8,128)(2,1)S(1)}, bf16[128,2048]{1,0:T(8,128)(2,1)}, u32[]{:S(2)}, u32[]{:S(2)}) collective-permute-start(bf16[128,2048]{1,0:T(8,128)(2,1)S(1)} %get-tuple-element.225), channel_id=1, source_target_pairs={{0,16},{16,0},{1,17},{17,1},{2,18},{18,2},{3,19},{19,3},{4,20},{20... | collective-permute-start | bytes 1572872 | tf_op jit(solution)/shard_map/ppermute | solution.py:685
  79.1 236.8 %reduce-scatter.3.cloned.1.call-start = ((), (), s32[]{:S(2)}) async-start(), calls=%async_computation.4 | async-start | bytes 1310720 | tf_op jit(solution)/shard_map/reduce_scatter | solution.py:841
  87.2 22.3 %collective-permute-start.22 = (bf16[256,2048]{1,0:T(8,128)(2,1)}, bf16[256,2048]{1,0:T(8,128)(2,1)}, u32[]{:S(2)}, u32[]{:S(2)}) collective-permute-start(bf16[256,2048]{1,0:T(8,128)(2,1)} %pad_maximum_fusion.refs_4_), channel_id=1, source_target_pairs={{0,1},{1,0},{2,3},{3,2},{4,5},{5,4},{6,7},{7,6},{8,9},{9,8},{10,11... | collective-permute-start | bytes 3145736 | tf_op jit(solution)/shard_map/ppermute | solution.py:685
  87.8 22.2 %collective-permute-start.24 = (bf16[256,2048]{1,0:T(8,128)(2,1)S(1)}, bf16[256,2048]{1,0:T(8,128)(2,1)}, u32[]{:S(2)}, u32[]{:S(2)}) collective-permute-start(bf16[256,2048]{1,0:T(8,128)(2,1)S(1)} %pad_maximum_fusion.1.refs_4_), channel_id=1, source_target_pairs={{0,16},{16,0},{1,17},{17,1},{2,18},{18,2},{3,19},{19,3},{4,20},{20... | collective-permute-start | bytes 3145736 | tf_op jit(solution)/shard_map/ppermute | solution.py:685
  115.6 18.8 %collective-permute-start.28 = (bf16[128,2048]{1,0:T(8,128)(2,1)S(1)}, bf16[128,2048]{1,0:T(8,128)(2,1)S(1)}, u32[]{:S(2)}, u32[]{:S(2)}) collective-permute-start(bf16[128,2048]{1,0:T(8,128)(2,1)S(1)} %get-tuple-element.230), channel_id=1, source_target_pairs={{0,16},{16,0},{1,17},{17,1},{2,18},{18,2},{3,19},{19,3},{4,20},{20... | collective-permute-start | bytes 1572872 | tf_op jit(solution)/shard_map/ppermute | solution.py:685
  116.7 17.9 %collective-permute-start.26 = (bf16[128,2048]{1,0:T(8,128)(2,1)S(1)}, bf16[128,2048]{1,0:T(8,128)(2,1)S(1)}, u32[]{:S(2)}, u32[]{:S(2)}) collective-permute-start(bf16[128,2048]{1,0:T(8,128)(2,1)S(1)} %get-tuple-element.231), channel_id=1, source_target_pairs={{0,1},{1,0},{2,3},{3,2},{4,5},{5,4},{6,7},{7,6},{8,9},{9,8},{10,11... | collective-permute-start | bytes 1572872 | tf_op jit(solution)/shard_map/ppermute | solution.py:685
  134.7 24.7 %collective-permute-start.27 = (bf16[256,2048]{1,0:T(8,128)(2,1)S(1)}, bf16[256,2048]{1,0:T(8,128)(2,1)S(1)}, u32[]{:S(2)}, u32[]{:S(2)}) collective-permute-start(bf16[256,2048]{1,0:T(8,128)(2,1)S(1)} %pad_maximum_fusion.2.refs_4_), channel_id=1, source_target_pairs={{0,16},{16,0},{1,17},{17,1},{2,18},{18,2},{3,19},{19,3},{4,20},{20... | collective-permute-start | bytes 3145736 | tf_op jit(solution)/shard_map/ppermute | solution.py:685
  135.3 24.4 %collective-permute-start.29 = (bf16[256,2048]{1,0:T(8,128)(2,1)S(1)}, bf16[256,2048]{1,0:T(8,128)(2,1)S(1)}, u32[]{:S(2)}, u32[]{:S(2)}) collective-permute-start(bf16[256,2048]{1,0:T(8,128)(2,1)S(1)} %pad_maximum_fusion.3.refs_4_), channel_id=1, source_target_pairs={{0,1},{1,0},{2,3},{3,2},{4,5},{5,4},{6,7},{7,6},{8,9},{9,8},{10,11... | collective-permute-start | bytes 3145736 | tf_op jit(solution)/shard_map/ppermute | solution.py:685
  159.7 33.9 %collective-permute-start.30 = (bf16[256,2048]{1,0:T(8,128)(2,1)S(1)}, bf16[256,2048]{1,0:T(8,128)(2,1)S(1)}, u32[]{:S(2)}, u32[]{:S(2)}) collective-permute-start(bf16[256,2048]{1,0:T(8,128)(2,1)S(1)} %copy-done.41), channel_id=1, source_target_pairs={{0,16},{16,0},{1,17},{17,1},{2,18},{18,2},{3,19},{19,3},{4,20},{20... | collective-permute-start | bytes 3145736 | tf_op jit(solution)/shard_map/ppermute | solution.py:696
  161.1 32.4 %collective-permute-start.31 = (bf16[256,2048]{1,0:T(8,128)(2,1)}, bf16[256,2048]{1,0:T(8,128)(2,1)S(1)}, u32[]{:S(2)}, u32[]{:S(2)}) collective-permute-start(bf16[256,2048]{1,0:T(8,128)(2,1)} %get-tuple-element.158), channel_id=1, source_target_pairs={{0,1},{1,0},{2,3},{3,2},{4,5},{5,4},{6,7},{7,6},{8,9},{9,8},{10,11... | collective-permute-start | bytes 3145736 | tf_op jit(solution)/shard_map/ppermute | solution.py:696
  203.8 17.6 %collective-permute-start.32 = (bf16[1024,1024]{1,0:T(8,128)(2,1)}, bf16[1024,1024]{1,0:T(8,128)(2,1)S(1)}, u32[]{:S(2)}, u32[]{:S(2)}) collective-permute-start(bf16[1024,1024]{1,0:T(8,128)(2,1)} %hidden_backward.1), channel_id=1, source_target_pairs={{0,8},{8,0},{1,9},{9,1},{2,10},{10,2},{3,11},{11,3},{4,12},{12,4},... | collective-permute-start | bytes 6291464 | tf_op jit(solution)/shard_map/ppermute | solution.py:746
  205.4 14.8 %collective-permute-start.34 = (bf16[128,2048]{1,0:T(8,128)(2,1)S(1)}, bf16[128,2048]{1,0:T(8,128)(2,1)S(1)}, u32[]{:S(2)}, u32[]{:S(2)}) collective-permute-start(bf16[128,2048]{1,0:T(8,128)(2,1)S(1)} %get-tuple-element.216), channel_id=1, source_target_pairs={{0,16},{16,0},{1,17},{17,1},{2,18},{18,2},{3,19},{19,3},{4,20},{20... | collective-permute-start | bytes 1572872 | tf_op jit(solution)/shard_map/ppermute | solution.py:696
  205.9 36.3 %collective-permute-start.35 = (bf16[256,2048]{1,0:T(8,128)(2,1)}, bf16[256,2048]{1,0:T(8,128)(2,1)}, u32[]{:S(2)}, u32[]{:S(2)}) collective-permute-start(bf16[256,2048]{1,0:T(8,128)(2,1)} %get-tuple-element.175), channel_id=1, source_target_pairs={{0,16},{16,0},{1,17},{17,1},{2,18},{18,2},{3,19},{19,3},{4,20},{20... | collective-permute-start | bytes 3145736 | tf_op jit(solution)/shard_map/ppermute | solution.py:696
  207.4 33.8 %collective-permute-start.36 = (bf16[256,2048]{1,0:T(8,128)(2,1)}, bf16[256,2048]{1,0:T(8,128)(2,1)S(1)}, u32[]{:S(2)}, u32[]{:S(2)}) collective-permute-start(bf16[256,2048]{1,0:T(8,128)(2,1)} %get-tuple-element.180), channel_id=1, source_target_pairs={{0,1},{1,0},{2,3},{3,2},{4,5},{5,4},{6,7},{7,6},{8,9},{9,8},{10,11... | collective-permute-start | bytes 3145736 | tf_op jit(solution)/shard_map/ppermute | solution.py:696
  246.9 24.9 %collective-permute-start.40 = (bf16[128,2048]{1,0:T(8,128)(2,1)}, bf16[128,2048]{1,0:T(8,128)(2,1)}, u32[]{:S(2)}, u32[]{:S(2)}) collective-permute-start(bf16[128,2048]{1,0:T(8,128)(2,1)} %get-tuple-element.212), channel_id=1, source_target_pairs={{0,16},{16,0},{1,17},{17,1},{2,18},{18,2},{3,19},{19,3},{4,20},{20... | collective-permute-start | bytes 1572872 | tf_op jit(solution)/shard_map/ppermute | solution.py:696
  247.5 69.7 %reduce-scatter.5.cloned.1.call-start = ((), (), s32[]{:S(2)}) async-start(), calls=%async_computation.5 | async-start | bytes 1310720 | tf_op jit(solution)/shard_map/reduce_scatter | solution.py:841
  247.7 25.3 %collective-permute-start.39 = (bf16[128,2048]{1,0:T(8,128)(2,1)}, bf16[128,2048]{1,0:T(8,128)(2,1)S(1)}, u32[]{:S(2)}, u32[]{:S(2)}) collective-permute-start(bf16[128,2048]{1,0:T(8,128)(2,1)} %get-tuple-element.214), channel_id=1, source_target_pairs={{0,1},{1,0},{2,3},{3,2},{4,5},{5,4},{6,7},{7,6},{8,9},{9,8},{10,11... | collective-permute-start | bytes 1572872 | tf_op jit(solution)/shard_map/ppermute | solution.py:696
  250.2 23.0 %collective-permute-start.38 = (bf16[256,1024]{1,0:T(8,128)(2,1)S(1)}, bf16[256,1024]{1,0:T(8,128)(2,1)S(1)}, u32[]{:S(2)}, u32[]{:S(2)}) collective-permute-start(bf16[256,1024]{1,0:T(8,128)(2,1)S(1)} %get-tuple-element.210), channel_id=1, source_target_pairs={{0,16},{16,0},{1,17},{17,1},{2,18},{18,2},{3,19},{19,3},{4,20},{20... | collective-permute-start | bytes 1572872 | tf_op jit(solution)/shard_map/ppermute | solution.py:696
  273.0 32.4 %collective-permute-start.46 = (bf16[1024,1024]{1,0:T(8,128)(2,1)S(1)}, bf16[1024,1024]{1,0:T(8,128)(2,1)}, u32[]{:S(2)}, u32[]{:S(2)}) collective-permute-start(bf16[1024,1024]{1,0:T(8,128)(2,1)S(1)} %copy-done.6), channel_id=1, source_target_pairs={{0,8},{8,0},{1,9},{9,1},{2,10},{10,2},{3,11},{11,3},{4,12},{12,4},... | collective-permute-start | bytes 6291464 | tf_op jit(solution)/shard_map/ppermute | solution.py:746
  (75 other events, 634.8 us)
Sparse Core Ops, SparseCore 0:
  25.2 32.1 all-gather.2
  79.2 25.1 all-gather.4
  247.6 26.7 reduce-scatter.2
  287.3 26.9 reduce-scatter.4
